TPU v7x, 32 devices: a whole 2x2x4 slice. The times are simulated.
32 devices in a mesh: batch: 2 (over core), seq: 16 (over z, y, x).
Axes of the slice: x: 2, y: 2, z: 4, core: 2. Of those that a mesh axis runs over, the one named last changes fastest.
Arguments:
- tokens: bfloat16 [2, 2, 4096, 1024], P(None, 'batch', 'seq'), may hold values from -6 to 6
- cotangent: bfloat16 [2, 2, 4096, 1024], P(None, 'batch', 'seq'), may hold values from -6 to 6
- lengths: int32 [2, 2], P(None, 'batch'), may hold values from 1024 to 4096, as said below
- random_blocks: int32 [2, 2, 64, 16, 3], P(None, 'batch'), may hold values from 0 to 63, as said below
- query_key_value_weight: bfloat16 [1024, 3072], P('seq', 'batch'), may hold values from -0.1875 to 0.1875
- output_weight: bfloat16 [1024, 1024], P('seq', 'batch'), may hold values from -2 to 2
- up_weight: bfloat16 [1024, 4096], P('seq', 'batch'), may hold values from -0.1875 to 0.1875
- down_weight: bfloat16 [4096, 1024], P('seq', 'batch'), may hold values from -0.09375 to 0.09375
- out_bias: float32 [1024], replicated, may hold values from -3 to 3
- up_bias: float32 [4096], replicated, may hold values from -3 to 3
- down_bias: float32 [1024], replicated, may hold values from -3 to 3
- gain_attn: float32 [1024], replicated, may hold values from 0.1 to 1.9
- shift_attn: float32 [1024], replicated, may hold values from -3 to 3
- gain_ffn: float32 [1024], replicated, may hold values from 0.1 to 1.9
- shift_ffn: float32 [1024], replicated, may hold values from -3 to 3
Outputs:
- output: bfloat16 [2, 2, 4096, 1024], P(None, 'batch', 'seq')
- input_grad: float32 [2, 2, 4096, 1024], P(None, 'batch', 'seq')
- grad_qkv: float32 [1024, 3072], P('seq', 'batch')
- output_weight_gradient: float32 [1024, 1024], P('seq', 'batch')
- grad_up: float32 [1024, 4096], P('seq', 'batch')
- down_weight_gradient: float32 [4096, 1024], P('seq', 'batch')
- grad_out_bias: float32 [1024], replicated
- grad_up_bias: float32 [4096], replicated
- grad_down_bias: float32 [1024], replicated
- grad_gain_attn: float32 [1024], replicated
- grad_shift_attn: float32 [1024], replicated
- grad_gain_ffn: float32 [1024], replicated
- grad_shift_ffn: float32 [1024], replicated
Inputs may be any that keep to these rules, and one draw needn't show every extreme that they name: `lengths`: multiples of 64. Among the 2 sequences of each index of batch, one has 4096 tokens. `random_blocks`: split the blocks of a sequence into 16 groups of 4 consecutive blocks. For each micro-batch, sequence and group of query blocks, its 192 entries name blocks of each group exactly 12 times.
All inputs are finite; a program needn't handle non-finite values.
Results may differ from a plain program's by a relative error of at most 0.02.
Values may be sent and summed in bfloat16 or wider, within the bound.
No kernel may reach another device: no remote copies, remote signals or barrier semaphores. Data moves between devices by JAX's collectives and lax.ppermute only.
A program may use at most 384 MiB of HBM per device.

v0:
```python
import jax
import jax.numpy as jnp
from jax import lax
from jax.sharding import PartitionSpec as P

H = 16
HD = 64
BLOCK = 64
NGLOB = 2
NRAND = 3
BLK_DEV = 4


EPS = 1e-05
BIG = 1e30
HIGH = lax.Precision.HIGHEST


def broadcast(block, axis, source):
    block = jnp.where(lax.axis_index(axis) == source, block, jnp.zeros_like(block))
    return lax.psum(block, axis)


def padded(value, sides, width):
    for axis, dim in sides:
        size, length = (lax.axis_size(axis), value.shape[dim])
        up = [(i, (i + 1) % size) for i in range(size - 1)]
        down = [(j, i) for i, j in up]
        last = lax.slice_in_dim(value, length - width, length, axis=dim)
        first = lax.slice_in_dim(value, 0, width, axis=dim)
        before = lax.ppermute(last, axis, up)
        after = lax.ppermute(first, axis, down)
        value = jnp.concatenate([before, value, after], axis=dim)
    return value


def combined_all(value, axis, combine):
    everything = jax.tree.map(lambda part: lax.all_gather(part, axis), value)
    first = jax.tree.map(lambda part: part[0], everything)

    def turn(k, so_far):
        return combine(so_far, jax.tree.map(lambda part: part[k], everything))

    return lax.fori_loop(1, lax.axis_size(axis), turn, first)


def normalize(value, gain, shift):
    centre = jnp.mean(value, axis=-1, keepdims=True)
    centered = value - centre
    spread = jnp.mean(centered * centered, axis=-1, keepdims=True)
    return centered * lax.rsqrt(spread + EPS) * gain + shift


def smooth_gate(value):
    return jax.nn.gelu(value, approximate=True)


def gather_weights(shards):
    widened = (
        lax.all_gather(shards[0], "batch", axis=1, tiled=True),
        lax.all_gather(shards[1], "batch", axis=1, tiled=True),
        lax.all_gather(shards[2], "batch", axis=1, tiled=True),
        lax.all_gather(shards[3], "batch", axis=1, tiled=True),
    )
    return (
        lax.all_gather(widened[0], "seq", axis=0, tiled=True),
        lax.all_gather(widened[1], "seq", axis=0, tiled=True),
        lax.all_gather(widened[2], "seq", axis=0, tiled=True),
        lax.all_gather(widened[3], "seq", axis=0, tiled=True),
    )


def reduce_weights(grads):
    stripes = (
        lax.psum_scatter(
            grads[0].astype(jnp.bfloat16), "seq", scatter_dimension=0, tiled=True
        ).astype(jnp.float32),
        lax.psum_scatter(
            grads[1].astype(jnp.bfloat16), "seq", scatter_dimension=0, tiled=True
        ).astype(jnp.float32),
        lax.psum_scatter(
            grads[2].astype(jnp.bfloat16), "seq", scatter_dimension=0, tiled=True
        ).astype(jnp.float32),
        lax.psum_scatter(
            grads[3].astype(jnp.bfloat16), "seq", scatter_dimension=0, tiled=True
        ).astype(jnp.float32),
    )
    return (
        lax.psum_scatter(
            stripes[0].astype(jnp.bfloat16), "batch", scatter_dimension=1, tiled=True
        ).astype(jnp.float32),
        lax.psum_scatter(
            stripes[1].astype(jnp.bfloat16), "batch", scatter_dimension=1, tiled=True
        ).astype(jnp.float32),
        lax.psum_scatter(
            stripes[2].astype(jnp.bfloat16), "batch", scatter_dimension=1, tiled=True
        ).astype(jnp.float32),
        lax.psum_scatter(
            stripes[3].astype(jnp.bfloat16), "batch", scatter_dimension=1, tiled=True
        ).astype(jnp.float32),
    )


def join_stats(first, second):
    highest = jnp.maximum(first[0], second[0])
    return (
        highest,
        first[1] * jnp.exp(first[0] - highest) + second[1] * jnp.exp(second[0] - highest),
    )


def routing(request_grid, position, devices):
    requests = request_grid.shape[-1]
    slots_each = requests // devices
    source = request_grid // BLK_DEV
    head_of = jnp.arange(requests) // NRAND % H
    piece_of = request_grid % BLK_DEV * H + head_of
    earlier = jnp.arange(requests)[None, :] < jnp.arange(requests)[:, None]
    same_source = source[..., :, None] == source[..., None, :]
    standing = jnp.sum(same_source & earlier, axis=-1)
    owned = source == position
    slot_hit = owned[..., None] & (standing[..., None] == jnp.arange(slots_each))
    piece_hit = piece_of[..., None] == jnp.arange(BLK_DEV * H)
    select = jnp.einsum(
        "snic,snip->sncp", slot_hit.astype(jnp.float32), piece_hit.astype(jnp.float32)
    )
    own_source = lax.dynamic_index_in_dim(source, position, 1, keepdims=False)
    own_standing = lax.dynamic_index_in_dim(standing, position, 1, keepdims=False)
    arrival = own_source * slots_each + own_standing
    receive = (arrival[..., None] == jnp.arange(devices * slots_each)).astype(jnp.float32)
    own_blocks = lax.dynamic_index_in_dim(request_grid, position, 1, keepdims=False)
    return (select, receive, own_blocks)


def assemble(glob_kv, halo_kv, fetched, valid_glob, valid_halo, valid_far):
    seqs, grows = (glob_kv.shape[0], glob_kv.shape[1])
    block = BLOCK
    parts = BLK_DEV
    glob_keys = glob_kv.reshape(seqs, 1, grows, 2, H, HD).transpose(0, 1, 3, 4, 2, 5)
    glob_keys = jnp.broadcast_to(glob_keys, (seqs, parts, 2, H, grows, HD))
    near = jnp.stack(
        [halo_kv[:, member * block : (member + 3) * block] for member in range(parts)], 1
    )
    near = near.reshape(seqs, parts, 3 * block, 2, H, HD).transpose(0, 1, 3, 4, 2, 5)
    distant = fetched.reshape(seqs, parts, H, NRAND, block, 2, HD).transpose(0, 1, 5, 2, 3, 4, 6)
    distant = distant.reshape(seqs, parts, 2, H, NRAND * block, HD)
    keys = jnp.concatenate([glob_keys, near, distant], axis=4)
    near_ok = jnp.stack(
        [valid_halo[:, member * block : (member + 3) * block] for member in range(parts)], 1
    )
    allowed = jnp.concatenate(
        [
            jnp.broadcast_to(valid_glob[:, None, None, :], (seqs, parts, H, grows)),
            jnp.broadcast_to(near_ok[:, :, None, :], (seqs, parts, H, 3 * block)),
            valid_far.reshape(seqs, parts, H, NRAND * block),
        ],
        axis=3,
    )
    return (keys, allowed)


def sparse_scores(query_blocks, keys, allowed, scale):
    raw = (
        jnp.einsum(
            "sjqhd,sjhkd->sjhqk", query_blocks, keys[:, :, 0], preferred_element_type=jnp.float32
        )
        * scale
    )
    return jnp.where(allowed[:, :, :, None, :], raw, -BIG)


def global_scores(glob_heads, key_local, valid_local, scale):
    raw = (
        jnp.einsum("sqhd,skhd->shqk", glob_heads, key_local, preferred_element_type=jnp.float32)
        * scale
    )
    return jnp.where(valid_local[:, None, None, :], raw, -BIG)


def micro_step(
    gathered, vectors, x_low, cotangent_reduced, limits, request_grid, devices, position
):
    query_key_value_weight, output_weight, up_weight, down_weight = gathered
    out_bias, up_bias, down_bias, gain_attn, shift_attn, gain_ffn, shift_ffn = vectors
    seqs, local, width = x_low.shape
    block = BLOCK
    parts = BLK_DEV
    grows = NGLOB * block
    scale = HD ** (-0.5)
    is_first = position == 0
    glob_row = is_first & (jnp.arange(local) < grows)
    hidden = x_low.astype(jnp.float32)
    normed_one, pull_one = jax.vjp(normalize, hidden, gain_attn, shift_attn)
    normed_reduced = normed_one.astype(jnp.bfloat16)
    projected_rows = jnp.einsum(
        "znj,jq->znq", normed_reduced, query_key_value_weight, preferred_element_type=jnp.float32
    )
    queries = projected_rows[..., :width].astype(jnp.bfloat16)
    keyval = projected_rows[..., width:].astype(jnp.bfloat16)
    limit_col = limits[:, None]
    own_rows = position * local + jnp.arange(local)
    valid_local = own_rows[None, :] < limit_col
    halo_rows = position * local - block + jnp.arange(local + 2 * block)
    valid_halo = (halo_rows[None, :] >= 0) & (halo_rows[None, :] < limit_col)
    valid_glob = jnp.arange(grows)[None, :] < limit_col
    glob_query, glob_kv = (
        broadcast(queries[:, :grows], "seq", 0),
        broadcast(keyval[:, :grows], "seq", 0),
    )
    halo_kv = padded(keyval, (("seq", 1),), block)
    select, receive, own_blocks = routing(request_grid, position, devices)
    slots_each = select.shape[2]
    pieces = (
        keyval.reshape(seqs, parts, block, 2, H, HD)
        .transpose(0, 1, 4, 2, 3, 5)
        .reshape(seqs, parts * H, block, 2 * HD)
    )
    outgoing = jnp.einsum(
        "sncp,spbe->sncbe", select.astype(jnp.bfloat16), pieces, preferred_element_type=jnp.float32
    ).astype(jnp.bfloat16)
    incoming = lax.all_to_all(outgoing, "seq", split_axis=1, concat_axis=1, tiled=True)
    fetched = jnp.einsum(
        "sif,sfbe->sibe",
        receive.astype(jnp.bfloat16),
        incoming.reshape(seqs, devices * slots_each, block, 2 * HD),
        preferred_element_type=jnp.float32,
    ).astype(jnp.bfloat16)
    valid_far = own_blocks[..., None] * block + jnp.arange(block) < limits[:, None, None]
    keys, allowed = assemble(glob_kv, halo_kv, fetched, valid_glob, valid_halo, valid_far)
    query_blocks = queries.reshape(seqs, parts, block, H, HD)
    scores = sparse_scores(query_blocks, keys, allowed, scale)
    highest = jnp.max(scores, axis=-1, keepdims=True)
    sparse_lse = highest + jnp.log(jnp.sum(jnp.exp(scores - highest), axis=-1, keepdims=True))
    weights = jnp.exp(scores - sparse_lse)
    sparse_out = jnp.einsum(
        "sjhqk,sjhkd->sjqhd",
        weights.astype(jnp.bfloat16),
        keys[:, :, 1],
        preferred_element_type=jnp.float32,
    ).reshape(seqs, local, width)
    key_local = keyval[..., :width].reshape(seqs, local, H, HD)
    value_local = keyval[..., width:].reshape(seqs, local, H, HD)
    glob_heads = glob_query.reshape(seqs, grows, H, HD)
    glob_scores = global_scores(glob_heads, key_local, valid_local, scale)
    glob_top = jnp.max(glob_scores, axis=-1)
    glob_total = jnp.sum(
        jnp.where(valid_local[:, None, None, :], jnp.exp(glob_scores - glob_top[..., None]), 0.0),
        axis=-1,
    )
    glob_top, glob_total = combined_all((glob_top, glob_total), "seq", join_stats)
    glob_lse = glob_top + jnp.log(glob_total)
    glob_weights = jnp.exp(glob_scores - glob_lse[..., None])
    glob_part = jnp.einsum(
        "shqk,skhd->sqhd",
        glob_weights.astype(jnp.bfloat16),
        value_local,
        preferred_element_type=jnp.float32,
    )
    glob_exact = jnp.einsum(
        "shqk,skhd->sqhd", glob_weights, value_local.astype(jnp.float32), precision=HIGH
    )
    glob_out, glob_mean = (
        lax.psum(glob_part.astype(jnp.bfloat16), "seq").astype(jnp.float32),
        lax.psum(glob_exact.astype(jnp.bfloat16), "seq").astype(jnp.float32),
    )
    glob_full = jnp.pad(glob_out.reshape(seqs, grows, width), ((0, 0), (0, local - grows), (0, 0)))
    attended = jnp.where(glob_row[None, :, None], glob_full, sparse_out)
    attention_reduced = attended.astype(jnp.bfloat16)
    middle = (
        hidden
        + jnp.einsum(
            "znj,jq->znq", attention_reduced, output_weight, preferred_element_type=jnp.float32
        )
        + out_bias
    )
    normed_two, pull_two = jax.vjp(normalize, middle, gain_ffn, shift_ffn)
    second_normed_reduced = normed_two.astype(jnp.bfloat16)
    before = (
        jnp.einsum(
            "znj,jq->znq", second_normed_reduced, up_weight, preferred_element_type=jnp.float32
        )
        + up_bias
    )
    activated, pull_gate = jax.vjp(smooth_gate, before)
    activation_reduced = activated.astype(jnp.bfloat16)
    result = (
        middle
        + jnp.einsum(
            "xwg,gc->xwc", activation_reduced, down_weight, preferred_element_type=jnp.float32
        )
        + down_bias
    ).astype(jnp.bfloat16)
    down_weight_gradient = jnp.einsum(
        "kmn,kmw->nw", activation_reduced, cotangent_reduced, preferred_element_type=jnp.float32
    )
    d_down_bias = jnp.sum(cotangent_reduced.astype(jnp.float32), axis=(0, 1))
    activation_gradient = jnp.einsum(
        "mav,yv->may", cotangent_reduced, down_weight, preferred_element_type=jnp.float32
    )
    prior_gradient = pull_gate(activation_gradient)[0].astype(jnp.bfloat16)
    grad_up = jnp.einsum(
        "xwz,xwk->zk", second_normed_reduced, prior_gradient, preferred_element_type=jnp.float32
    )
    d_up_bias = jnp.sum(prior_gradient.astype(jnp.float32), axis=(0, 1))
    second_normed_gradient = jnp.einsum(
        "kut,jt->kuj", prior_gradient, up_weight, preferred_element_type=jnp.float32
    )
    d_middle_norm, d_gain_ffn, d_shift_ffn = pull_two(second_normed_gradient)
    d_middle = cotangent_reduced.astype(jnp.float32) + d_middle_norm
    branch_gradient = d_middle.astype(jnp.bfloat16)
    output_weight_gradient = jnp.einsum(
        "xwz,xwk->zk", attention_reduced, branch_gradient, preferred_element_type=jnp.float32
    )
    d_out_bias = jnp.sum(branch_gradient.astype(jnp.float32), axis=(0, 1))
    attention_gradient = jnp.einsum(
        "kut,jt->kuj", branch_gradient, output_weight, preferred_element_type=jnp.float32
    ).astype(jnp.bfloat16)
    d_sparse = jnp.where(
        glob_row[None, :, None], jnp.zeros_like(attention_gradient), attention_gradient
    ).reshape(seqs, parts, block, H, HD)
    scores = sparse_scores(query_blocks, keys, allowed, scale)
    weights = jnp.exp(scores - sparse_lse)
    d_weights = jnp.einsum(
        "sjqhd,sjhkd->sjhqk", d_sparse, keys[:, :, 1], preferred_element_type=jnp.float32
    )
    centre = jnp.sum(weights * d_weights, axis=-1, keepdims=True)
    d_scores = (weights * (d_weights - centre)).astype(jnp.bfloat16)
    d_query = (
        jnp.einsum(
            "sjhqk,sjhkd->sjqhd", d_scores, keys[:, :, 0], preferred_element_type=jnp.float32
        )
        * scale
    )
    d_keys = (
        jnp.einsum("sjhqk,sjqhd->sjhkd", d_scores, query_blocks, preferred_element_type=jnp.float32)
        * scale
    )
    d_values = jnp.einsum(
        "sjhqk,sjqhd->sjhkd",
        weights.astype(jnp.bfloat16),
        d_sparse,
        preferred_element_type=jnp.float32,
    )
    d_pairs = jnp.stack([d_keys, d_values], 2)
    d_glob = (
        jnp.sum(d_pairs[..., :grows, :], axis=1)
        .transpose(0, 3, 1, 2, 4)
        .reshape(seqs, grows, 2 * width)
    )
    d_near = (
        d_pairs[..., grows : grows + 3 * block, :]
        .transpose(0, 1, 4, 2, 3, 5)
        .reshape(seqs, parts, 3 * block, 2 * width)
    )
    near_sum = d_near[:, 0] * 0.0
    near_sum = jnp.pad(near_sum, ((0, 0), (0, (parts - 1) * block), (0, 0)))
    for member in range(parts):
        near_sum = near_sum + jnp.pad(
            d_near[:, member], ((0, 0), (member * block, (parts - 1 - member) * block), (0, 0))
        )
    d_distant = d_pairs[..., grows + 3 * block :, :].reshape(seqs, parts, 2, H, NRAND, block, HD)
    d_distant = d_distant.transpose(0, 1, 3, 4, 5, 2, 6).reshape(
        seqs, parts * H * NRAND, block, 2 * HD
    )
    d_outgoing = jnp.einsum("sif,sibe->sfbe", receive, d_distant, precision=HIGH).reshape(
        seqs, devices, slots_each, block, 2 * HD
    )
    d_incoming = lax.all_to_all(
        d_outgoing.astype(jnp.bfloat16), "seq", split_axis=1, concat_axis=1, tiled=True
    ).astype(d_outgoing.dtype)
    d_pieces = jnp.einsum("sncp,sncbe->spbe", select, d_incoming, precision=HIGH)
    d_from_far = (
        d_pieces.reshape(seqs, parts, H, block, 2, HD)
        .transpose(0, 1, 3, 4, 2, 5)
        .reshape(seqs, local, 2 * width)
    )
    edges = jnp.concatenate([near_sum[:, :block], near_sum[:, local + block :]], axis=1)
    returned = padded(edges.astype(jnp.bfloat16), (("seq", 1),), block).astype(edges.dtype)
    d_keyval = near_sum[:, block : local + block] + d_from_far
    d_keyval = d_keyval.at[:, :block].add(returned[:, :block])
    d_keyval = d_keyval.at[:, local - block :].add(returned[:, 3 * block :])
    d_glob_out = broadcast(attention_gradient[:, :grows], "seq", 0).reshape(seqs, grows, H, HD)
    glob_scores = global_scores(glob_heads, key_local, valid_local, scale)
    glob_weights = jnp.exp(glob_scores - glob_lse[..., None])
    d_glob_weights = jnp.einsum(
        "sqhd,skhd->shqk", d_glob_out, value_local, preferred_element_type=jnp.float32
    )
    glob_centre = jnp.sum(d_glob_out.astype(jnp.float32) * glob_mean, axis=-1).transpose(0, 2, 1)
    d_glob_scores = (glob_weights * (d_glob_weights - glob_centre[..., None])).astype(jnp.bfloat16)
    d_glob_query = (
        jnp.einsum("shqk,skhd->sqhd", d_glob_scores, key_local, preferred_element_type=jnp.float32)
        * scale
    )
    d_glob_key = (
        jnp.einsum("shqk,sqhd->skhd", d_glob_scores, glob_heads, preferred_element_type=jnp.float32)
        * scale
    )
    d_glob_value = jnp.einsum(
        "shqk,sqhd->skhd",
        glob_weights.astype(jnp.bfloat16),
        d_glob_out,
        preferred_element_type=jnp.float32,
    )
    d_keyval = d_keyval + jnp.concatenate(
        [d_glob_key.reshape(seqs, local, width), d_glob_value.reshape(seqs, local, width)], axis=-1
    )
    sum_query, sum_glob = (
        lax.psum(d_glob_query.reshape(seqs, grows, width).astype(jnp.bfloat16), "seq").astype(
            jnp.float32
        ),
        lax.psum(d_glob.astype(jnp.bfloat16), "seq").astype(jnp.float32),
    )
    rest = ((0, 0), (0, local - grows), (0, 0))
    d_query_all = d_query.reshape(seqs, local, width) + jnp.where(
        is_first, jnp.pad(sum_query, rest), 0.0
    )
    d_keyval = d_keyval + jnp.where(is_first, jnp.pad(sum_glob, rest), 0.0)
    projected_gradient = jnp.concatenate(
        [d_query_all.astype(jnp.bfloat16), d_keyval.astype(jnp.bfloat16)], axis=-1
    )
    grad_qkv = jnp.einsum(
        "xwz,xwk->zk", normed_reduced, projected_gradient, preferred_element_type=jnp.float32
    )
    first_normed_gradient = jnp.einsum(
        "kut,jt->kuj",
        projected_gradient,
        query_key_value_weight,
        preferred_element_type=jnp.float32,
    )
    d_hidden_norm, d_gain_attn, d_shift_attn = pull_one(first_normed_gradient)
    input_grad = d_middle + d_hidden_norm
    weight_grads = (grad_qkv, output_weight_gradient, grad_up, down_weight_gradient)
    vector_grads = (
        d_out_bias,
        d_up_bias,
        d_down_bias,
        d_gain_attn,
        d_shift_attn,
        d_gain_ffn,
        d_shift_ffn,
    )
    return (result, input_grad, weight_grads, vector_grads)


def body(
    tokens,
    cotangent,
    lengths,
    random_blocks,
    query_key_value_weight,
    output_weight,
    up_weight,
    down_weight,
    out_bias,
    up_bias,
    down_bias,
    gain_attn,
    shift_attn,
    gain_ffn,
    shift_ffn,
):
    devices = lax.axis_size("seq")
    position = lax.axis_index("seq")
    shards = (query_key_value_weight, output_weight, up_weight, down_weight)
    vectors = (out_bias, up_bias, down_bias, gain_attn, shift_attn, gain_ffn, shift_ffn)
    batches, seqs, local, width = tokens.shape
    shard_sums = tuple((jnp.zeros(member.shape, jnp.float32) for member in shards))
    vector_sums = tuple((jnp.zeros(member.shape, jnp.float32) for member in vectors))
    results = []
    input_grads = []
    for micro in range(batches):
        gathered = gather_weights(shards)
        request_grid = random_blocks[micro].reshape(seqs, devices, BLK_DEV * H * NRAND)
        result, input_grad, weight_grads, vector_grads = micro_step(
            gathered,
            vectors,
            tokens[micro],
            cotangent[micro],
            lengths[micro],
            request_grid,
            devices,
            position,
        )
        results.append(result)
        input_grads.append(input_grad)
        vector_sums = tuple((total + extra for total, extra in zip(vector_sums, vector_grads)))
        reduced = reduce_weights(weight_grads)
        shard_sums = tuple((total + extra for total, extra in zip(shard_sums, reduced)))
    totals = lax.psum(vector_sums, ("batch", "seq"))
    return (
        jnp.stack(results),
        jnp.stack(input_grads),
        shard_sums[0],
        shard_sums[1],
        shard_sums[2],
        shard_sums[3],
        totals[0],
        totals[1],
        totals[2],
        totals[3],
        totals[4],
        totals[5],
        totals[6],
    )


def solution(mesh):
    return jax.shard_map(
        body,
        mesh=mesh,
        in_specs=(
            P(None, "batch", "seq", None),
            P(None, "batch", "seq", None),
            P(None, "batch"),
            P(None, "batch", None, None, None),
            P("seq", "batch"),
            P("seq", "batch"),
            P("seq", "batch"),
            P("seq", "batch"),
            P(),
            P(),
            P(),
            P(),
            P(),
            P(),
            P(),
        ),
        out_specs=(
            P(None, "batch", "seq", None),
            P(None, "batch", "seq", None),
            P("seq", "batch"),
            P("seq", "batch"),
            P("seq", "batch"),
            P("seq", "batch"),
            P(),
            P(),
            P(),
            P(),
            P(),
            P(),
            P(),
        ),
        check_vma=False,
    )
```

profile of v0, /device:TPU:0, one launch (start us, length us, event | category | flops | bytes accessed | tf_op | source)
XLA Modules:
  0.0 2543.5 jit_solution(5919697925198036121)
XLA Ops:
  18.1 89.9 %all-gather.9.cloned.1.call-done = bf16[1024,3072]{1,0:T(8,128)(2,1)} async-done(((bf16[64,3072]{1,0:T(8,128)(2,1)}), bf16[1024,3072]{1,0:T(8,128)(2,1)}) %all-gather.9.cloned.1.call-update) | async-done | bytes 6291472 | tf_op jit(solution)/shard_map/all_gather | solution.py:66
  133.3 97.2 %all-reduce.32.cloned.1.call-done = (bf16[128,16,64]{0,2,1:T(8,128)(2,1)}, bf16[128,16,64]{0,2,1:T(8,128)(2,1)}) async-done(((bf16[128,16,64]{0,2,1:T(8,128)(2,1)}, bf16[128,16,64]{0,2,1:T(8,128)(2,1)}), (bf16[128,16,64]{0,2,1:T(8,128)(2,1)}, bf16[128,16,64]{0,2,1:T(8,128)(2,1)})) %all-reduce.32.cloned.1.call-update) | async-done | bytes 524304 | tf_op jit(solution)/shard_map/psum | solution.py:21
  232.3 39.3 %all-gather.2 = f32[256,128]{1,0:T(8,128)S(1)} all-gather(f32[16,128]{1,0:T(8,128)S(1)} %get-tuple-element.477), channel_id=4, replica_groups=mesh['batch'=2,'seq'=16] {'seq'}, dimensions={0}, use_global_device_ids=true | all-gather | bytes 139264 | tf_op jit(solution)/shard_map/all_gather | solution.py:38
  273.0 36.1 %all-gather.3 = f32[256,128]{1,0:T(8,128)S(1)} all-gather(f32[16,128]{1,0:T(8,128)S(1)} %select_reduce_fusion), channel_id=5, replica_groups=mesh['batch'=2,'seq'=16] {'seq'}, dimensions={0}, use_global_device_ids=true | all-gather | bytes 139264 | tf_op jit(solution)/shard_map/all_gather | solution.py:38
  326.5 38.3 %all-gather = f32[256,128]{1,0:T(8,128)S(1)} all-gather(f32[16,128]{1,0:T(8,128)S(1)} %get-tuple-element.479), channel_id=2, replica_groups=mesh['batch'=2,'seq'=16] {'seq'}, dimensions={0}, use_global_device_ids=true | all-gather | bytes 139264 | tf_op jit(solution)/shard_map/all_gather | solution.py:38
  365.6 36.1 %all-gather.1 = f32[256,128]{1,0:T(8,128)S(1)} all-gather(f32[16,128]{1,0:T(8,128)S(1)} %select_reduce_fusion.1), channel_id=3, replica_groups=mesh['batch'=2,'seq'=16] {'seq'}, dimensions={0}, use_global_device_ids=true | all-gather | bytes 139264 | tf_op jit(solution)/shard_map/all_gather | solution.py:38
  473.9 36.0 %all-to-all-done.1 = bf16[1,16,12,64,128]{4,3,2,0,1:T(8,128)(2,1)} async-done(((bf16[1,16,12,64,128]{4,3,2,0,1:T(8,128)(2,1)}), bf16[1,16,12,64,128]{4,3,2,0,1:T(8,128)(2,1)}, u32[]{:S(2)}, u32[]{:S(2)}) %all-to-all-start.1) | async-done | bytes 3145760 | tf_op jit(solution)/shard_map/all_to_all | solution.py:221
  509.9 18.3 all-to-all-start
  604.5 11.8 reshape.2677
  639.9 12.0 reshape.2662
  719.2 55.7 %all-gather.13.cloned.1.call-done = bf16[1024,4096]{1,0:T(8,128)(2,1)} async-done(((bf16[64,4096]{1,0:T(8,128)(2,1)}), bf16[1024,4096]{1,0:T(8,128)(2,1)}) %all-gather.13.cloned.1.call-update) | async-done | bytes 8388624 | tf_op jit(solution)/shard_map/all_gather | solution.py:68
  787.5 101.3 %all-gather.15.cloned.1.call-done = bf16[4096,1024]{1,0:T(8,128)(2,1)} async-done(((bf16[256,1024]{1,0:T(8,128)(2,1)}), bf16[4096,1024]{1,0:T(8,128)(2,1)}) %all-gather.15.cloned.1.call-update) | async-done | bytes 8388624 | tf_op jit(solution)/shard_map/all_gather | solution.py:69
  989.7 45.7 %all-reduce.28.cloned.1.call-done = (bf16[1,128,1024]{2,1,0:T(8,128)(2,1)}, bf16[1,128,16,64]{1,3,2,0:T(8,128)(2,1)}, bf16[1,128,1024]{2,1,0:T(8,128)(2,1)}, bf16[1,128,16,64]{1,3,2,0:T(8,128)(2,1)}) async-done(((bf16[1,128,1024]{2,1,0:T(8,128)(2,1)}, bf16[1,128,16,64]{1,3,2,0:T(8,128)(2,1)}, bf16[1,128,1024]{2,1,0:T(8,128)(2,1)}, bf16[1,128,16,64]{1,3,2,0:T(8,128)(2,1)}), (bf16[1,128,1024]{2,1,0:T(8,128)(2,1)}, ...) | async-done | bytes 1048592 | tf_op jit(solution)/shard_map/psum | solution.py:21
  1080.3 37.5 %reduce-scatter.29.cloned.1.call-done = bf16[64,1024]{1,0:T(8,128)(2,1)} async-done(((bf16[1024,1024]{1,0:T(8,128)(2,1)}), bf16[64,1024]{1,0:T(8,128)(2,1)}) %reduce-scatter.29.cloned.1.call-update) | async-done | bytes 131088 | tf_op jit(solution)/shard_map/reduce_scatter | solution.py:78
  1117.8 80.4 %reduce-scatter.25.cloned.1.call-done = bf16[64,1024]{1,0:T(8,128)(2,1)} async-done(((bf16[1024,1024]{1,0:T(8,128)(2,1)}), bf16[64,1024]{1,0:T(8,128)(2,1)}) %reduce-scatter.25.cloned.1.call-update) | async-done | bytes 131088 | tf_op jit(solution)/shard_map/reduce_scatter | solution.py:78
  1204.2 12.4 fusion.6
  1227.8 22.1 copy.387
  1249.9 12.8 reshape.2738
  1310.8 15.6 collective-permute-done.6
  1326.4 12.6 collective-permute-done.7
  1426.4 22.1 copy.370
  1448.5 13.1 reshape.2733
  1470.7 42.3 %all-to-all-start.2 = ((bf16[1,16,12,64,128]{4,3,2,0,1:T(8,128)(2,1)}), bf16[1,16,12,64,128]{4,3,2,0,1:T(8,128)(2,1)}, u32[]{:S(2)}, u32[]{:S(2)}) async-start(bf16[1,16,12,64,128]{4,3,2,0,1:T(8,128)(2,1)} %copy.371), calls=%async_computation.2 | async-start | bytes 6291456 | tf_op jit(solution)/shard_map/all_to_all | solution.py:368
  1543.8 40.8 %collective-permute-done.4 = bf16[1,64,2048]{1,2,0:T(8,128)(2,1)} collective-permute-done((bf16[1,64,2048]{1,2,0:T(8,128)(2,1)}, bf16[1,64,2048]{1,2,0:T(8,128)(2,1)}, u32[]{:S(2)}, u32[]{:S(2)}) %collective-permute-start.4) | collective-permute-done | bytes 262176 | tf_op jit(solution)/shard_map/ppermute | solution.py:31
  1591.7 11.6 reshape.2746
  1603.4 11.7 fusion.56
  1653.7 122.9 %reduce-scatter.45.cloned.1.call-done = bf16[256,1024]{1,0:T(8,128)(2,1)} async-done(((bf16[4096,1024]{1,0:T(8,128)(2,1)}), bf16[256,1024]{1,0:T(8,128)(2,1)}) %reduce-scatter.45.cloned.1.call-update) | async-done | bytes 524304 | tf_op jit(solution)/shard_map/reduce_scatter | solution.py:84
  1785.2 174.1 %reduce-scatter.33.cloned.1.call-done = bf16[64,4096]{1,0:T(8,128)(2,1)} async-done(((bf16[1024,4096]{1,0:T(8,128)(2,1)}), bf16[64,4096]{1,0:T(8,128)(2,1)}) %reduce-scatter.33.cloned.1.call-update) | async-done | bytes 524304 | tf_op jit(solution)/shard_map/reduce_scatter | solution.py:81
  1988.6 174.9 %reduce-scatter.37.cloned.1.call-done = bf16[64,4096]{1,0:T(8,128)(2,1)} async-done(((bf16[1024,4096]{1,0:T(8,128)(2,1)}), bf16[64,4096]{1,0:T(8,128)(2,1)}) %reduce-scatter.37.cloned.1.call-update) | async-done | bytes 524304 | tf_op jit(solution)/shard_map/reduce_scatter | solution.py:81
  2172.6 144.7 %reduce-scatter.21.cloned.1.call-done = bf16[64,3072]{1,0:T(8,128)(2,1)} async-done(((bf16[1024,3072]{1,0:T(8,128)(2,1)}), bf16[64,3072]{1,0:T(8,128)(2,1)}) %reduce-scatter.21.cloned.1.call-update) | async-done | bytes 393232 | tf_op jit(solution)/shard_map/reduce_scatter | solution.py:75
  2320.7 147.7 %reduce-scatter.17.cloned.1.call-done = bf16[64,3072]{1,0:T(8,128)(2,1)} async-done(((bf16[1024,3072]{1,0:T(8,128)(2,1)}), bf16[64,3072]{1,0:T(8,128)(2,1)}) %reduce-scatter.17.cloned.1.call-update) | async-done | bytes 393232 | tf_op jit(solution)/shard_map/reduce_scatter | solution.py:75
  2471.6 40.9 %all-reduce.16 = (f32[1024]{0:T(1024)}, f32[4096]{0:T(1024)}, f32[1024]{0:T(1024)}, f32[1024]{0:T(1024)}, f32[1024]{0:T(1024)}, /*index=5*/f32[1024]{0:T(1024)}, f32[1024]{0:T(1024)}) all-reduce(f32[1024]{0:T(1024)S(1)} %add.835, f32[4096]{0:T(1024)S(1)} %add.836, ...), channel_id=1, replica_groups=mesh['batch'=2,'seq'=16] {'batch','seq'}, use_global_device_ids=true, to_apply=%region_68.69 | all-reduce | flops 10240 | bytes 81920 | tf_op jit(solution)/shard_map/psum | solution.py:489
  (683 shorter events, 779.4 us)
Async XLA Ops:
  7.2 100.8 %all-gather.9.cloned.1.call-start = ((), (), s32[]{:S(2)}) async-start(), calls=%async_computation.20 | async-start | bytes 6684672 | tf_op jit(solution)/shard_map/all_gather | solution.py:66
  11.3 219.3 %all-reduce.32.cloned.1.call-start = ((), (), s32[]{:S(2)}) async-start(), calls=%async_computation.43 | async-start | bytes 1048576 | tf_op jit(solution)/shard_map/psum | solution.py:21
  123.6 545.9 %all-reduce.30.cloned.1.call-start = ((), (), s32[]{:S(2)}) async-start(), calls=%async_computation.42 | async-start | bytes 3145728 | tf_op jit(solution)/shard_map/psum | solution.py:21
  404.9 308.2 %all-gather.11.cloned.1.call-start = ((), (), s32[]{:S(2)}) async-start(), calls=%async_computation.21 | async-start | bytes 2228224 | tf_op jit(solution)/shard_map/all_gather | solution.py:67
  407.0 367.9 %all-gather.13.cloned.1.call-start = ((), (), s32[]{:S(2)}) async-start(), calls=%async_computation.22 | async-start | bytes 8912896 | tf_op jit(solution)/shard_map/all_gather | solution.py:68
  440.9 69.0 %all-to-all-start.1 = ((bf16[1,16,12,64,128]{4,3,2,0,1:T(8,128)(2,1)}), bf16[1,16,12,64,128]{4,3,2,0,1:T(8,128)(2,1)}, u32[]{:S(2)}, u32[]{:S(2)}) async-start(bf16[1,16,12,64,128]{4,3,2,0,1:T(8,128)(2,1)} %copy.354), calls=%async_computation.1 | async-start | bytes 6291456 | tf_op jit(solution)/shard_map/all_to_all | solution.py:221
  445.5 443.4 %all-gather.15.cloned.1.call-start = ((), (), s32[]{:S(2)}) async-start(), calls=%async_computation.23 | async-start | bytes 8912896 | tf_op jit(solution)/shard_map/all_gather | solution.py:69
  509.9 124.0 %all-to-all-start = ((bf16[1,16,12,64,128]{4,3,2,0,1:T(8,128)(2,1)}), bf16[1,16,12,64,128]{4,3,2,0,1:T(8,128)(2,1)}, u32[]{:S(2)}, u32[]{:S(2)}) async-start(bf16[1,16,12,64,128]{4,3,2,0,1:T(8,128)(2,1)} %copy.331), calls=%async_computation | async-start | bytes 6291456 | tf_op jit(solution)/shard_map/all_to_all | solution.py:221
  528.2 507.1 %all-reduce.28.cloned.1.call-start = ((), (), s32[]{:S(2)}) async-start(), calls=%async_computation.41 | async-start | bytes 2097152 | tf_op jit(solution)/shard_map/psum | solution.py:21
  534.4 38.3 %collective-permute-start.2 = (bf16[1,64,2048]{2,1,0:T(8,128)(2,1)}, bf16[1,64,2048]{2,1,0:T(8,128)(2,1)}, u32[]{:S(2)}, u32[]{:S(2)}) collective-permute-start(bf16[1,64,2048]{2,1,0:T(8,128)(2,1)} %get-tuple-element.440), channel_id=1, source_target_pairs={{0,1},{1,2},{2,3},{3,4},{4,5},{5,6},{6,7},{7,8},{8,9},{9,10},{10,1... | collective-permute-start | bytes 786440 | tf_op jit(solution)/shard_map/ppermute | solution.py:31
  924.3 193.4 %reduce-scatter.29.cloned.1.call-start = ((), (), s32[]{:S(2)}) async-start(), calls=%async_computation.30 | async-start | bytes 2228224 | tf_op jit(solution)/shard_map/reduce_scatter | solution.py:78
  927.5 270.7 %reduce-scatter.25.cloned.1.call-start = ((), (), s32[]{:S(2)}) async-start(), calls=%async_computation.28 | async-start | bytes 2228224 | tf_op jit(solution)/shard_map/reduce_scatter | solution.py:78
  965.3 380.9 %all-reduce.26.cloned.1.call-start = ((), (), s32[]{:S(2)}) async-start(), calls=%async_computation.40 | async-start | bytes 3145728 | tf_op jit(solution)/shard_map/psum | solution.py:411
  1055.1 597.8 %reduce-scatter.41.cloned.1.call-start = ((), (), s32[]{:S(2)}) async-start(), calls=%async_computation.36 | async-start | bytes 8912896 | tf_op jit(solution)/shard_map/reduce_scatter | solution.py:84
  1063.7 712.9 %reduce-scatter.45.cloned.1.call-start = ((), (), s32[]{:S(2)}) async-start(), calls=%async_computation.38 | async-start | bytes 8912896 | tf_op jit(solution)/shard_map/reduce_scatter | solution.py:84
  1072.5 886.8 %reduce-scatter.33.cloned.1.call-start = ((), (), s32[]{:S(2)}) async-start(), calls=%async_computation.32 | async-start | bytes 8912896 | tf_op jit(solution)/shard_map/reduce_scatter | solution.py:81
  1080.2 891.1 %reduce-scatter.31.cloned.1.call-start = ((), (), s32[]{:S(2)}) async-start(), calls=%async_computation.31 | async-start | bytes 196608 | tf_op jit(solution)/shard_map/reduce_scatter | solution.py:92
  1117.8 864.4 %reduce-scatter.27.cloned.1.call-start = ((), (), s32[]{:S(2)}) async-start(), calls=%async_computation.29 | async-start | bytes 196608 | tf_op jit(solution)/shard_map/reduce_scatter | solution.py:92
  1198.3 965.2 %reduce-scatter.37.cloned.1.call-start = ((), (), s32[]{:S(2)}) async-start(), calls=%async_computation.34 | async-start | bytes 8912896 | tf_op jit(solution)/shard_map/reduce_scatter | solution.py:81
  1271.7 78.7 %all-to-all-start.3 = ((bf16[1,16,12,64,128]{4,3,2,0,1:T(8,128)(2,1)}), bf16[1,16,12,64,128]{4,3,2,0,1:T(8,128)(2,1)S(1)}, u32[]{:S(2)}, u32[]{:S(2)}) async-start(bf16[1,16,12,64,128]{4,3,2,0,1:T(8,128)(2,1)} %copy.388), calls=%async_computation.3 | async-start | bytes 6291456 | tf_op jit(solution)/shard_map/all_to_all | solution.py:368
  1275.6 1041.7 %reduce-scatter.21.cloned.1.call-start = ((), (), s32[]{:S(2)}) async-start(), calls=%async_computation.26 | async-start | bytes 6684672 | tf_op jit(solution)/shard_map/reduce_scatter | solution.py:75
  1299.1 39.9 %collective-permute-start.7 = (bf16[1,64,2048]{1,2,0:T(8,128)(2,1)}, bf16[1,64,2048]{1,2,0:T(8,128)(2,1)}, u32[]{:S(2)}, u32[]{:S(2)}) collective-permute-start(bf16[1,64,2048]{1,2,0:T(8,128)(2,1)} %get-tuple-element.425), channel_id=1, source_target_pairs={{1,0},{2,1},{3,2},{4,3},{5,4},{6,5},{7,6},{8,7},{9,8},{10,9},{11,1... | collective-permute-start | bytes 786440 | tf_op jit(solution)/shard_map/ppermute | solution.py:32
  1470.7 121.0 %all-to-all-start.2 = ((bf16[1,16,12,64,128]{4,3,2,0,1:T(8,128)(2,1)}), bf16[1,16,12,64,128]{4,3,2,0,1:T(8,128)(2,1)}, u32[]{:S(2)}, u32[]{:S(2)}) async-start(bf16[1,16,12,64,128]{4,3,2,0,1:T(8,128)(2,1)} %copy.371), calls=%async_computation.2 | async-start | bytes 6291456 | tf_op jit(solution)/shard_map/all_to_all | solution.py:368
  1513.0 955.4 %reduce-scatter.17.cloned.1.call-start = ((), (), s32[]{:S(2)}) async-start(), calls=%async_computation.24 | async-start | bytes 6684672 | tf_op jit(solution)/shard_map/reduce_scatter | solution.py:75
  1530.6 54.0 %collective-permute-start.4 = (bf16[1,64,2048]{1,2,0:T(8,128)(2,1)}, bf16[1,64,2048]{1,2,0:T(8,128)(2,1)}, u32[]{:S(2)}, u32[]{:S(2)}) collective-permute-start(bf16[1,64,2048]{1,2,0:T(8,128)(2,1)} %get-tuple-element.426), channel_id=1, source_target_pairs={{0,1},{1,2},{2,3},{3,4},{4,5},{5,6},{6,7},{7,8},{8,9},{9,10},{10,1... | collective-permute-start | bytes 786440 | tf_op jit(solution)/shard_map/ppermute | solution.py:31
  1535.2 49.4 %collective-permute-start.5 = (bf16[1,64,2048]{1,2,0:T(8,128)(2,1)}, bf16[1,64,2048]{1,2,0:T(8,128)(2,1)}, u32[]{:S(2)}, u32[]{:S(2)}) collective-permute-start(bf16[1,64,2048]{1,2,0:T(8,128)(2,1)} %get-tuple-element.427), channel_id=1, source_target_pairs={{1,0},{2,1},{3,2},{4,3},{5,4},{6,5},{7,6},{8,7},{9,8},{10,9},{11,1... | collective-permute-start | bytes 786440 | tf_op jit(solution)/shard_map/ppermute | solution.py:32
  1652.9 859.6 %reduce-scatter.43.cloned.1.call-start = ((), (), s32[]{:S(2)}) async-start(), calls=%async_computation.37 | async-start | bytes 786432 | tf_op jit(solution)/shard_map/reduce_scatter | solution.py:98
  1653.6 858.8 %reduce-scatter.47.cloned.1.call-start = ((), (), s32[]{:S(2)}) async-start(), calls=%async_computation.39 | async-start | bytes 786432 | tf_op jit(solution)/shard_map/reduce_scatter | solution.py:98
  1776.6 737.8 %reduce-scatter.35.cloned.1.call-start = ((), (), s32[]{:S(2)}) async-start(), calls=%async_computation.33 | async-start | bytes 786432 | tf_op jit(solution)/shard_map/reduce_scatter | solution.py:95
  1959.4 555.0 %reduce-scatter.39.cloned.1.call-start = ((), (), s32[]{:S(2)}) async-start(), calls=%async_computation.35 | async-start | bytes 786432 | tf_op jit(solution)/shard_map/reduce_scatter | solution.py:95
  2163.6 359.8 %reduce-scatter.23.cloned.1.call-start = ((), (), s32[]{:S(2)}) async-start(), calls=%async_computation.27 | async-start | bytes 589824 | tf_op jit(solution)/shard_map/reduce_scatter | solution.py:89
  2317.3 217.1 %reduce-scatter.19.cloned.1.call-start = ((), (), s32[]{:S(2)}) async-start(), calls=%async_computation.25 | async-start | bytes 589824 | tf_op jit(solution)/shard_map/reduce_scatter | solution.py:89
  (147 other events, 5425.5 us)
Sparse Core Ops, SparseCore 0:
  11.4 96.5 all-gather.8
  123.7 106.7 all-reduce.31
  405.0 167.2 all-reduce.29
  574.9 85.7 all-gather.10
  663.4 111.4 all-gather.12
  777.5 111.3 all-gather.14
  924.5 110.8 all-reduce.27
  1038.2 79.4 reduce-scatter.28
  1120.0 78.1 reduce-scatter.24
  1203.9 142.3 all-reduce.25
  1348.6 205.4 reduce-scatter.40
  1556.4 220.1 reduce-scatter.44
  1779.0 180.2 reduce-scatter.32
  1961.4 9.8 reduce-scatter.30
  1973.5 8.6 reduce-scatter.26
  1984.5 178.9 reduce-scatter.36
  2169.4 147.7 reduce-scatter.20
  2323.2 145.2 reduce-scatter.16
  2470.8 7.0 reduce-scatter.42
  2480.0 9.0 reduce-scatter.46
  2491.5 9.1 reduce-scatter.34
  2502.9 9.0 reduce-scatter.38
  2514.3 8.9 reduce-scatter.22
  2525.4 8.9 reduce-scatter.18
where the time goes:
time: 2560 us; the launch traced here: 2540 us
  waiting for transfers between devices  1410 us (55%)
  local copies, waits for them, and re-layouts  404 us (16%)
  matrix products  250 us (10%)
  blocking collectives  204 us (8%)
  other arithmetic  163 us (6%)
  starting transfers between devices  94.1 us (4%)
    reduce_scatter x2, waiting for transfers between devices, reduce_weights(): lax.psum_scatter(grads[2].astype(jnp.bfloat16), 'seq', scatter_dimension=...  349 us
    reduce_scatter x2, waiting for transfers between devices, reduce_weights(): lax.psum_scatter(grads[0].astype(jnp.bfloat16), 'seq', scatter_dimension=...  292 us
    all_gather x4, blocking collectives, combined_all(): everything = jax.tree.map(lambda part: lax.all_gather(part, axis), value)  150 us
    psum x3, waiting for transfers between devices, broadcast(): return lax.psum(block, axis)  143 us
    reduce_scatter x2, waiting for transfers between devices, reduce_weights(): lax.psum_scatter(grads[3].astype(jnp.bfloat16), 'seq', scatter_dimension=...  123 us
    reduce_scatter x2, waiting for transfers between devices, reduce_weights(): lax.psum_scatter(grads[1].astype(jnp.bfloat16), 'seq', scatter_dimension=...  118 us
    all_gather x1, waiting for transfers between devices, gather_weights(): lax.all_gather(widened[3], 'seq', axis=0, tiled=True)  101 us
    all_gather x1, waiting for transfers between devices, gather_weights(): lax.all_gather(widened[0], 'seq', axis=0, tiled=True)  89.9 us
  transfers between devices with their start and end apart: 36, of which 21 were waited for; matrix products, arithmetic and copies ran while one was open for 29% of the time, Pallas kernels for 0%

commit v1 on v0

v1 whole, which is shorter than its diff:
```python
import functools

import jax
import jax.numpy as jnp
from jax import lax
from jax.experimental import pallas as pl
from jax.experimental.pallas import tpu as pltpu
from jax.sharding import PartitionSpec as P

H = 16
HD = 64
BLOCK = 64
NGLOB = 2
NRAND = 3

EPS = 1e-05
BIG = 1e30
SCALE = HD ** (-0.5)
GELU_C = 0.7978845608028654
GELU_A = 0.044715
BF = jnp.bfloat16
F32 = jnp.float32
VMEM_LIMIT = 56 * 1024 * 1024

WHOLE = pl.BlockSpec(memory_space=pltpu.VMEM)
SMEM = pl.BlockSpec(memory_space=pltpu.SMEM)


def nn(a, b):
    return lax.dot_general(a, b, (((1,), (0,)), ((), ())), preferred_element_type=F32)


def nt(a, b):
    return lax.dot_general(a, b, (((1,), (1,)), ((), ())), preferred_element_type=F32)


def tn(a, b):
    return lax.dot_general(a, b, (((0,), (0,)), ((), ())), preferred_element_type=F32)


def params():
    return pltpu.CompilerParams(vmem_limit_bytes=VMEM_LIMIT)


def cost(flops, nbytes, trans=0):
    return pl.CostEstimate(flops=int(flops), bytes_accessed=int(nbytes), transcendentals=int(trans))


def constant(shape):
    return pl.BlockSpec(shape, lambda i: (0,) * len(shape))


def norm_stats(value):
    centre = jnp.mean(value, axis=-1, keepdims=True)
    centered = value - centre
    spread = jnp.mean(centered * centered, axis=-1, keepdims=True)
    rstd = lax.rsqrt(spread + EPS)
    return centered * rstd, rstd


def project_kernel(x_ref, gain_ref, shift_ref, w_ref, qkv_ref, h_ref, *, micros, local, lanes):
    fb = w_ref.shape[3]
    width = x_ref.shape[1]

    @pl.when(pl.program_id(0) == 0)
    def _():
        xhat, _ = norm_stats(x_ref[...].astype(F32))
        h_ref[...] = (xhat * gain_ref[...] + shift_ref[...]).astype(BF)

    y = nn(h_ref[...], w_ref[0].reshape(width, fb)).astype(BF)
    for m in range(micros):
        for i in range(fb // lanes):
            qkv_ref[m, i, 0] = y[m * local : (m + 1) * local, i * lanes : (i + 1) * lanes]


def project(x, gain, shift, w, micros, local, lanes):
    nb, n, _, fb = w.shape
    rows, width = x.shape
    groups = width // lanes
    kr = width // n
    kernel = functools.partial(project_kernel, micros=micros, local=local, lanes=lanes)
    return pl.pallas_call(
        kernel,
        grid=(3 * nb,),
        in_specs=[
            constant((rows, width)),
            constant((1, width)),
            constant((1, width)),
            pl.BlockSpec((1, n, kr, fb), lambda g: (g // 3, 0, g % 3, 0)),
        ],
        out_specs=[
            pl.BlockSpec((micros, fb // lanes, 1, local, lanes), lambda g: (0, g % nb, g // nb, 0, 0)),
            constant((rows, width)),
        ],
        out_shape=[
            jax.ShapeDtypeStruct((micros, groups, 3, local, lanes), BF),
            jax.ShapeDtypeStruct((rows, width), BF),
        ],
        compiler_params=params(),
        cost_estimate=cost(6 * rows * width * width, 14 * width * width),
        name="project",
    )(x, gain, shift, w)


def lane_item(shape):
    return lax.broadcasted_iota(jnp.int32, shape, len(shape) - 1) // HD


def block_diagonal(value, per):
    if per == 1:
        return value
    item = lane_item(value.shape)
    zero = jnp.zeros_like(value)
    return jnp.concatenate([jnp.where(item == i, value, zero) for i in range(per)], axis=0)


def take_diagonal(full, per):
    if per == 1:
        return full
    item = lane_item((BLOCK, full.shape[1]))
    out = full[:BLOCK]
    for i in range(1, per):
        out = jnp.where(item == i, full[i * BLOCK : (i + 1) * BLOCK], out)
    return out


def pick(ref, part, blocks, bpd):
    out = ref[blocks[0] // bpd, part, blocks[0] % bpd]
    item = lane_item(out.shape)
    for i in range(1, len(blocks)):
        out = jnp.where(item == i, ref[blocks[i] // bpd, part, blocks[i] % bpd], out)
    return out


def key_lists(b, table_ref, limit, nblk, per):
    shared = [0, 1, b - 1, b, jnp.minimum(b + 1, nblk - 1)]
    lists = [[s] for s in shared]
    biases = [
        None,
        None,
        jnp.where((b - 1) * BLOCK < limit, 0.0, -BIG),
        jnp.where(b * BLOCK < limit, 0.0, -BIG),
        jnp.where(((b + 1) * BLOCK < limit) & (b + 1 < nblk), 0.0, -BIG),
    ]
    item = lane_item((1, per * HD))
    for r in range(NRAND):
        blocks = [table_ref[b * per * NRAND + i * NRAND + r] for i in range(per)]
        bias = jnp.where(blocks[0] * BLOCK < limit, 0.0, -BIG)
        for i in range(1, per):
            bias = jnp.where(item == i, jnp.where(blocks[i] * BLOCK < limit, 0.0, -BIG), bias)
        lists.append(blocks)
        biases.append(bias)
    return lists, biases


def masked_scores(keys, queries, biases):
    s = nt(keys, queries)
    parts = []
    for i, bias in enumerate(biases):
        part = s[i * BLOCK : (i + 1) * BLOCK]
        parts.append(part if bias is None else part + bias)
    return jnp.concatenate(parts, axis=0)


def global_keys(ref, part, c, bpd, chunk):
    span = chunk // (bpd * BLOCK)
    return ref[pl.ds(c * span, span), part].reshape(chunk, ref.shape[4])


def attend_kernel(table_ref, limit_ref, qkv_ref, out_ref, lse_ref, s_ref, *, per, bpd, nblk):
    limit = limit_ref[0]
    lanes = per * HD
    chunk = 2 * bpd * BLOCK
    chunks = nblk * BLOCK // chunk

    def query(b):
        q = qkv_ref[b // bpd, 0, b % bpd] * jnp.asarray(SCALE, BF)
        return block_diagonal(q, per)

    both = jnp.concatenate([query(g) for g in range(NGLOB)], axis=0)
    rowid = lax.broadcasted_iota(jnp.int32, (chunk, NGLOB * lanes), 0)

    def score(c, top):
        s = nt(global_keys(qkv_ref, 1, c, bpd, chunk), both)
        s = jnp.where(c * chunk + rowid < limit, s, -BIG)
        s_ref[pl.ds(c * chunk, chunk), :] = s
        return jnp.maximum(top, jnp.max(s, axis=0, keepdims=True))

    top = lax.fori_loop(0, chunks, score, jnp.full((1, NGLOB * lanes), -BIG, F32))

    def total(c, sums):
        p = jnp.exp(s_ref[pl.ds(c * chunk, chunk), :] - top)
        s_ref[pl.ds(c * chunk, chunk), :] = p
        return sums + jnp.sum(p, axis=0, keepdims=True)

    sums = lax.fori_loop(0, chunks, total, jnp.zeros((1, NGLOB * lanes), F32))
    inv = 1.0 / sums
    lse = top + jnp.log(sums)
    for g in range(NGLOB):
        lse_ref[pl.ds(g, 1), :] = lse[:, g * lanes : (g + 1) * lanes]

    def mix(c, acc):
        w = (s_ref[pl.ds(c * chunk, chunk), :] * inv).astype(BF)
        return acc + tn(w, global_keys(qkv_ref, 2, c, bpd, chunk))

    acc = lax.fori_loop(0, chunks, mix, jnp.zeros((NGLOB * lanes, lanes), F32))
    for g in range(NGLOB):
        out_ref[g // bpd, g % bpd] = take_diagonal(acc[g * lanes : (g + 1) * lanes], per).astype(BF)

    def sparse(b, carry):
        lists, biases = key_lists(b, table_ref, limit, nblk, per)
        keys = jnp.concatenate([pick(qkv_ref, 1, blocks, bpd) for blocks in lists], axis=0)
        values = jnp.concatenate([pick(qkv_ref, 2, blocks, bpd) for blocks in lists], axis=0)
        s = masked_scores(keys, query(b), biases)
        top = jnp.max(s, axis=0, keepdims=True)
        p = jnp.exp(s - top)
        sums = jnp.sum(p, axis=0, keepdims=True)
        w = (p * (1.0 / sums)).astype(BF)
        lse_ref[pl.ds(b, 1), :] = top + jnp.log(sums)
        out_ref[b // bpd, b % bpd] = take_diagonal(tn(w, values), per).astype(BF)
        return carry

    lax.fori_loop(NGLOB, nblk, sparse, 0, unroll=2)


def attend(qkv, table, limit, per):
    n, _, bpd, _, lanes = qkv.shape
    nblk = n * bpd
    kernel = functools.partial(attend_kernel, per=per, bpd=bpd, nblk=nblk)
    return pl.pallas_call(
        kernel,
        in_specs=[SMEM, SMEM, WHOLE],
        out_specs=[WHOLE, WHOLE],
        out_shape=[
            jax.ShapeDtypeStruct((n, bpd, BLOCK, lanes), BF),
            jax.ShapeDtypeStruct((nblk, lanes), F32),
        ],
        scratch_shapes=[pltpu.VMEM((nblk * BLOCK, NGLOB * lanes), F32)],
        compiler_params=params(),
        cost_estimate=cost(40e9, 4e6, 1e7),
        name="attend",
    )(table, limit, qkv)


def attend_back_kernel(
    table_ref, limit_ref, qkv_ref, dout_ref, lse_ref, grad_ref, dk_ref, dv_ref, w_ref, dw_ref, *, per, bpd, nblk
):
    limit = limit_ref[0]
    lanes = per * HD
    chunk = 2 * bpd * BLOCK
    span = 2
    chunks = nblk * BLOCK // chunk
    scale_low = jnp.asarray(SCALE, BF)

    def query(b):
        return block_diagonal(qkv_ref[b // bpd, 0, b % bpd] * scale_low, per)

    def upstream(b):
        return block_diagonal(dout_ref[b // bpd, b % bpd], per)

    both = jnp.concatenate([query(g) for g in range(NGLOB)], axis=0)
    dboth = jnp.concatenate([upstream(g) for g in range(NGLOB)], axis=0)
    lse = jnp.concatenate([lse_ref[pl.ds(g, 1), :] for g in range(NGLOB)], axis=1)
    rowid = lax.broadcasted_iota(jnp.int32, (chunk, NGLOB * lanes), 0)

    def first(c, centre):
        s = nt(global_keys(qkv_ref, 1, c, bpd, chunk), both)
        s = jnp.where(c * chunk + rowid < limit, s, -BIG)
        w = jnp.exp(s - lse)
        dw = nt(global_keys(qkv_ref, 2, c, bpd, chunk), dboth)
        w_ref[pl.ds(c * chunk, chunk), :] = w
        dw_ref[pl.ds(c * chunk, chunk), :] = dw
        return centre + jnp.sum(w * dw, axis=0, keepdims=True)

    centre = lax.fori_loop(0, chunks, first, jnp.zeros((1, NGLOB * lanes), F32))

    def second(c, acc):
        w = w_ref[pl.ds(c * chunk, chunk), :]
        ds = (w * (dw_ref[pl.ds(c * chunk, chunk), :] - centre)).astype(BF)
        dk_ref[pl.ds(c * span, span)] = nn(ds, both).reshape(span, bpd, BLOCK, lanes)
        dv_ref[pl.ds(c * span, span)] = nn(w.astype(BF), dboth).reshape(span, bpd, BLOCK, lanes)
        return acc + tn(ds, global_keys(qkv_ref, 1, c, bpd, chunk))

    acc = lax.fori_loop(0, chunks, second, jnp.zeros((NGLOB * lanes, lanes), F32))
    for g in range(NGLOB):
        dq = take_diagonal(acc[g * lanes : (g + 1) * lanes], per) * SCALE
        grad_ref[g // bpd, 0, g % bpd] = dq.astype(BF)

    def sparse(b, carry):
        lists, biases = key_lists(b, table_ref, limit, nblk, per)
        keys = jnp.concatenate([pick(qkv_ref, 1, blocks, bpd) for blocks in lists], axis=0)
        values = jnp.concatenate([pick(qkv_ref, 2, blocks, bpd) for blocks in lists], axis=0)
        q = query(b)
        do = upstream(b)
        s = masked_scores(keys, q, biases)
        w = jnp.exp(s - lse_ref[pl.ds(b, 1), :])
        dw = nt(values, do)
        centre = jnp.sum(w * dw, axis=0, keepdims=True)
        ds = (w * (dw - centre)).astype(BF)
        grad_ref[b // bpd, 0, b % bpd] = (take_diagonal(tn(ds, keys), per) * SCALE).astype(BF)
        dk = nn(ds, q)
        dv = nn(w.astype(BF), do)
        item = lane_item((BLOCK, lanes))
        for ref, full in ((dk_ref, dk), (dv_ref, dv)):
            for k, blocks in enumerate(lists):
                part = full[k * BLOCK : (k + 1) * BLOCK]
                for i, block in enumerate(blocks):
                    term = part if len(blocks) == 1 else jnp.where(item == i, part, 0.0)
                    ref[block // bpd, block % bpd] += term
        return carry

    lax.fori_loop(NGLOB, nblk, sparse, 0, unroll=2)

    def finish(c, carry):
        grad_ref[c, 1] = dk_ref[c].astype(BF)
        grad_ref[c, 2] = dv_ref[c].astype(BF)
        return carry

    lax.fori_loop(0, nblk // bpd, finish, 0)


def attend_back(qkv, dout, lse, table, limit, per):
    n, _, bpd, _, lanes = qkv.shape
    nblk = n * bpd
    kernel = functools.partial(attend_back_kernel, per=per, bpd=bpd, nblk=nblk)
    return pl.pallas_call(
        kernel,
        in_specs=[SMEM, SMEM, WHOLE, WHOLE, WHOLE],
        out_specs=WHOLE,
        out_shape=jax.ShapeDtypeStruct((n, 3, bpd, BLOCK, lanes), BF),
        scratch_shapes=[
            pltpu.VMEM((n, bpd, BLOCK, lanes), F32),
            pltpu.VMEM((n, bpd, BLOCK, lanes), F32),
            pltpu.VMEM((nblk * BLOCK, NGLOB * lanes), F32),
            pltpu.VMEM((nblk * BLOCK, NGLOB * lanes), F32),
        ],
        compiler_params=params(),
        cost_estimate=cost(80e9, 8e6, 1e7),
        name="attend_back",
    )(table, limit, qkv, dout, lse)


def middle_kernel(
    o_ref,
    x_ref,
    g_ref,
    wo_ref,
    u_ref,
    d_ref,
    out_bias_ref,
    up_bias_ref,
    down_bias_ref,
    gain_ref,
    shift_ref,
    result_ref,
    dmid_ref,
    branch_ref,
    dout_ref,
    att_ref,
    h_ref,
    act_ref,
    pre_grad_ref,
    d_out_bias_ref,
    d_up_bias_ref,
    d_down_bias_ref,
    d_gain_ref,
    d_shift_ref,
    mid_ref,
    acc_ref,
    dh_ref,
    *,
    local,
    lanes,
):
    step = pl.program_id(0)
    micros, groups = o_ref.shape[:2]
    nb, fb = wo_ref.shape[0], wo_ref.shape[3]
    width = x_ref.shape[1]

    @pl.when(step == 0)
    def _():
        for m in range(micros):
            for i in range(groups):
                att_ref[m * local : (m + 1) * local, i * lanes : (i + 1) * lanes] = o_ref[m, i]
        att = att_ref[...]
        for b in range(nb):
            cols = slice(b * fb, (b + 1) * fb)
            y = nn(att, wo_ref[b].reshape(width, fb))
            mid_ref[:, cols] = x_ref[:, cols].astype(F32) + y + out_bias_ref[:, cols]
        mid = mid_ref[...]
        xhat, _ = norm_stats(mid)
        h_ref[...] = (xhat * gain_ref[...] + shift_ref[...]).astype(BF)
        acc_ref[...] = mid + down_bias_ref[...]
        dh_ref[...] = jnp.zeros_like(dh_ref)
        d_down_bias_ref[...] = jnp.sum(g_ref[...].astype(F32), axis=0, keepdims=True)

    up = u_ref[0].reshape(width, fb)
    pre = nn(h_ref[...], up) + up_bias_ref[...]
    square = pre * pre
    gate = jnp.tanh(GELU_C * pre * (1.0 + GELU_A * square))
    half = 0.5 * (1.0 + gate)
    act = (pre * half).astype(BF)
    slope = half + 0.5 * pre * (1.0 - gate * gate) * (GELU_C * (1.0 + 3.0 * GELU_A * square))
    act_ref[...] = act
    dact = None
    for b in range(nb):
        cols = slice(b * fb, (b + 1) * fb)
        term = nt(g_ref[:, cols], d_ref[b].reshape(fb, fb))
        dact = term if dact is None else dact + term
    pre_grad = (dact * slope).astype(BF)
    pre_grad_ref[...] = pre_grad
    d_up_bias_ref[...] = jnp.sum(pre_grad.astype(F32), axis=0, keepdims=True)
    for b in range(nb):
        cols = slice(b * fb, (b + 1) * fb)
        acc_ref[:, cols] += nn(act, d_ref[b].reshape(fb, fb))
    dh_ref[...] += nt(pre_grad, up)

    @pl.when(step == pl.num_programs(0) - 1)
    def _():
        result_ref[...] = acc_ref[...].astype(BF)
        dh = dh_ref[...]
        xhat, rstd = norm_stats(mid_ref[...])
        d_gain_ref[...] = jnp.sum(dh * xhat, axis=0, keepdims=True)
        d_shift_ref[...] = jnp.sum(dh, axis=0, keepdims=True)
        d = dh * gain_ref[...]
        inner = d - jnp.mean(d, axis=-1, keepdims=True) - xhat * jnp.mean(d * xhat, axis=-1, keepdims=True)
        dmid = g_ref[...].astype(F32) + rstd * inner
        dmid_ref[...] = dmid
        branch = dmid.astype(BF)
        branch_ref[...] = branch
        d_out_bias_ref[...] = jnp.sum(branch.astype(F32), axis=0, keepdims=True)
        dout = None
        for b in range(nb):
            term = nt(branch[:, b * fb : (b + 1) * fb], wo_ref[b].reshape(width, fb))
            dout = term if dout is None else dout + term
        dout = dout.astype(BF)
        for m in range(micros):
            for i in range(groups):
                dout_ref[m, i] = dout[m * local : (m + 1) * local, i * lanes : (i + 1) * lanes]


def middle(o, x, g, w, out_bias, up_bias, down_bias, gain, shift):
    micros, groups, local, lanes = o.shape
    rows, width = x.shape
    nb, n, _, fb = w.shape
    hidden = up_bias.shape[1]
    kr = width // n
    fr = hidden // n
    nd = fb // fr
    steps = hidden // fb
    per_b = steps // nb
    up_at = fr // kr
    out_at = up_at + per_b
    full = lambda dtype: jax.ShapeDtypeStruct((rows, width), dtype)
    vector = jax.ShapeDtypeStruct((1, width), F32)
    kernel = functools.partial(middle_kernel, local=local, lanes=lanes)
    return pl.pallas_call(
        kernel,
        grid=(steps,),
        in_specs=[
            constant((micros, groups, local, lanes)),
            constant((rows, width)),
            constant((rows, width)),
            pl.BlockSpec((nb, n, kr, fb), lambda i: (0, 0, out_at, 0)),
            pl.BlockSpec((1, n, kr, fb), lambda i: (i // per_b, 0, up_at + i % per_b, 0)),
            pl.BlockSpec((nb, nd, fr, fb), lambda i: (0, i, 0, 0)),
            constant((1, width)),
            pl.BlockSpec((1, fb), lambda i: (0, i)),
            constant((1, width)),
            constant((1, width)),
            constant((1, width)),
        ],
        out_specs=[
            constant((rows, width)),
            constant((rows, width)),
            constant((rows, width)),
            constant((micros, groups, local, lanes)),
            constant((rows, width)),
            constant((rows, width)),
            pl.BlockSpec((rows, fb), lambda i: (0, i)),
            pl.BlockSpec((rows, fb), lambda i: (0, i)),
            constant((1, width)),
            pl.BlockSpec((1, fb), lambda i: (0, i)),
            constant((1, width)),
            constant((1, width)),
            constant((1, width)),
        ],
        out_shape=[
            full(BF),
            full(F32),
            full(BF),
            jax.ShapeDtypeStruct((micros, groups, local, lanes), BF),
            full(BF),
            full(BF),
            jax.ShapeDtypeStruct((rows, hidden), BF),
            jax.ShapeDtypeStruct((rows, hidden), BF),
            vector,
            jax.ShapeDtypeStruct((1, hidden), F32),
            vector,
            vector,
            vector,
        ],
        scratch_shapes=[pltpu.VMEM((rows, width), F32)] * 3,
        compiler_params=params(),
        cost_estimate=cost(8 * rows * width * hidden + 4 * rows * width * width, 50e6),
        name="middle",
    )(o, x, g, w, w, w, out_bias, up_bias, down_bias, gain, shift)


def ffn_grads_kernel(act_ref, g_ref, h_ref, pre_grad_ref, down_ref, up_ref, ht_ref):
    nb, nd, fr, fb = down_ref.shape
    n, kr = up_ref.shape[1:3]

    @pl.when(pl.program_id(0) == 0)
    def _():
        ht_ref[...] = h_ref[...].T

    up_ref[0] = nn(ht_ref[...], pre_grad_ref[...]).astype(BF).reshape(n, kr, fb)
    act_t = act_ref[...].T
    for b in range(nb):
        y = nn(act_t, g_ref[:, b * fb : (b + 1) * fb])
        down_ref[b] = y.astype(BF).reshape(nd, fr, fb)


def ffn_grads(act, g, h, pre_grad, nb, n):
    rows, hidden = act.shape
    width = g.shape[1]
    fb = width // nb
    kr, fr = width // n, hidden // n
    steps = hidden // fb
    per_b = steps // nb
    return pl.pallas_call(
        ffn_grads_kernel,
        grid=(steps,),
        in_specs=[
            pl.BlockSpec((rows, fb), lambda i: (0, i)),
            constant((rows, width)),
            constant((rows, width)),
            pl.BlockSpec((rows, fb), lambda i: (0, i)),
        ],
        out_specs=[
            pl.BlockSpec((nb, fb // fr, fr, fb), lambda i: (0, i, 0, 0)),
            pl.BlockSpec((1, n, kr, fb), lambda i: (i // per_b, 0, i % per_b, 0)),
        ],
        out_shape=[
            jax.ShapeDtypeStruct((nb, n, fr, fb), BF),
            jax.ShapeDtypeStruct((nb, n, per_b * kr, fb), BF),
        ],
        scratch_shapes=[pltpu.VMEM((width, rows), BF)],
        compiler_params=params(),
        cost_estimate=cost(4 * rows * width * hidden, 30e6),
        name="ffn_grads",
    )(act, g, h, pre_grad)


def out_grad_kernel(att_ref, branch_ref, out_ref, at_ref):
    n, kr, fb = out_ref.shape[1:]

    @pl.when(pl.program_id(0) == 0)
    def _():
        at_ref[...] = att_ref[...].T

    out_ref[0] = nn(at_ref[...], branch_ref[...]).astype(BF).reshape(n, kr, fb)


def out_grad(att, branch, nb, n):
    rows, width = att.shape
    fb = width // nb
    kr = width // n
    return pl.pallas_call(
        out_grad_kernel,
        grid=(nb,),
        in_specs=[constant((rows, width)), pl.BlockSpec((rows, fb), lambda b: (0, b))],
        out_specs=pl.BlockSpec((1, n, kr, fb), lambda b: (b, 0, 0, 0)),
        out_shape=jax.ShapeDtypeStruct((nb, n, kr, fb), BF),
        scratch_shapes=[pltpu.VMEM((width, rows), BF)],
        compiler_params=params(),
        cost_estimate=cost(2 * rows * width * width, 5e6),
        name="out_grad",
    )(att, branch)


def qkv_grad_kernel(h_ref, grad_ref, all_ref, out_ref, ht_ref, *, local, lanes):
    micros, groups = grad_ref.shape[:2]
    n, kr, fb = out_ref.shape[1:]

    @pl.when(pl.program_id(0) == 0)
    def _():
        ht_ref[...] = h_ref[...].T
        for m in range(micros):
            for i in range(groups):
                for j in range(3):
                    col = (j * groups + i) * lanes
                    all_ref[m * local : (m + 1) * local, col : col + lanes] = grad_ref[m, i, j]

    cols = pl.ds(pl.multiple_of(pl.program_id(0) * fb, fb), fb)
    out_ref[0] = nn(ht_ref[...], all_ref[:, cols]).astype(BF).reshape(n, kr, fb)


def qkv_grad(h, grad, nb, n):
    micros, groups, _, local, lanes = grad.shape
    rows, width = h.shape
    fb = width // nb
    kr = width // n
    kernel = functools.partial(qkv_grad_kernel, local=local, lanes=lanes)
    return pl.pallas_call(
        kernel,
        grid=(3 * nb,),
        in_specs=[constant((rows, width)), constant((micros, groups, 3, local, lanes))],
        out_specs=[
            constant((rows, 3 * width)),
            pl.BlockSpec((1, n, kr, fb), lambda g: (g // 3, 0, g % 3, 0)),
        ],
        out_shape=[
            jax.ShapeDtypeStruct((rows, 3 * width), BF),
            jax.ShapeDtypeStruct((nb, n, 3 * kr, fb), BF),
        ],
        scratch_shapes=[pltpu.VMEM((width, rows), BF)],
        compiler_params=params(),
        cost_estimate=cost(6 * rows * width * width, 15e6),
        name="qkv_grad",
    )(h, grad)


def input_grad_kernel(all_ref, w_ref, x_ref, gain_ref, dmid_ref, out_ref, d_gain_ref, d_shift_ref, dh_ref):
    width = x_ref.shape[1]
    fb = w_ref.shape[3]
    term = nt(all_ref[...], w_ref[0].reshape(width, fb))

    @pl.when(pl.program_id(0) == 0)
    def _():
        dh_ref[...] = term

    @pl.when(pl.program_id(0) > 0)
    def _():
        dh_ref[...] += term

    @pl.when(pl.program_id(0) == pl.num_programs(0) - 1)
    def _():
        dh = dh_ref[...]
        xhat, rstd = norm_stats(x_ref[...].astype(F32))
        d_gain_ref[...] = jnp.sum(dh * xhat, axis=0, keepdims=True)
        d_shift_ref[...] = jnp.sum(dh, axis=0, keepdims=True)
        d = dh * gain_ref[...]
        inner = d - jnp.mean(d, axis=-1, keepdims=True) - xhat * jnp.mean(d * xhat, axis=-1, keepdims=True)
        out_ref[...] = dmid_ref[...] + rstd * inner


def input_grad(grad_all, w, x, gain, dmid):
    rows, width = x.shape
    nb, n, _, fb = w.shape
    kr = width // n
    vector = jax.ShapeDtypeStruct((1, width), F32)
    return pl.pallas_call(
        input_grad_kernel,
        grid=(3 * nb,),
        in_specs=[
            pl.BlockSpec((rows, fb), lambda g: (0, g)),
            pl.BlockSpec((1, n, kr, fb), lambda g: (g // 3, 0, g % 3, 0)),
            constant((rows, width)),
            constant((1, width)),
            constant((rows, width)),
        ],
        out_specs=[constant((rows, width)), constant((1, width)), constant((1, width))],
        out_shape=[jax.ShapeDtypeStruct((rows, width), F32), vector, vector],
        scratch_shapes=[pltpu.VMEM((rows, width), F32)],
        compiler_params=params(),
        cost_estimate=cost(6 * rows * width * width, 20e6),
        name="input_grad",
    )(grad_all, w, x, gain, dmid)


def stacked(shard, fb):
    rows, cols = shard.shape
    return shard.reshape(rows, cols // fb, fb).transpose(1, 0, 2).reshape(-1, fb)


def unstacked(stack, cols):
    fb = stack.shape[1]
    parts = cols // fb
    return stack.reshape(parts, -1, fb).transpose(1, 0, 2).reshape(-1, cols)


def body(
    tokens,
    cotangent,
    lengths,
    random_blocks,
    query_key_value_weight,
    output_weight,
    up_weight,
    down_weight,
    out_bias,
    up_bias,
    down_bias,
    gain_attn,
    shift_attn,
    gain_ffn,
    shift_ffn,
):
    n = lax.axis_size("seq")
    nb = lax.axis_size("batch")
    position = lax.axis_index("seq")
    micros, _, local, width = tokens.shape
    nblk = n * local // BLOCK
    bpd = local // BLOCK
    per = micros * H // n
    lanes = per * HD
    groups = H // per
    fb = width // nb
    both = ("batch", "seq")
    row = lambda v: v.reshape(1, -1)

    w_qkv = lax.all_gather(stacked(query_key_value_weight, fb), both)
    rest = jnp.concatenate([down_weight, stacked(up_weight, fb), output_weight], axis=0)
    w_rest = lax.all_gather(rest, both)
    w_qkv = w_qkv.reshape((nb, n) + w_qkv.shape[1:])
    w_rest = w_rest.reshape((nb, n) + w_rest.shape[1:])

    x = tokens.reshape(micros * local, width)
    g = cotangent.reshape(micros * local, width)
    micro = position * per // H
    head = position * per % H
    table = lax.dynamic_slice(
        random_blocks[:, 0], (micro, 0, head, 0), (1, nblk, per, NRAND)
    ).reshape(-1)
    limit = lax.dynamic_slice(lengths[:, 0], (micro,), (1,))

    def swap(value):
        return lax.all_to_all(value, "seq", split_axis=0, concat_axis=0, tiled=True)

    qkv, h1 = project(x, row(gain_attn), row(shift_attn), w_qkv, micros, local, lanes)
    qkv_all = swap(qkv.reshape(n, 3, local, lanes)).reshape(n, 3, bpd, BLOCK, lanes)
    mixed, lse = attend(qkv_all, table, limit, per)
    o = swap(mixed.reshape(n, local, lanes)).reshape(micros, groups, local, lanes)
    (
        result,
        dmid,
        branch,
        dout,
        att,
        h2,
        act,
        pre_grad,
        d_out_bias,
        d_up_bias,
        d_down_bias,
        d_gain_ffn,
        d_shift_ffn,
    ) = middle(
        o, x, g, w_rest, row(out_bias), row(up_bias), row(down_bias), row(gain_ffn), row(shift_ffn)
    )
    dout_all = swap(dout.reshape(n, local, lanes)).reshape(n, bpd, BLOCK, lanes)

    def scatter(grad):
        return lax.psum_scatter(
            grad.reshape((nb * n,) + grad.shape[2:]), both, scatter_dimension=0, tiled=True
        )[0].astype(F32)

    grad_down_all, grad_up_all = ffn_grads(act, g, h2, pre_grad, nb, n)
    grad_out_all = out_grad(att, branch, nb, n)
    grad_down = scatter(grad_down_all)
    grad_up = unstacked(scatter(grad_up_all), up_weight.shape[1])
    grad_out = scatter(grad_out_all)
    early = lax.psum(
        jnp.concatenate([d_out_bias, d_up_bias, d_down_bias, d_gain_ffn, d_shift_ffn], axis=1), both
    )[0]

    grads = attend_back(qkv_all, dout_all, lse, table, limit, per)
    grads_back = swap(grads.reshape(n, 3, local, lanes)).reshape(micros, groups, 3, local, lanes)
    grad_all, grad_qkv_all = qkv_grad(h1, grads_back, nb, n)
    grad_qkv = unstacked(scatter(grad_qkv_all), query_key_value_weight.shape[1])
    grad_x, d_gain_attn, d_shift_attn = input_grad(grad_all, w_qkv, x, row(gain_attn), dmid)
    late = lax.psum(jnp.concatenate([d_gain_attn, d_shift_attn], axis=1), both)[0]

    ends = [width, width + up_bias.shape[0]]
    ends += [ends[1] + width, ends[1] + 2 * width]
    s_out_bias, s_up_bias, s_down_bias, s_gain_ffn, s_shift_ffn = jnp.split(early, ends)
    return (
        result.reshape(tokens.shape),
        grad_x.reshape(tokens.shape),
        grad_qkv,
        grad_out,
        grad_up,
        grad_down,
        s_out_bias,
        s_up_bias,
        s_down_bias,
        late[:width],
        late[width:],
        s_gain_ffn,
        s_shift_ffn,
    )


def solution(mesh):
    rows = P(None, "batch", "seq", None)
    weight = P("seq", "batch")
    return jax.shard_map(
        body,
        mesh=mesh,
        in_specs=(rows, rows, P(None, "batch"), P(None, "batch", None, None, None))
        + (weight,) * 4
        + (P(),) * 7,
        out_specs=(rows, rows) + (weight,) * 4 + (P(),) * 7,
        check_vma=False,
    )
```

time: 2560 us -> 1060 us (0.41)
  waiting for transfers between devices: 1410 us -> 729 us
  local copies, waits for them, and re-layouts: 404 us -> 12 us
  matrix products: 250 us -> 0 us
  Pallas kernels: 0 us -> 164 us
  other arithmetic: 163 us -> 6.82 us
  starting transfers between devices: 94.1 us -> 8.44 us
  blocking collectives: 204 us -> 125 us
    reduce_scatter x16 -> x4, waiting for transfers between devices: 914 us -> 500 us  [scatter(): lax.psum_scatter(grad.reshape((nb * n,) + grad.shape[2:]), both, scatter_...]
    dot_general x60 -> x0, matrix products: 250 us -> none  [the longest x2 23 us: micro_step(): jnp.einsum('sncp,sncbe->spbe', select, d_incoming, precision=HIGH)]
    all_gather x4 -> x2, waiting for transfers between devices: 247 us -> 71.8 us  [the longest x1 71.8 us: body(): w_qkv = lax.all_gather(stacked(query_key_value_weight, fb), both)]
    pallas_call x0 -> x8, Pallas kernels: none -> 164 us  [the longest x1 41 us: attend_back(): pl.pallas_call(kernel, in_specs=[SMEM, SMEM, WHOLE, WHOLE, WHOLE], out_sp...]
    all_gather x8 -> x0, blocking collectives: 163 us -> none  [the longest x4 150 us: combined_all(): everything = jax.tree.map(lambda part: lax.all_gather(part, axis), value)]
    psum x4 -> x0, waiting for transfers between devices: 144 us -> none  [the longest x3 143 us: broadcast(): return lax.psum(block, axis)]
    all_to_all x4 -> x2, waiting for transfers between devices: 36 us -> 156 us  [swap(): return lax.all_to_all(value, 'seq', split_axis=0, concat_axis=0, tiled=True)]
    reshape x18 -> x5, local copies, waits for them, and re-layouts: 90.3 us -> 4.76 us  [the longest x2 2.03 us: stacked(): shard.reshape(rows, cols // fb, fb).transpose(1, 0, 2).reshape(-1, fb)]
  transfers between devices with their start and end apart: 36 -> 8, of which waited for: 21 -> 7; matrix products, arithmetic and copies ran while one was open for 29% -> 1% of each run, Pallas kernels for 0% -> 8%
where the time goes in v1:
time: 1060 us
  waiting for transfers between devices  729 us (69%)
  Pallas kernels  164 us (15%)
  blocking collectives  125 us (12%)
  between operations  14.3 us (1%)
  local copies, waits for them, and re-layouts  12 us (1%)
    reduce_scatter x4, waiting for transfers between devices, scatter(): lax.psum_scatter(grad.reshape((nb * n,) + grad.shape[2:]), both, scatter_...  500 us
    all_to_all x2, waiting for transfers between devices, swap(): return lax.all_to_all(value, 'seq', split_axis=0, concat_axis=0, tiled=True)  156 us
    all_to_all x2, blocking collectives, swap(): return lax.all_to_all(value, 'seq', split_axis=0, concat_axis=0, tiled=True)  85.1 us
    all_gather x1, waiting for transfers between devices, body(): w_qkv = lax.all_gather(stacked(query_key_value_weight, fb), both)  71.8 us
    pallas_call x1, Pallas kernels, attend_back(): pl.pallas_call(kernel, in_specs=[SMEM, SMEM, WHOLE, WHOLE, WHOLE], out_sp...  41 us
    psum x1, blocking collectives, body(): lax.psum(jnp.concatenate([d_out_bias, d_up_bias, d_down_bias, d_gain_ffn,...  40.3 us
    pallas_call x1, Pallas kernels, attend(): pl.pallas_call(kernel, in_specs=[SMEM, SMEM, WHOLE], out_specs=[WHOLE, WH...  38.1 us
    pallas_call x1, Pallas kernels, middle(): pl.pallas_call(kernel, grid=(steps,), in_specs=[constant((micros, groups,...  33.1 us
  transfers between devices with their start and end apart: 8, of which 7 were waited for; matrix products, arithmetic and copies ran while one was open for 1% of the time, Pallas kernels for 8%

profile of v1, /device:TPU:0, one launch (start us, length us, event | category | flops | bytes accessed | tf_op | source)
XLA Modules:
  0.0 1059.6 jit_solution(5702045538698142317)
XLA Ops:
  7.2 1.1 reshape.152
  9.1 1.0 copy.57
  10.1 1.8 pad_maximum_fusion
  11.9 71.8 %all-gather.4.cloned.1.call-done = bf16[32,192,512]{2,1,0:T(8,128)(2,1)} async-done(((bf16[1,192,512]{2,1,0:T(8,128)(2,1)}), bf16[32,192,512]{2,1,0:T(8,128)(2,1)}) %all-gather.4.cloned.1.call-update) | async-done | bytes 6291472 | tf_op jit(solution)/shard_map/all_gather | solution.py:714
  83.8 9.5 project.1
  93.3 4.2 all-to-all-start
  98.3 0.8 reshape.148.table_ref
  99.1 92.4 %all-to-all-done = bf16[16,3,256,128]{3,2,1,0:T(8,128)(2,1)S(1)} async-done(((bf16[16,3,256,128]{3,2,1,0:T(8,128)(2,1)}), bf16[16,3,256,128]{3,2,1,0:T(8,128)(2,1)S(1)}, u32[]{:S(2)}, u32[]{:S(2)}) %all-to-all-start) | async-done | bytes 3145760 | tf_op jit(solution)/shard_map/all_to_all | solution.py:730
  191.5 1.6 copy-done.2
  193.1 38.1 %attend.1 = (bf16[16,4,64,128]{3,2,1,0:T(8,128)(2,1)}, f32[64,128]{1,0:T(8,128)}) custom-call(s32[384]{0:T(512)} %reshape.148.table_ref, s32[1]{0:T(128)} %bitcast.limit_ref, bf16[16,3,4,64,128]{4,3,2,1,0:T(8,128)(2,1)} %bitcast.69), custom_call_target="tpu_custom_call" | custom-call | flops 40000000000 | bytes 4000000 | tf_op jit(solution)/shard_map/attend/pallas_call | solution.py:230
  231.2 52.9 %all_to_all.20 = bf16[16,256,128]{2,1,0:T(8,128)(2,1)} all-to-all(bf16[16,256,128]{2,1,0:T(8,128)(2,1)} %bitcast.82), channel_id=1, replica_groups=mesh['batch'=2,'seq'=16] {'seq'}, dimensions={0} | all-to-all | bytes 2097152 | tf_op jit(solution)/shard_map/all_to_all | solution.py:730
  284.1 33.1 %middle.1 = (bf16[512,1024]{1,0:T(8,128)(2,1)}, f32[512,1024]{1,0:T(8,128)}, bf16[512,1024]{1,0:T(8,128)(2,1)}, bf16[2,8,256,128]{3,2,1,0:T(8,128)(2,1)}, bf16[5...) custom-call(bf16[2,8,256,128]{3,2,1,0:T(8,128)(2,1)} %bitcast.79, ...), custom_call_target="tpu_custom_call" | custom-call | flops 19327352832 | bytes 50000000 | tf_op jit(solution)/shard_map/middle/pallas_call | solution.py:457
  317.2 32.2 %all_to_all.21 = bf16[16,256,128]{2,1,0:T(8,128)(2,1)} all-to-all(bf16[16,256,128]{2,1,0:T(8,128)(2,1)} %bitcast.80), channel_id=1, replica_groups=mesh['batch'=2,'seq'=16] {'seq'}, dimensions={0} | all-to-all | bytes 2097152 | tf_op jit(solution)/shard_map/all_to_all | solution.py:730
  349.4 41.0 %attend_back.1 = bf16[16,3,4,64,128]{4,3,2,1,0:T(8,128)(2,1)} custom-call(s32[384]{0:T(512)} %reshape.148.table_ref, s32[1]{0:T(128)} %bitcast.limit_ref, bf16[16,3,4,64,128]{4,3,2,1,0:T(8,128)(2,1)} %bitcast.70, bf16[16,4,64,128]{3,2,1,0:T(8,128)(2,1)} %bitcast.81, f32[64,128]{1,0:T(8,128)} %get-tuple-element.42.lse_ref), custom_call_target="tpu_custom_call" | custom-call | flops 80000000000 | bytes 8000000 | tf_op jit(solution)/shard_map/attend_back/pallas_call | solution.py:326
  390.4 4.0 all-to-all-start.3
  394.4 4.1 out_grad.1
  398.6 64.1 %all-to-all-done.3 = bf16[16,3,256,128]{3,2,1,0:T(8,128)(2,1)S(1)} async-done(((bf16[16,3,256,128]{3,2,1,0:T(8,128)(2,1)}), bf16[16,3,256,128]{3,2,1,0:T(8,128)(2,1)S(1)}, u32[]{:S(2)}, u32[]{:S(2)}) %all-to-all-start.3) | async-done | bytes 3145760 | tf_op jit(solution)/shard_map/all_to_all | solution.py:730
  462.7 1.7 copy-done.3
  464.4 9.9 qkv_grad.1
  474.4 16.1 %ffn_grads.1 = (bf16[2,16,256,512]{3,2,1,0:T(8,128)(2,1)}, bf16[2,16,256,512]{3,2,1,0:T(8,128)(2,1)}) custom-call(bf16[512,4096]{1,0:T(8,128)(2,1)} %get-tuple-element.49.act_ref, bf16[512,1024]{1,0:T(8,128)(2,1)} %bitcast.104, bf16[512,1024]{1,0:T(8,128)(2,1)} %get-tuple-element.50.h_ref, bf16[512,4096]{1,0:T(8,128)(2,1)} %get-tuple-element.51.pre_grad_ref), custom_call_target="tpu_custom_call" | custom-call | flops 8589934592 | bytes 30000000 | tf_op jit(solution)/shard_map/ffn_grads/pallas_call | solution.py:532
  491.3 64.9 %reduce-scatter.7.cloned.1.call-done = bf16[1,64,512]{2,1,0:T(8,128)(2,1)} async-done(((bf16[32,64,512]{2,1,0:T(8,128)(2,1)}), bf16[1,64,512]{2,1,0:T(8,128)(2,1)}) %reduce-scatter.7.cloned.1.call-update) | async-done | bytes 65552 | tf_op jit(solution)/shard_map/reduce_scatter | solution.py:756
  556.3 1.5 bitcast_convert_fusion.1
  557.8 12.1 %input_grad.1 = (f32[512,1024]{1,0:T(8,128)}, f32[1,1024]{1,0:T(1,128)}, f32[1,1024]{1,0:T(1,128)}) custom-call(bf16[512,3072]{1,0:T(8,128)(2,1)} %get-tuple-element.43.all_ref, bf16[2,16,192,512]{3,2,1,0:T(8,128)(2,1)} %bitcast.67, bf16[512,1024]{1,0:T(8,128)(2,1)} %bitcast.77, f32[1,1024]{1,0:T(1,128)} %bitcast.92, f32[512,1024]{1,0:T(8,128)} %get-tuple-element.44.dmid_ref), custom_call_target="tpu_custom_call" | custom-call | flops 3221225472 | bytes 20000000 | tf_op jit(solution)/shard_map/input_grad/pallas_call | solution.py:654
  570.6 40.3 %all-reduce = (f32[1,8192]{1,0:T(1,128)S(1)}, f32[1,2048]{1,0:T(1,128)S(1)}) all-reduce(f32[1,8192]{1,0:T(1,128)S(1)} %constant_dynamic-update-slice_fusion, f32[1,2048]{1,0:T(1,128)S(1)} %pad_maximum_fusion.1), channel_id=1, replica_groups=mesh['batch'=2,'seq'=16] {'batch','seq'}, use_global_device_ids=true, to_apply=%region_4.5 | all-reduce | flops 10240 | bytes 81920 | tf_op jit(solution)/shard_map/psum | solution.py:765
  612.2 66.7 %reduce-scatter.5.cloned.1.call-done = bf16[1,192,512]{2,1,0:T(8,128)(2,1)} async-done(((bf16[32,192,512]{2,1,0:T(8,128)(2,1)}), bf16[1,192,512]{2,1,0:T(8,128)(2,1)}) %reduce-scatter.5.cloned.1.call-update) | async-done | bytes 196624 | tf_op jit(solution)/shard_map/reduce_scatter | solution.py:756
  678.9 1.0 convert_bitcast_fusion
  679.8 0.8 copy.54
  680.6 183.6 %reduce-scatter.9.cloned.1.call-done = bf16[1,256,512]{2,1,0:T(8,128)(2,1)} async-done(((bf16[32,256,512]{2,1,0:T(8,128)(2,1)}), bf16[1,256,512]{2,1,0:T(8,128)(2,1)}) %reduce-scatter.9.cloned.1.call-update) | async-done | bytes 262160 | tf_op jit(solution)/shard_map/reduce_scatter | solution.py:756
  864.2 1.2 copy.50
  865.4 1.0 copy.55
  866.3 184.7 %reduce-scatter.11.cloned.1.call-done = bf16[1,256,512]{2,1,0:T(8,128)(2,1)} async-done(((bf16[32,256,512]{2,1,0:T(8,128)(2,1)}), bf16[1,256,512]{2,1,0:T(8,128)(2,1)}) %reduce-scatter.11.cloned.1.call-update) | async-done | bytes 262160 | tf_op jit(solution)/shard_map/reduce_scatter | solution.py:756
  1051.0 1.8 bitcast_convert_fusion
  (43 shorter events, 4.4 us)
Async XLA Ops:
  7.2 91.0 %copy-start = (s32[2,1,64,16,3]{2,3,4,1,0:T(8,128)S(1)}, s32[2,1,64,16,3]{2,3,4,1,0:T(8,128)}, u32[]{:S(2)}) copy-start(s32[2,1,64,16,3]{2,3,4,1,0:T(8,128)} %param.18) | copy-start | bytes 73732
  7.2 76.6 %all-gather.4.cloned.1.call-start = ((), (), s32[]{:S(2)}) async-start(), calls=%async_computation.8 | async-start | bytes 6488064 | tf_op jit(solution)/shard_map/all_gather | solution.py:714
  9.0 275.1 %all-gather.6.cloned.1.call-start = ((), (), s32[]{:S(2)}) async-start(), calls=%async_computation.13 | async-start | bytes 19464192 | tf_op jit(solution)/shard_map/all_gather | solution.py:716
  93.3 4.3 copy-start.9
  93.3 98.2 %all-to-all-start = ((bf16[16,3,256,128]{3,2,1,0:T(8,128)(2,1)}), bf16[16,3,256,128]{3,2,1,0:T(8,128)(2,1)S(1)}, u32[]{:S(2)}, u32[]{:S(2)}) async-start(bf16[16,3,256,128]{3,2,1,0:T(8,128)(2,1)} %bitcast.71), calls=%async_computation | async-start | bytes 6291456 | tf_op jit(solution)/shard_map/all_to_all | solution.py:730
  191.5 1.6 copy-start.2
  390.4 72.3 %all-to-all-start.3 = ((bf16[16,3,256,128]{3,2,1,0:T(8,128)(2,1)}), bf16[16,3,256,128]{3,2,1,0:T(8,128)(2,1)S(1)}, u32[]{:S(2)}, u32[]{:S(2)}) async-start(bf16[16,3,256,128]{3,2,1,0:T(8,128)(2,1)} %bitcast.73), calls=%async_computation.3 | async-start | bytes 6291456 | tf_op jit(solution)/shard_map/all_to_all | solution.py:730
  394.4 161.9 %reduce-scatter.7.cloned.1.call-start = ((), (), s32[]{:S(2)}) async-start(), calls=%async_computation.10 | async-start | bytes 2162688 | tf_op jit(solution)/shard_map/reduce_scatter | solution.py:756
  398.6 280.3 %reduce-scatter.5.cloned.1.call-start = ((), (), s32[]{:S(2)}) async-start(), calls=%async_computation.9 | async-start | bytes 6488064 | tf_op jit(solution)/shard_map/reduce_scatter | solution.py:756
  462.7 1.7 copy-start.3
  474.3 389.9 %reduce-scatter.9.cloned.1.call-start = ((), (), s32[]{:S(2)}) async-start(), calls=%async_computation.11 | async-start | bytes 8650752 | tf_op jit(solution)/shard_map/reduce_scatter | solution.py:756
  490.5 560.5 %reduce-scatter.11.cloned.1.call-start = ((), (), s32[]{:S(2)}) async-start(), calls=%async_computation.12 | async-start | bytes 8650752 | tf_op jit(solution)/shard_map/reduce_scatter | solution.py:756
  490.5 0.7 copy-start.8
  490.5 0.7 copy-start.4
  490.6 0.7 copy-start.7
  490.6 0.7 copy-start.6
  490.6 0.7 copy-start.5
  557.8 495.0 %copy-start.1 = (s32[2,1,64,16,3]{2,3,4,1,0:T(8,128)S(1)}, s32[2,1,64,16,3]{2,3,4,1,0:T(8,128)}, u32[]{:S(2)}) copy-start(s32[2,1,64,16,3]{2,3,4,1,0:T(8,128)} %param.18) | copy-start | bytes 73732
Sparse Core Ops, SparseCore 0:
  11.5 72.2 all-gather.3
  87.2 195.1 all-gather.5
  398.7 157.5 reduce-scatter.6
  562.7 116.1 reduce-scatter.4
  681.0 183.1 reduce-scatter.8
  866.4 184.5 reduce-scatter.10

commit v2 on v1

--- a/solution.py
+++ b/solution.py
@@ -58,36 +58,61 @@
     return centered * rstd, rstd
 
 
-def project_kernel(x_ref, gain_ref, shift_ref, w_ref, qkv_ref, h_ref, *, micros, local, lanes):
-    fb = w_ref.shape[3]
-    width = x_ref.shape[1]
+def load_pieces(refs, wa_ref, wb_ref, sems):
+    half = wa_ref.shape[1] // 2
+    copies = []
+    for i, ref in enumerate(refs):
+        target = (wa_ref, wb_ref)[i % 4 // 2].at[i // 4, pl.ds(i % 2 * half, half)]
+        copies.append(pltpu.make_async_copy(ref, target, sems.at[i]))
+    for copy in copies:
+        copy.start()
+    for copy in copies:
+        copy.wait()
+
+
+def qkv_block(core, part, place_ref, wa_ref, wb_ref):
+    n = wa_ref.shape[1]
+    rows = []
+    for s in range(n):
+        rows.append(wa_ref[core, place_ref[s], part])
+        rows.append(wb_ref[core, place_ref[n + s], part])
+    return jnp.concatenate(rows, axis=0)
+
+
+def piece_scratch(pieces, nb):
+    half = pieces[0].shape
+    full = (nb, 2 * half[0]) + half[1:]
+    return [pltpu.VMEM(full, BF), pltpu.VMEM(full, BF), pltpu.SemaphoreType.DMA((len(pieces),))]
+
+
+def project_kernel(place_ref, x_ref, gain_ref, shift_ref, *refs, micros, local, lanes):
+    *pieces, qkv_ref, h_ref, wa_ref, wb_ref, sems = refs
+    fb = wa_ref.shape[4]
 
     @pl.when(pl.program_id(0) == 0)
     def _():
         xhat, _ = norm_stats(x_ref[...].astype(F32))
         h_ref[...] = (xhat * gain_ref[...] + shift_ref[...]).astype(BF)
-
-    y = nn(h_ref[...], w_ref[0].reshape(width, fb)).astype(BF)
+        load_pieces(pieces, wa_ref, wb_ref, sems)
+
+    core = (pl.program_id(0) // 3) ^ place_ref[2 * wa_ref.shape[1]]
+    y = nn(h_ref[...], qkv_block(core, pl.program_id(0) % 3, place_ref, wa_ref, wb_ref)).astype(BF)
     for m in range(micros):
         for i in range(fb // lanes):
             qkv_ref[m, i, 0] = y[m * local : (m + 1) * local, i * lanes : (i + 1) * lanes]
 
 
-def project(x, gain, shift, w, micros, local, lanes):
-    nb, n, _, fb = w.shape
+def project(place, x, gain, shift, pieces, micros, local, lanes):
+    nb = len(pieces) // 4
+    fb = pieces[0].shape[-1]
     rows, width = x.shape
     groups = width // lanes
-    kr = width // n
     kernel = functools.partial(project_kernel, micros=micros, local=local, lanes=lanes)
     return pl.pallas_call(
         kernel,
         grid=(3 * nb,),
-        in_specs=[
-            constant((rows, width)),
-            constant((1, width)),
-            constant((1, width)),
-            pl.BlockSpec((1, n, kr, fb), lambda g: (g // 3, 0, g % 3, 0)),
-        ],
+        in_specs=[SMEM, constant((rows, width)), constant((1, width)), constant((1, width))]
+        + [pl.BlockSpec(memory_space=pl.ANY)] * len(pieces),
         out_specs=[
             pl.BlockSpec((micros, fb // lanes, 1, local, lanes), lambda g: (0, g % nb, g // nb, 0, 0)),
             constant((rows, width)),
@@ -96,10 +121,11 @@
             jax.ShapeDtypeStruct((micros, groups, 3, local, lanes), BF),
             jax.ShapeDtypeStruct((rows, width), BF),
         ],
+        scratch_shapes=piece_scratch(pieces, nb),
         compiler_params=params(),
         cost_estimate=cost(6 * rows * width * width, 14 * width * width),
         name="project",
-    )(x, gain, shift, w)
+    )(place, x, gain, shift, *pieces)
 
 
 def lane_item(shape):
@@ -340,18 +366,27 @@
     )(table, limit, qkv, dout, lse)
 
 
+MIDDLE_REFS = 16
+
+
 def middle_kernel(
+    place_ref,
     o_ref,
     x_ref,
     g_ref,
-    wo_ref,
-    u_ref,
-    d_ref,
     out_bias_ref,
     up_bias_ref,
     down_bias_ref,
     gain_ref,
     shift_ref,
+    *refs,
+    local,
+    lanes,
+):
+    *pieces, wa_ref, wb_ref, sems = refs
+    count = len(pieces) - MIDDLE_REFS
+    pieces, others = pieces[:count], pieces[count:]
+    (
     result_ref,
     dmid_ref,
     branch_ref,
@@ -368,24 +403,44 @@
     mid_ref,
     acc_ref,
     dh_ref,
-    *,
-    local,
-    lanes,
-):
+    ) = others
     step = pl.program_id(0)
     micros, groups = o_ref.shape[:2]
-    nb, fb = wo_ref.shape[0], wo_ref.shape[3]
+    nb, n, _, fb = wa_ref.shape
     width = x_ref.shape[1]
+    kr = width // n
+    kh = kr // 2
+    fr = wa_ref.shape[2] - kh
+    nd = fb // fr
+    me_core = place_ref[2 * n]
+    per_b = pl.num_programs(0) // nb
+
+    def out_block(b):
+        rows = []
+        for s in range(n):
+            rows.append(wa_ref[b ^ me_core, place_ref[s], fr : fr + kh])
+            rows.append(wb_ref[b ^ me_core, place_ref[n + s], fr : fr + kh])
+        return jnp.concatenate(rows, axis=0)
+
+    def down_block(b):
+        rows = [wa_ref[b ^ me_core, place_ref[step * nd + h], :fr] for h in range(nd)]
+        return jnp.concatenate(rows, axis=0)
+
+    def up_block():
+        core = (step // per_b) ^ me_core
+        at = pl.ds(pl.multiple_of(step % per_b * kr, kr), kr)
+        return jnp.concatenate([wb_ref[core, place_ref[n + s], at] for s in range(n)], axis=0)
 
     @pl.when(step == 0)
     def _():
+        load_pieces(pieces, wa_ref, wb_ref, sems)
         for m in range(micros):
             for i in range(groups):
                 att_ref[m * local : (m + 1) * local, i * lanes : (i + 1) * lanes] = o_ref[m, i]
         att = att_ref[...]
         for b in range(nb):
             cols = slice(b * fb, (b + 1) * fb)
-            y = nn(att, wo_ref[b].reshape(width, fb))
+            y = nn(att, out_block(b))
             mid_ref[:, cols] = x_ref[:, cols].astype(F32) + y + out_bias_ref[:, cols]
         mid = mid_ref[...]
         xhat, _ = norm_stats(mid)
@@ -394,7 +449,7 @@
         dh_ref[...] = jnp.zeros_like(dh_ref)
         d_down_bias_ref[...] = jnp.sum(g_ref[...].astype(F32), axis=0, keepdims=True)
 
-    up = u_ref[0].reshape(width, fb)
+    up = up_block()
     pre = nn(h_ref[...], up) + up_bias_ref[...]
     square = pre * pre
     gate = jnp.tanh(GELU_C * pre * (1.0 + GELU_A * square))
@@ -405,14 +460,14 @@
     dact = None
     for b in range(nb):
         cols = slice(b * fb, (b + 1) * fb)
-        term = nt(g_ref[:, cols], d_ref[b].reshape(fb, fb))
+        term = nt(g_ref[:, cols], down_block(b))
         dact = term if dact is None else dact + term
     pre_grad = (dact * slope).astype(BF)
-    pre_grad_ref[...] = pre_grad
+    pre_grad_ref[0] = pre_grad
     d_up_bias_ref[...] = jnp.sum(pre_grad.astype(F32), axis=0, keepdims=True)
     for b in range(nb):
         cols = slice(b * fb, (b + 1) * fb)
-        acc_ref[:, cols] += nn(act, d_ref[b].reshape(fb, fb))
+        acc_ref[:, cols] += nn(act, down_block(b))
     dh_ref[...] += nt(pre_grad, up)
 
     @pl.when(step == pl.num_programs(0) - 1)
@@ -431,7 +486,7 @@
         d_out_bias_ref[...] = jnp.sum(branch.astype(F32), axis=0, keepdims=True)
         dout = None
         for b in range(nb):
-            term = nt(branch[:, b * fb : (b + 1) * fb], wo_ref[b].reshape(width, fb))
+            term = nt(branch[:, b * fb : (b + 1) * fb], out_block(b))
             dout = term if dout is None else dout + term
         dout = dout.astype(BF)
         for m in range(micros):
@@ -439,52 +494,52 @@
                 dout_ref[m, i] = dout[m * local : (m + 1) * local, i * lanes : (i + 1) * lanes]
 
 
-def middle(o, x, g, w, out_bias, up_bias, down_bias, gain, shift):
+def middle(place, o, x, g, pieces, out_bias, up_bias, down_bias, gain, shift):
     micros, groups, local, lanes = o.shape
     rows, width = x.shape
-    nb, n, _, fb = w.shape
+    nb = len(pieces) // 4
+    fb = pieces[0].shape[-1]
     hidden = up_bias.shape[1]
-    kr = width // n
-    fr = hidden // n
-    nd = fb // fr
     steps = hidden // fb
+    n = 2 * pieces[0].shape[0]
     per_b = steps // nb
-    up_at = fr // kr
-    out_at = up_at + per_b
     full = lambda dtype: jax.ShapeDtypeStruct((rows, width), dtype)
     vector = jax.ShapeDtypeStruct((1, width), F32)
+    whole = lambda shape: pl.BlockSpec(shape, lambda i, place: (0,) * len(shape))
     kernel = functools.partial(middle_kernel, local=local, lanes=lanes)
     return pl.pallas_call(
         kernel,
+        grid_spec=pltpu.PrefetchScalarGridSpec(
+        num_scalar_prefetch=1,
         grid=(steps,),
         in_specs=[
-            constant((micros, groups, local, lanes)),
-            constant((rows, width)),
-            constant((rows, width)),
-            pl.BlockSpec((nb, n, kr, fb), lambda i: (0, 0, out_at, 0)),
-            pl.BlockSpec((1, n, kr, fb), lambda i: (i // per_b, 0, up_at + i % per_b, 0)),
-            pl.BlockSpec((nb, nd, fr, fb), lambda i: (0, i, 0, 0)),
-            constant((1, width)),
-            pl.BlockSpec((1, fb), lambda i: (0, i)),
-            constant((1, width)),
-            constant((1, width)),
-            constant((1, width)),
+            whole((micros, groups, local, lanes)),
+            whole((rows, width)),
+            whole((rows, width)),
+            whole((1, width)),
+            pl.BlockSpec((1, fb), lambda i, place: (0, i)),
+            whole((1, width)),
+            whole((1, width)),
+            whole((1, width)),
+        ]
+        + [pl.BlockSpec(memory_space=pl.ANY)] * len(pieces),
+        out_specs=[
+            whole((rows, width)),
+            whole((rows, width)),
+            whole((rows, width)),
+            whole((micros, groups, local, lanes)),
+            whole((rows, width)),
+            whole((rows, width)),
+            pl.BlockSpec((rows, fb), lambda i, place: (0, i)),
+            pl.BlockSpec((1, rows, fb), lambda i, place: ((i // per_b) ^ place[2 * n], 0, i % per_b)),
+            whole((1, width)),
+            pl.BlockSpec((1, fb), lambda i, place: (0, i)),
+            whole((1, width)),
+            whole((1, width)),
+            whole((1, width)),
         ],
-        out_specs=[
-            constant((rows, width)),
-            constant((rows, width)),
-            constant((rows, width)),
-            constant((micros, groups, local, lanes)),
-            constant((rows, width)),
-            constant((rows, width)),
-            pl.BlockSpec((rows, fb), lambda i: (0, i)),
-            pl.BlockSpec((rows, fb), lambda i: (0, i)),
-            constant((1, width)),
-            pl.BlockSpec((1, fb), lambda i: (0, i)),
-            constant((1, width)),
-            constant((1, width)),
-            constant((1, width)),
-        ],
+    scratch_shapes=[pltpu.VMEM((rows, width), F32)] * 3 + piece_scratch(pieces, nb),
+        ),
         out_shape=[
             full(BF),
             full(F32),
@@ -493,149 +548,227 @@
             full(BF),
             full(BF),
             jax.ShapeDtypeStruct((rows, hidden), BF),
-            jax.ShapeDtypeStruct((rows, hidden), BF),
+            jax.ShapeDtypeStruct((nb, rows, hidden // nb), BF),
             vector,
             jax.ShapeDtypeStruct((1, hidden), F32),
             vector,
             vector,
             vector,
         ],
-        scratch_shapes=[pltpu.VMEM((rows, width), F32)] * 3,
         compiler_params=params(),
         cost_estimate=cost(8 * rows * width * hidden + 4 * rows * width * width, 50e6),
         name="middle",
-    )(o, x, g, w, w, w, out_bias, up_bias, down_bias, gain, shift)
-
-
-def ffn_grads_kernel(act_ref, g_ref, h_ref, pre_grad_ref, down_ref, up_ref, ht_ref):
-    nb, nd, fr, fb = down_ref.shape
-    n, kr = up_ref.shape[1:3]
+    )(place, o, x, g, out_bias, up_bias, down_bias, gain, shift, *pieces)
+
+
+def relative_transpose(ref, target_ref, k, me, n):
+    kr = target_ref.shape[1] // n
+    value = ref[...].T
+    for s in range(n):
+        at = pl.ds(pl.multiple_of((s ^ me) * kr, kr), kr)
+        target_ref[k, at, :] = value[s * kr : (s + 1) * kr]
+
+
+def ffn_grads_kernel(place_ref, *refs, nb, n):
+    groups = [refs[i * nb : (i + 1) * nb] for i in range(6)]
+    act_refs, gc_refs, h_refs, gp_refs, att_refs, br_refs = groups
+    a_send_ref, a_keep_ref, b_send_ref, b_keep_ref, ht_ref, at_ref, out_ref = refs[6 * nb :]
+    step = pl.program_id(0)
+    me = place_ref[2 * n + 1]
+    first = n // 8
+    rows_a, fb = a_send_ref.shape[1:]
+    kr = ht_ref.shape[1] // n
+    kh = kr // 2
+    fr = rows_a - kh
+    per_b = fr // kr
+
+    @pl.when(step == 0)
+    def _():
+        total = None
+        for k in range(nb):
+            relative_transpose(h_refs[k], ht_ref, k, me, n)
+            relative_transpose(att_refs[k], at_ref, k, me, n)
+        for k in range(nb):
+            term = nn(at_ref[k], br_refs[k][...])
+            total = term if total is None else total + term
+        out_ref[...] = total.astype(BF).reshape(out_ref.shape)
+
+    send = step < 4
+    z = step % 4
+    down = None
+    for k in range(nb):
+        term = nn(act_refs[k][...].T, gc_refs[k][...])
+        down = term if down is None else down + term
+    down = down.astype(BF).reshape(first, fr, fb)
+    base_a = (2 * z + send.astype(jnp.int32)) * first
+
+    def put_a(ref):
+        for i in range(first):
+            place = i ^ (me % first)
+            ref[place, :fr] = down[i]
+        for i in range(first):
+            ref[i, fr:] = out_ref[base_a + i, :kh]
+
+    pl.when(send)(lambda: put_a(a_send_ref))
+    pl.when(jnp.logical_not(send))(lambda: put_a(a_keep_ref))
+
+    def put_b(ref, offset):
+        firsts = [pl.multiple_of(((2 * (step % 4 // 2) + i // first) * 2 * first + 2 * (i % first) + offset) * kr, kr) for i in range(2 * first)]
+        up = None
+        for k in range(nb):
+            rows = jnp.concatenate([ht_ref[k, pl.ds(at, kr), :] for at in firsts], axis=0)
+            term = nn(rows, gp_refs[k][0])
+            up = term if up is None else up + term
+        up = up.astype(BF).reshape(2 * first, kr, per_b * fb)
+        for i in range(2 * first):
+            for q in range(per_b):
+                ref[i, q * kr : (q + 1) * kr] = up[i, :, q * fb : (q + 1) * fb]
+            ref[i, fr:] = out_ref[firsts[i] // kr, kh:]
+
+    even = step % 2 == 0
+    pl.when(even & send)(lambda: put_b(b_send_ref, 1))
+    pl.when(even & jnp.logical_not(send))(lambda: put_b(b_keep_ref, 0))
+
+
+def ffn_grads(place, act, gc, h, gp, att, br, n):
+    nb = len(act)
+    rows, hidden = act[0].shape
+    fb = gc[0].shape[1]
+    width = h[0].shape[1]
+    first = n // 8
+    fr = hidden // n
+    kr = width // n
+    rows_a = fr + kr // 2
+    half = jax.ShapeDtypeStruct((n // 2, rows_a, fb), BF)
+    whole = lambda shape: pl.BlockSpec(shape, lambda i, place: (0,) * len(shape))
+    act_spec = pl.BlockSpec(
+        (rows, first * fr), lambda i, place: (0, (2 * (i % 4) + 1 - i // 4) ^ (place[2 * n + 1] // first))
+    )
+    return pl.pallas_call(
+        functools.partial(ffn_grads_kernel, nb=nb, n=n),
+        grid_spec=pltpu.PrefetchScalarGridSpec(
+            num_scalar_prefetch=1,
+            grid=(8,),
+            in_specs=[act_spec] * nb
+            + [whole((rows, fb))] * nb
+            + [whole((rows, width))] * nb
+            + [whole((1, rows, hidden // nb))] * nb
+            + [whole((rows, width))] * nb
+            + [whole((rows, fb))] * nb,
+            out_specs=[
+                pl.BlockSpec((first, rows_a, fb), lambda i, place: (jnp.minimum(i, 3), 0, 0)),
+                pl.BlockSpec((first, rows_a, fb), lambda i, place: (jnp.maximum(i - 4, 0), 0, 0)),
+                pl.BlockSpec((2 * first, rows_a, fb), lambda i, place: (jnp.minimum(i, 3) // 2, 0, 0)),
+                pl.BlockSpec((2 * first, rows_a, fb), lambda i, place: (jnp.maximum(i - 4, 0) // 2, 0, 0)),
+            ],
+            scratch_shapes=[
+                pltpu.VMEM((nb, width, rows), BF),
+                pltpu.VMEM((nb, width, rows), BF),
+                pltpu.VMEM((n, kr, fb), BF),
+            ],
+        ),
+        out_shape=[half] * 4,
+        compiler_params=params(),
+        cost_estimate=cost(4 * rows * width * hidden + 2 * rows * width * width, 40e6),
+        name="ffn_grads",
+    )(place, *act, *gc, *h, *gp, *att, *br)
+
+
+def split_kernel(place_ref, grad_ref, *out_refs, n, local, lanes):
+    micros, groups = grad_ref.shape[:2]
+    core = place_ref[2 * n]
+    count = out_refs[0].shape[1] // lanes
+    for k, out_ref in enumerate(out_refs):
+        for m in range(micros):
+            for i in range(count):
+                at = (core ^ k) * count + i
+                block = grad_ref[m, at % groups, at // groups]
+                out_ref[m * local : (m + 1) * local, i * lanes : (i + 1) * lanes] = block
+
+
+def split_by_core(place, grad, nb, n):
+    micros, groups, _, local, lanes = grad.shape
+    shape = jax.ShapeDtypeStruct((micros * local, 3 * groups * lanes // nb), BF)
+    return pl.pallas_call(
+        functools.partial(split_kernel, n=n, local=local, lanes=lanes),
+        in_specs=[SMEM, WHOLE],
+        out_specs=[WHOLE] * nb,
+        out_shape=[shape] * nb,
+        compiler_params=params(),
+        cost_estimate=cost(1e6, 6e6),
+        name="split_by_core",
+    )(place, grad)
+
+
+def qkv_grad_kernel(place_ref, *refs, nb, n):
+    h_refs, ga_refs = refs[:nb], refs[nb : 2 * nb]
+    a_send_ref, a_keep_ref, b_send_ref, b_keep_ref, ht_ref = refs[2 * nb :]
+    first = n // 8
+    _, _, kh, fb = a_send_ref.shape
 
     @pl.when(pl.program_id(0) == 0)
     def _():
-        ht_ref[...] = h_ref[...].T
-
-    up_ref[0] = nn(ht_ref[...], pre_grad_ref[...]).astype(BF).reshape(n, kr, fb)
-    act_t = act_ref[...].T
-    for b in range(nb):
-        y = nn(act_t, g_ref[:, b * fb : (b + 1) * fb])
-        down_ref[b] = y.astype(BF).reshape(nd, fr, fb)
-
-
-def ffn_grads(act, g, h, pre_grad, nb, n):
-    rows, hidden = act.shape
-    width = g.shape[1]
-    fb = width // nb
-    kr, fr = width // n, hidden // n
-    steps = hidden // fb
-    per_b = steps // nb
+        for k in range(nb):
+            relative_transpose(h_refs[k], ht_ref, k, place_ref[2 * n + 1], n)
+
+    y = None
+    for k in range(nb):
+        term = nn(ht_ref[k], ga_refs[k][...])
+        y = term if y is None else y + term
+    y = y.astype(BF).reshape(4, 2 * first, 2, kh, fb)
+    for z in range(4):
+        for i in range(first):
+            at = z * first + i
+            a_send_ref[at, 0] = y[z, first + i, 0]
+            a_keep_ref[at, 0] = y[z, i, 0]
+            b_send_ref[at, 0] = y[z, 2 * i + 1, 1]
+            b_keep_ref[at, 0] = y[z, 2 * i, 1]
+
+
+def qkv_grad(place, h, ga, n):
+    nb = len(h)
+    rows, width = h[0].shape
+    fb = ga[0].shape[1] // 3
+    kh = width // n // 2
+    half = jax.ShapeDtypeStruct((n // 2, 3, kh, fb), BF)
     return pl.pallas_call(
-        ffn_grads_kernel,
-        grid=(steps,),
-        in_specs=[
-            pl.BlockSpec((rows, fb), lambda i: (0, i)),
-            constant((rows, width)),
-            constant((rows, width)),
-            pl.BlockSpec((rows, fb), lambda i: (0, i)),
-        ],
-        out_specs=[
-            pl.BlockSpec((nb, fb // fr, fr, fb), lambda i: (0, i, 0, 0)),
-            pl.BlockSpec((1, n, kr, fb), lambda i: (i // per_b, 0, i % per_b, 0)),
-        ],
-        out_shape=[
-            jax.ShapeDtypeStruct((nb, n, fr, fb), BF),
-            jax.ShapeDtypeStruct((nb, n, per_b * kr, fb), BF),
-        ],
-        scratch_shapes=[pltpu.VMEM((width, rows), BF)],
-        compiler_params=params(),
-        cost_estimate=cost(4 * rows * width * hidden, 30e6),
-        name="ffn_grads",
-    )(act, g, h, pre_grad)
-
-
-def out_grad_kernel(att_ref, branch_ref, out_ref, at_ref):
-    n, kr, fb = out_ref.shape[1:]
-
-    @pl.when(pl.program_id(0) == 0)
-    def _():
-        at_ref[...] = att_ref[...].T
-
-    out_ref[0] = nn(at_ref[...], branch_ref[...]).astype(BF).reshape(n, kr, fb)
-
-
-def out_grad(att, branch, nb, n):
-    rows, width = att.shape
-    fb = width // nb
-    kr = width // n
-    return pl.pallas_call(
-        out_grad_kernel,
-        grid=(nb,),
-        in_specs=[constant((rows, width)), pl.BlockSpec((rows, fb), lambda b: (0, b))],
-        out_specs=pl.BlockSpec((1, n, kr, fb), lambda b: (b, 0, 0, 0)),
-        out_shape=jax.ShapeDtypeStruct((nb, n, kr, fb), BF),
-        scratch_shapes=[pltpu.VMEM((width, rows), BF)],
-        compiler_params=params(),
-        cost_estimate=cost(2 * rows * width * width, 5e6),
-        name="out_grad",
-    )(att, branch)
-
-
-def qkv_grad_kernel(h_ref, grad_ref, all_ref, out_ref, ht_ref, *, local, lanes):
-    micros, groups = grad_ref.shape[:2]
-    n, kr, fb = out_ref.shape[1:]
-
-    @pl.when(pl.program_id(0) == 0)
-    def _():
-        ht_ref[...] = h_ref[...].T
-        for m in range(micros):
-            for i in range(groups):
-                for j in range(3):
-                    col = (j * groups + i) * lanes
-                    all_ref[m * local : (m + 1) * local, col : col + lanes] = grad_ref[m, i, j]
-
-    cols = pl.ds(pl.multiple_of(pl.program_id(0) * fb, fb), fb)
-    out_ref[0] = nn(ht_ref[...], all_ref[:, cols]).astype(BF).reshape(n, kr, fb)
-
-
-def qkv_grad(h, grad, nb, n):
-    micros, groups, _, local, lanes = grad.shape
-    rows, width = h.shape
-    fb = width // nb
-    kr = width // n
-    kernel = functools.partial(qkv_grad_kernel, local=local, lanes=lanes)
-    return pl.pallas_call(
-        kernel,
-        grid=(3 * nb,),
-        in_specs=[constant((rows, width)), constant((micros, groups, 3, local, lanes))],
-        out_specs=[
-            constant((rows, 3 * width)),
-            pl.BlockSpec((1, n, kr, fb), lambda g: (g // 3, 0, g % 3, 0)),
-        ],
-        out_shape=[
-            jax.ShapeDtypeStruct((rows, 3 * width), BF),
-            jax.ShapeDtypeStruct((nb, n, 3 * kr, fb), BF),
-        ],
-        scratch_shapes=[pltpu.VMEM((width, rows), BF)],
+        functools.partial(qkv_grad_kernel, nb=nb, n=n),
+        grid=(3,),
+        in_specs=[SMEM]
+        + [constant((rows, width))] * nb
+        + [pl.BlockSpec((rows, fb), lambda t: (0, t))] * nb,
+        out_specs=[pl.BlockSpec((n // 2, 1, kh, fb), lambda t: (0, t, 0, 0))] * 4,
+        out_shape=[half] * 4,
+        scratch_shapes=[pltpu.VMEM((nb, width, rows), BF)],
         compiler_params=params(),
         cost_estimate=cost(6 * rows * width * width, 15e6),
         name="qkv_grad",
-    )(h, grad)
-
-
-def input_grad_kernel(all_ref, w_ref, x_ref, gain_ref, dmid_ref, out_ref, d_gain_ref, d_shift_ref, dh_ref):
-    width = x_ref.shape[1]
-    fb = w_ref.shape[3]
-    term = nt(all_ref[...], w_ref[0].reshape(width, fb))
-
-    @pl.when(pl.program_id(0) == 0)
+    )(place, *h, *ga)
+
+
+def input_grad_kernel(place_ref, x_ref, gain_ref, dmid_ref, *refs, nb):
+    grad_refs = refs[:nb]
+    *pieces, _, out_ref, d_gain_ref, d_shift_ref, dh_ref, wa_ref, wb_ref, sems = refs[nb:]
+    step = pl.program_id(0)
+
+    @pl.when(step == 0)
     def _():
-        dh_ref[...] = term
-
-    @pl.when(pl.program_id(0) > 0)
+        load_pieces(pieces, wa_ref, wb_ref, sems)
+
+    total = None
+    for k in range(nb):
+        term = nt(grad_refs[k][...], qkv_block(k, step, place_ref, wa_ref, wb_ref))
+        total = term if total is None else total + term
+
+    @pl.when(step == 0)
     def _():
-        dh_ref[...] += term
-
-    @pl.when(pl.program_id(0) == pl.num_programs(0) - 1)
+        dh_ref[...] = total
+
+    @pl.when(step > 0)
+    def _():
+        dh_ref[...] += total
+
+    @pl.when(step == pl.num_programs(0) - 1)
     def _():
         dh = dh_ref[...]
         xhat, rstd = norm_stats(x_ref[...].astype(F32))
@@ -646,39 +779,163 @@
         out_ref[...] = dmid_ref[...] + rstd * inner
 
 
-def input_grad(grad_all, w, x, gain, dmid):
+def input_grad(place, grads, pieces, x, gain, dmid, earlier):
     rows, width = x.shape
-    nb, n, _, fb = w.shape
-    kr = width // n
+    nb = len(grads)
+    fb = pieces[0].shape[-1]
     vector = jax.ShapeDtypeStruct((1, width), F32)
     return pl.pallas_call(
-        input_grad_kernel,
-        grid=(3 * nb,),
-        in_specs=[
-            pl.BlockSpec((rows, fb), lambda g: (0, g)),
-            pl.BlockSpec((1, n, kr, fb), lambda g: (g // 3, 0, g % 3, 0)),
-            constant((rows, width)),
-            constant((1, width)),
-            constant((rows, width)),
-        ],
+        functools.partial(input_grad_kernel, nb=nb),
+        grid=(3,),
+        in_specs=[SMEM, constant((rows, width)), constant((1, width)), constant((rows, width))]
+        + [pl.BlockSpec((rows, fb), lambda t: (0, t))] * nb
+        + [pl.BlockSpec(memory_space=pl.ANY)] * (len(pieces) + 1),
         out_specs=[constant((rows, width)), constant((1, width)), constant((1, width))],
         out_shape=[jax.ShapeDtypeStruct((rows, width), F32), vector, vector],
-        scratch_shapes=[pltpu.VMEM((rows, width), F32)],
+        scratch_shapes=[pltpu.VMEM((rows, width), F32)] + piece_scratch(pieces, nb),
         compiler_params=params(),
         cost_estimate=cost(6 * rows * width * width, 20e6),
         name="input_grad",
-    )(grad_all, w, x, gain, dmid)
-
-
-def stacked(shard, fb):
-    rows, cols = shard.shape
-    return shard.reshape(rows, cols // fb, fb).transpose(1, 0, 2).reshape(-1, fb)
-
-
-def unstacked(stack, cols):
-    fb = stack.shape[1]
-    parts = cols // fb
-    return stack.reshape(parts, -1, fb).transpose(1, 0, 2).reshape(-1, cols)
+    )(place, x, gain, dmid, *grads, *pieces, earlier)
+
+
+def swap_with(value, axis, k):
+    size = lax.axis_size(axis)
+    return lax.ppermute(value, axis, [(i, i ^ k) for i in range(size)])
+
+
+def low_bits(n):
+    return [1 << i for i in range((n // 4).bit_length() - 1)]
+
+
+def direct(shard, n):
+    return [swap_with(shard, "seq", k * n // 4) for k in range(1, 4)]
+
+
+def move(value, step, n):
+    quarter = n // 4
+    if step > 0:
+        return lax.ppermute(value, "seq", [(i, i + quarter) for i in range(n - quarter)])
+    return lax.ppermute(value, "seq", [(i + quarter, i) for i in range(n - quarter)])
+
+
+def line_gather(shard, n):
+    up, down = [shard], [shard]
+    for _ in range(3):
+        up.append(move(up[-1], 1, n))
+        down.append(move(down[-1], -1, n))
+    return up[1:], down[1:]
+
+
+def line_halves(shard, up, down, position, n):
+    z = position // (n // 4)
+    by_distance = {**{-i - 1: up[i] for i in range(3)}, **{i + 1: down[i] for i in range(3)}}
+    arrived = []
+    for k in range(1, 4):
+        found = by_distance[k]
+        for at in range(1, 4):
+            found = jnp.where(z == at, by_distance[(at ^ k) - at], found)
+        arrived.append(found)
+    return halves(shard, arrived)
+
+
+def line_reduce(total, position, n):
+    z = position // (n // 4)
+    block = lambda to: lax.dynamic_index_in_dim(total, z ^ jnp.clip(to, 0, 3), 0, keepdims=False)
+    up, down = block(z + 3), block(z - 3)
+    for step in range(1, 4):
+        up, down = move(up, 1, n), move(down, -1, n)
+        if step < 3:
+            up = plus(block(z + 3 - step), up)
+            down = plus(block(z - 3 + step), down)
+    return up, down
+
+
+def halves(shard, arrived):
+    both = jnp.stack([shard] + arrived)
+    return both[:, 0], both[:, 1]
+
+
+def together(*values):
+    return lax.optimization_barrier(values)
+
+
+def gather_rest(part, bits):
+    for bit in bits[:-1]:
+        part = jnp.concatenate([part, swap_with(part, "seq", bit)])
+    return part
+
+
+def gather_last(part, bits):
+    return [part, swap_with(part, "seq", bits[-1])]
+
+
+def gather_cores(pieces, nb):
+    out = list(pieces)
+    for k in range(1, nb):
+        out += [swap_with(piece, "batch", k) for piece in pieces]
+    return out
+
+
+def place_of(relative, bits, n):
+    place = relative // (n // 4)
+    for i, bit in enumerate(bits):
+        place = place + jnp.where(relative & bit, 4 << i, 0)
+    return place
+
+
+def place_table(position, core, n):
+    relative = jnp.arange(n, dtype=jnp.int32) ^ position
+    bits = low_bits(n)
+    ends = jnp.stack([core, position]).astype(jnp.int32)
+    return jnp.concatenate([place_of(relative, bits, n), place_of(relative, bits[::-1], n), ends])
+
+
+def plus(value, arrived):
+    return (value.astype(F32) + arrived.astype(F32)).astype(BF)
+
+
+def reduce_first(a_send, b_send, n):
+    return swap_with(a_send, "seq", n // 8), swap_with(b_send, "seq", 1)
+
+
+def split_next(total):
+    m = total.shape[1] // 2
+    return total[:, :m], total[:, m:]
+
+
+def reduce_steps(total, bit_of, n):
+    total = total.reshape((4, n // 8) + total.shape[1:])
+    while total.shape[1] > 1:
+        keep, send = split_next(total)
+        total = plus(keep, swap_with(send, "seq", bit_of(send.shape[1])))
+    return total[:, 0]
+
+
+def reduce_rest(a, b, n):
+    a = reduce_steps(a, lambda m: m, n)
+    b = reduce_steps(b, lambda m: 2 * m, n)
+    return jnp.stack([a, b], axis=1)
+
+
+def reduce_direct(total, n):
+    return [swap_with(total[k], "seq", k * n // 4) for k in range(1, 4)]
+
+
+def reduce_last(total, arrived):
+    out = total[0].astype(F32)
+    for term in arrived:
+        out = out + term.astype(F32)
+    return out[0], out[1]
+
+
+def total_over_all(value, nb, n):
+    for axis, size in (("batch", nb), ("seq", n)):
+        k = 1
+        while k < size:
+            value = value + swap_with(value, axis, k)
+            k *= 2
+    return value
 
 
 def body(
@@ -701,22 +958,37 @@
     n = lax.axis_size("seq")
     nb = lax.axis_size("batch")
     position = lax.axis_index("seq")
+    core = lax.axis_index("batch")
     micros, _, local, width = tokens.shape
+    hidden = up_bias.shape[0]
     nblk = n * local // BLOCK
     bpd = local // BLOCK
     per = micros * H // n
     lanes = per * HD
     groups = H // per
     fb = width // nb
-    both = ("batch", "seq")
+    kr = width // n
+    kh = kr // 2
+    fr = hidden // n
+    per_b = hidden // width
+    bits = low_bits(n)
     row = lambda v: v.reshape(1, -1)
-
-    w_qkv = lax.all_gather(stacked(query_key_value_weight, fb), both)
-    rest = jnp.concatenate([down_weight, stacked(up_weight, fb), output_weight], axis=0)
-    w_rest = lax.all_gather(rest, both)
-    w_qkv = w_qkv.reshape((nb, n) + w_qkv.shape[1:])
-    w_rest = w_rest.reshape((nb, n) + w_rest.shape[1:])
-
+    place = place_table(position, core, n)
+
+    shard = query_key_value_weight.reshape(2, kh, 3, fb).transpose(0, 2, 1, 3)
+    part_a, part_b = halves(shard, direct(shard, n))
+    stacked_up = up_weight.reshape(kr, per_b, fb).transpose(1, 0, 2).reshape(per_b * kr, fb)
+    rest = jnp.stack(
+        [
+            jnp.concatenate([down_weight, output_weight[:kh]]),
+            jnp.concatenate([stacked_up, output_weight[kh:]]),
+        ]
+    )
+    part_a, rest = together(part_a, rest)
+    rest_up, rest_down = line_gather(rest, n)
+    part_a = gather_rest(part_a, bits)
+    part_b = gather_rest(part_b, bits[::-1])
+    qkv_pieces = gather_cores(gather_last(part_a, bits) + gather_last(part_b, bits[::-1]), nb)
     x = tokens.reshape(micros * local, width)
     g = cotangent.reshape(micros * local, width)
     micro = position * per // H
@@ -729,9 +1001,25 @@
     def swap(value):
         return lax.all_to_all(value, "seq", split_axis=0, concat_axis=0, tiled=True)
 
-    qkv, h1 = project(x, row(gain_attn), row(shift_attn), w_qkv, micros, local, lanes)
+    def over_cores(value):
+        return [value] + [swap_with(value, "batch", k) for k in range(1, nb)]
+
+    def columns_over_cores(value, cols):
+        mine = lambda c: lax.dynamic_slice_in_dim(value, c * cols, cols, axis=1)
+        return [mine(core)] + [swap_with(mine(core ^ k), "batch", k) for k in range(1, nb)]
+
+    qkv, h1 = project(place, x, row(gain_attn), row(shift_attn), qkv_pieces, micros, local, lanes)
+    qkv, rest_up[2], rest_down[2] = together(qkv, rest_up[2], rest_down[2])
+    rest_a, rest_b = line_halves(rest, rest_up, rest_down, position, n)
     qkv_all = swap(qkv.reshape(n, 3, local, lanes)).reshape(n, 3, bpd, BLOCK, lanes)
+    rest_a = gather_rest(rest_a, bits)
+    rest_b = gather_rest(rest_b, bits[::-1])
+    qkv_all, rest_a, rest_b = together(qkv_all, rest_a, rest_b)
+    rest_a = gather_last(rest_a, bits)
+    rest_b = gather_last(rest_b, bits[::-1])
     mixed, lse = attend(qkv_all, table, limit, per)
+    mixed, rest_a[1], rest_b[1] = together(mixed, rest_a[1], rest_b[1])
+    rest_pieces = gather_cores(rest_a + rest_b, nb)
     o = swap(mixed.reshape(n, local, lanes)).reshape(micros, groups, local, lanes)
     (
         result,
@@ -748,34 +1036,63 @@
         d_gain_ffn,
         d_shift_ffn,
     ) = middle(
-        o, x, g, w_rest, row(out_bias), row(up_bias), row(down_bias), row(gain_ffn), row(shift_ffn)
+        place,
+        o,
+        x,
+        g,
+        rest_pieces,
+        row(out_bias),
+        row(up_bias),
+        row(down_bias),
+        row(gain_ffn),
+        row(shift_ffn),
     )
+    h1_cores = over_cores(h1)
     dout_all = swap(dout.reshape(n, local, lanes)).reshape(n, bpd, BLOCK, lanes)
 
-    def scatter(grad):
-        return lax.psum_scatter(
-            grad.reshape((nb * n,) + grad.shape[2:]), both, scatter_dimension=0, tiled=True
-        )[0].astype(F32)
-
-    grad_down_all, grad_up_all = ffn_grads(act, g, h2, pre_grad, nb, n)
-    grad_out_all = out_grad(att, branch, nb, n)
-    grad_down = scatter(grad_down_all)
-    grad_up = unstacked(scatter(grad_up_all), up_weight.shape[1])
-    grad_out = scatter(grad_out_all)
-    early = lax.psum(
-        jnp.concatenate([d_out_bias, d_up_bias, d_down_bias, d_gain_ffn, d_shift_ffn], axis=1), both
-    )[0]
-
+    parts = ffn_grads(
+        place,
+        over_cores(act),
+        columns_over_cores(g, fb),
+        over_cores(h2),
+        [pre_grad] + [swap_with(pre_grad[k : k + 1], "batch", k) for k in range(1, nb)],
+        over_cores(att),
+        columns_over_cores(branch, fb),
+        n,
+    )
+    dout_all, *parts = together(dout_all, *parts)
+    a_send, a_keep, b_send, b_keep = parts
+    first_a, first_b = reduce_first(a_send, b_send, n)
     grads = attend_back(qkv_all, dout_all, lse, table, limit, per)
+    grads, first_a, first_b = together(grads, first_a, first_b)
     grads_back = swap(grads.reshape(n, 3, local, lanes)).reshape(micros, groups, 3, local, lanes)
-    grad_all, grad_qkv_all = qkv_grad(h1, grads_back, nb, n)
-    grad_qkv = unstacked(scatter(grad_qkv_all), query_key_value_weight.shape[1])
-    grad_x, d_gain_attn, d_shift_attn = input_grad(grad_all, w_qkv, x, row(gain_attn), dmid)
-    late = lax.psum(jnp.concatenate([d_gain_attn, d_shift_attn], axis=1), both)[0]
-
-    ends = [width, width + up_bias.shape[0]]
-    ends += [ends[1] + width, ends[1] + 2 * width]
-    s_out_bias, s_up_bias, s_down_bias, s_gain_ffn, s_shift_ffn = jnp.split(early, ends)
+    reduced = reduce_rest(plus(a_keep, first_a), plus(b_keep, first_b), n)
+    early = [d_out_bias, d_up_bias, d_down_bias, d_gain_ffn, d_shift_ffn]
+    early_sums = total_over_all(jnp.concatenate(early, axis=1), nb, n)[0]
+    grads_back, early_sums, reduced = together(grads_back, early_sums, reduced)
+
+    own_grads = split_by_core(place, grads_back, nb, n)
+    rest_arrived = line_reduce(reduced, position, n)
+
+    grad_cores = [own_grads[0]] + [swap_with(own_grads[k], "batch", k) for k in range(1, nb)]
+    a_send, a_keep, b_send, b_keep = qkv_grad(place, h1_cores, grad_cores, n)
+    first_a, first_b = reduce_first(a_send, b_send, n)
+    grad_x, d_gain_attn, d_shift_attn = input_grad(
+        place, own_grads, qkv_pieces, x, row(gain_attn), dmid, a_keep
+    )
+    late = jnp.concatenate([d_gain_attn, d_shift_attn], axis=1)
+    late, first_a, first_b = together(late, first_a, first_b)
+    late = total_over_all(late, nb, n)[0]
+    qkv_reduced = reduce_rest(plus(a_keep, first_a), plus(b_keep, first_b), n)
+    qkv_reduced, *rest_arrived = together(qkv_reduced, *rest_arrived)
+    grad_a, grad_b = reduce_last(qkv_reduced, reduce_direct(qkv_reduced, n))
+    grad_qkv = jnp.stack([grad_a, grad_b]).transpose(0, 2, 1, 3).reshape(kr, 3 * fb)
+    grad_a, grad_b = reduce_last(reduced, rest_arrived)
+    grad_down = grad_a[:fr]
+    grad_up = grad_b[:fr].reshape(per_b, kr, fb).transpose(1, 0, 2).reshape(kr, per_b * fb)
+    grad_out = jnp.concatenate([grad_a[fr:], grad_b[fr:]])
+    ends = [width, width + hidden, 2 * width + hidden, 3 * width + hidden]
+    s_out_bias, s_up_bias, s_down_bias, s_gain_ffn, s_shift_ffn = jnp.split(early_sums, ends)
     return (
         result.reshape(tokens.shape),
         grad_x.reshape(tokens.shape),

time: 1060 us -> 601 us (0.57)
  waiting for transfers between devices: 729 us -> 253 us
  blocking collectives: 125 us -> 0 us
  starting transfers between devices: 8.44 us -> 120 us
  other arithmetic: 6.82 us -> 22.6 us
  between operations: 14.3 us -> 2.06 us
    reduce_scatter x4 -> x0, waiting for transfers between devices: 500 us -> none  [scatter(): lax.psum_scatter(grad.reshape((nb * n,) + grad.shape[2:]), both, scatter_...]
    ppermute x0 -> x60, waiting for transfers between devices: none -> 228 us  [the longest x48 188 us: swap_with(): return lax.ppermute(value, axis, [(i, i ^ k) for i in range(size)])]
    all_to_all x2 -> x4, waiting for transfers between devices: 156 us -> 24.6 us  [swap(): return lax.all_to_all(value, 'seq', split_axis=0, concat_axis=0, tiled=True)]
    ppermute x0 -> x60, starting transfers between devices: none -> 92.7 us  [the longest x48 55.6 us: swap_with(): return lax.ppermute(value, axis, [(i, i ^ k) for i in range(size)])]
    all_to_all x2 -> x0, blocking collectives: 85.1 us -> none  [swap(): return lax.all_to_all(value, 'seq', split_axis=0, concat_axis=0, tiled=True)]
    all_gather x2 -> x0, waiting for transfers between devices: 71.8 us -> none  [the longest x1 71.8 us: body(): w_qkv = lax.all_gather(stacked(query_key_value_weight, fb), both)]
    psum x1 -> x0, blocking collectives: 40.3 us -> none  [body(): lax.psum(jnp.concatenate([d_out_bias, d_up_bias, d_down_bias, d_gain_ffn,...]
    all_to_all x2 -> x4, starting transfers between devices: 8.19 us -> 27.8 us  [swap(): return lax.all_to_all(value, 'seq', split_axis=0, concat_axis=0, tiled=True)]
  transfers between devices with their start and end apart: 8 -> 64, of which waited for: 7 -> 29; matrix products, arithmetic and copies ran while one was open for 1% -> 6% of each run, Pallas kernels for 8% -> 22%
where the time goes in v2:
time: 601 us; the launch traced here: 592 us
  waiting for transfers between devices  253 us (42%)
  Pallas kernels  174 us (29%)
  starting transfers between devices  120 us (20%)
  other arithmetic  22.6 us (4%)
  local copies, waits for them, and re-layouts  20.4 us (3%)
    ppermute x48, waiting for transfers between devices, swap_with(): return lax.ppermute(value, axis, [(i, i ^ k) for i in range(size)])  188 us
    ppermute x48, starting transfers between devices, swap_with(): return lax.ppermute(value, axis, [(i, i ^ k) for i in range(size)])  55.6 us
    pallas_call x1, Pallas kernels, attend_back(): pl.pallas_call(kernel, in_specs=[SMEM, SMEM, WHOLE, WHOLE, WHOLE], out_sp...  40.9 us
    pallas_call x1, Pallas kernels, middle(): pl.pallas_call(kernel, grid_spec=pltpu.PrefetchScalarGridSpec(num_scalar_...  38.6 us
    pallas_call x1, Pallas kernels, attend(): pl.pallas_call(kernel, in_specs=[SMEM, SMEM, WHOLE], out_specs=[WHOLE, WH...  37.9 us
    ppermute x6, starting transfers between devices, move(): lax.ppermute(value, 'seq', [(i, i + quarter) for i in range(n - quarter)])  29.1 us
    all_to_all x4, starting transfers between devices, swap(): return lax.all_to_all(value, 'seq', split_axis=0, concat_axis=0, tiled=True)  27.8 us
    all_to_all x4, waiting for transfers between devices, swap(): return lax.all_to_all(value, 'seq', split_axis=0, concat_axis=0, tiled=True)  24.6 us
  transfers between devices with their start and end apart: 64, of which 29 were waited for; matrix products, arithmetic and copies ran while one was open for 6% of the time, Pallas kernels for 22%

profile of v2, /device:TPU:0, one launch (start us, length us, event | category | flops | bytes accessed | tf_op | source)
XLA Modules:
  0.0 592.4 jit_solution(9296723002547656724)
XLA Ops:
  13.2 8.8 %collective-permute-done.1 = bf16[2,3,32,512]{3,2,1,0:T(8,128)(2,1)S(1)} collective-permute-done((bf16[2,3,32,512]{3,2,1,0:T(8,128)(2,1)S(1)}, bf16[2,3,32,512]{3,2,1,0:T(8,128)(2,1)S(1)}, u32[]{:S(2)}, u32[]{:S(2)}) %collective-permute-start.1) | collective-permute-done | bytes 196640 | tf_op jit(solution)/shard_map/ppermute | solution.py:804
  25.3 5.3 collective-permute-done.3
  34.0 6.5 %collective-permute-start.11 = (bf16[2,288,512]{2,1,0:T(8,128)(2,1)S(1)}, bf16[2,288,512]{2,1,0:T(8,128)(2,1)S(1)}, u32[]{:S(2)}, u32[]{:S(2)}) collective-permute-start(bf16[2,288,512]{2,1,0:T(8,128)(2,1)S(1)} %pad_maximum_fusion.7), channel_id=1, source_target_pairs={{0,4},{1,5},{2,6},{3,7},{4,8},{5,9},{6,10},{7,11},{8,12},{9,13},{1... | collective-permute-start | bytes 1769480 | tf_op jit(solution)/shard_map/ppermute | solution.py:818
  41.8 11.6 %collective-permute-done.11 = bf16[2,288,512]{2,1,0:T(8,128)(2,1)S(1)} collective-permute-done((bf16[2,288,512]{2,1,0:T(8,128)(2,1)S(1)}, bf16[2,288,512]{2,1,0:T(8,128)(2,1)S(1)}, u32[]{:S(2)}, u32[]{:S(2)}) %collective-permute-start.11) | collective-permute-done | bytes 589856 | tf_op jit(solution)/shard_map/ppermute | solution.py:818
  53.5 5.3 collective-permute-start.12
  61.6 8.5 %collective-permute-done.12 = bf16[2,288,512]{2,1,0:T(8,128)(2,1)} collective-permute-done((bf16[2,288,512]{2,1,0:T(8,128)(2,1)S(1)}, bf16[2,288,512]{2,1,0:T(8,128)(2,1)}, u32[]{:S(2)}, u32[]{:S(2)}) %collective-permute-start.12) | collective-permute-done | bytes 589856 | tf_op jit(solution)/shard_map/ppermute | solution.py:818
  70.1 5.3 collective-permute-start.13
  77.4 10.0 %project.1 = (bf16[2,8,3,256,128]{4,3,2,1,0:T(8,128)(2,1)}, bf16[512,1024]{1,0:T(8,128)(2,1)}) custom-call(s32[34]{0:T(128)} %pad_add_fusion.place_ref, bf16[512,1024]{1,0:T(8,128)(2,1)} %bitcast.134, f32[1,1024]{1,0:T(1,128)} %bitcast.155, f32[1,1024]{1,0:T(1,128)} %bitcast.161, bf16[8,3,32,512]{3,2,1,0:T(8,128)(2,1)} %copy-done.9, ...), custom_call_target="tpu_custom_call" | custom-call | flops 3221225472 | bytes 14680064 | tf_op jit(solution)/shard_map/project/pallas_call | solution.py:111
  91.2 4.6 all-to-all-start
  103.6 50.9 %collective-permute-done.18 = bf16[4,288,512]{2,1,0:T(8,128)(2,1)} collective-permute-done((bf16[4,288,512]{2,1,0:T(8,128)(2,1)S(1)}, bf16[4,288,512]{2,1,0:T(8,128)(2,1)}, u32[]{:S(2)}, u32[]{:S(2)}) %collective-permute-start.18) | collective-permute-done | bytes 1179680 | tf_op jit(solution)/shard_map/ppermute | solution.py:804
  162.4 37.9 %attend.1 = (bf16[16,4,64,128]{3,2,1,0:T(8,128)(2,1)}, f32[64,128]{1,0:T(8,128)}) custom-call(s32[384]{0:T(512)} %reshape.139.table_ref, s32[1]{0:T(128)} %bitcast.2.limit_ref, bf16[16,3,4,64,128]{4,3,2,1,0:T(8,128)(2,1)} %bitcast.21.qkv_ref), custom_call_target="tpu_custom_call" | custom-call | flops 40000000000 | bytes 4000000 | tf_op jit(solution)/shard_map/attend/pallas_call | solution.py:256
  200.3 9.1 %collective-permute-done.19.refs_1_ = bf16[8,288,512]{2,1,0:T(8,128)(2,1)S(1)} collective-permute-done((bf16[8,288,512]{2,1,0:T(8,128)(2,1)}, bf16[8,288,512]{2,1,0:T(8,128)(2,1)S(1)}, u32[]{:S(2)}, u32[]{:S(2)}) %collective-permute-start.19) | collective-permute-done | bytes 2359328 | tf_op jit(solution)/shard_map/ppermute | solution.py:804
  209.4 5.0 collective-permute-done.20.refs_3_
  214.9 10.3 %all-to-all-start.1 = ((bf16[16,256,128]{2,1,0:T(8,128)(2,1)}), bf16[16,256,128]{2,1,0:T(8,128)(2,1)S(1)}, u32[]{:S(2)}, u32[]{:S(2)}) async-start(bf16[16,256,128]{2,1,0:T(8,128)(2,1)} %bitcast.139), calls=%async_computation.1 | async-start | bytes 2097152 | tf_op jit(solution)/shard_map/all_to_all | solution.py:1002
  225.2 24.6 %all-to-all-done.1 = bf16[16,256,128]{2,1,0:T(8,128)(2,1)S(1)} async-done(((bf16[16,256,128]{2,1,0:T(8,128)(2,1)}), bf16[16,256,128]{2,1,0:T(8,128)(2,1)S(1)}, u32[]{:S(2)}, u32[]{:S(2)}) %all-to-all-start.1) | async-done | bytes 1048608 | tf_op jit(solution)/shard_map/all_to_all | solution.py:1002
  250.7 38.6 %middle.1 = (bf16[512,1024]{1,0:T(8,128)(2,1)}, f32[512,1024]{1,0:T(8,128)}, bf16[512,1024]{1,0:T(8,128)(2,1)}, bf16[2,8,256,128]{3,2,1,0:T(8,128)(2,1)}, bf16[5...) custom-call(s32[34]{0:T(128)} %pad_add_fusion.place_ref, ...), custom_call_target="tpu_custom_call" | custom-call | flops 19327352832 | bytes 50000000 | tf_op jit(solution)/shard_map/middle/pallas_call | solution.py:510
  291.7 6.1 %all-to-all-start.2 = ((bf16[16,256,128]{2,1,0:T(8,128)(2,1)}), bf16[16,256,128]{2,1,0:T(8,128)(2,1)S(1)}, u32[]{:S(2)}, u32[]{:S(2)}) async-start(bf16[16,256,128]{2,1,0:T(8,128)(2,1)} %bitcast.41), calls=%async_computation.2 | async-start | bytes 2097152 | tf_op jit(solution)/shard_map/all_to_all | solution.py:1002
  307.2 22.1 %ffn_grads.1 = (bf16[8,288,512]{2,1,0:T(8,128)(2,1)}, bf16[8,288,512]{2,1,0:T(8,128)(2,1)}, bf16[8,288,512]{2,1,0:T(8,128)(2,1)}, bf16[8,288,512]{2,1,0:T(8,128)(2,1)}) custom-call(s32[34]{0:T(128)} %pad_add_fusion.place_ref, bf16[512,4096]{1,0:T(8,128)(2,1)} %get-tuple-element.87.refs_0_, bf16[512,4096]{1,0:T(8,128)(2,1)} %collective-permute-done.25.refs_1_, ...), custom_call_target="tpu_custom_call" | custom-call | flops 9663676416 | bytes 40000000 | tf_op jit(solution)/shard_map/ffn_grads/pallas_call | solution.py:647
  332.8 40.9 %attend_back.1 = bf16[16,3,4,64,128]{4,3,2,1,0:T(8,128)(2,1)} custom-call(s32[384]{0:T(512)} %reshape.139.table_ref, s32[1]{0:T(128)} %bitcast.2.limit_ref, bf16[16,3,4,64,128]{4,3,2,1,0:T(8,128)(2,1)} %bitcast.21.qkv_ref, bf16[16,4,64,128]{3,2,1,0:T(8,128)(2,1)} %bitcast.137, f32[64,128]{1,0:T(8,128)} %get-tuple-element.97.lse_ref), custom_call_target="tpu_custom_call" | custom-call | flops 80000000000 | bytes 8000000 | tf_op jit(solution)/shard_map/attend_back/pallas_call | solution.py:352
  373.7 9.4 %collective-permute-done.31 = bf16[8,288,512]{2,1,0:T(8,128)(2,1)S(1)} collective-permute-done((bf16[8,288,512]{2,1,0:T(8,128)(2,1)}, bf16[8,288,512]{2,1,0:T(8,128)(2,1)S(1)}, u32[]{:S(2)}, u32[]{:S(2)}) %collective-permute-start.31) | collective-permute-done | bytes 2359328 | tf_op jit(solution)/shard_map/ppermute | solution.py:804
  386.0 6.8 %all-to-all-start.3 = ((bf16[16,3,256,128]{3,2,1,0:T(8,128)(2,1)}), bf16[16,3,256,128]{3,2,1,0:T(8,128)(2,1)}, u32[]{:S(2)}, u32[]{:S(2)}) async-start(bf16[16,3,256,128]{3,2,1,0:T(8,128)(2,1)} %bitcast.128), calls=%async_computation.3 | async-start | bytes 6291456 | tf_op jit(solution)/shard_map/all_to_all | solution.py:1002
  402.8 43.1 %collective-permute-done.34 = f32[1,8192]{1,0:T(1,128)S(1)} collective-permute-done((f32[1,8192]{1,0:T(1,128)S(1)}, f32[1,8192]{1,0:T(1,128)S(1)}, u32[]{:S(2)}, u32[]{:S(2)}) %collective-permute-start.34) | collective-permute-done | bytes 32800 | tf_op jit(solution)/shard_map/ppermute | solution.py:804
  445.9 11.3 %collective-permute-start.35 = (f32[1,8192]{1,0:T(1,128)S(1)}, f32[1,8192]{1,0:T(1,128)S(1)}, u32[]{:S(2)}, u32[]{:S(2)}) collective-permute-start(f32[1,8192]{1,0:T(1,128)S(1)} %add.166), channel_id=1, source_target_pairs={{0,2},{1,3},{2,0},{3,1},{4,6},{5,7},{6,4},{7,5},{8,10},{9,11},{10,... | collective-permute-start | bytes 98312 | tf_op jit(solution)/shard_map/ppermute | solution.py:804
  476.1 5.1 collective-permute-start.46
  481.2 11.0 %collective-permute-done.49 = bf16[2,288,512]{2,1,0:T(8,128)(2,1)} collective-permute-done((bf16[2,288,512]{2,1,0:T(8,128)(2,1)}, bf16[2,288,512]{2,1,0:T(8,128)(2,1)}, u32[]{:S(2)}, u32[]{:S(2)}) %collective-permute-start.49) | collective-permute-done | bytes 589856 | tf_op jit(solution)/shard_map/ppermute | solution.py:819
  495.8 7.7 %qkv_grad.1 = (bf16[8,3,32,512]{3,2,1,0:T(8,128)(2,1)}, bf16[8,3,32,512]{3,2,1,0:T(8,128)(2,1)}, bf16[8,3,32,512]{3,2,1,0:T(8,128)(2,1)}, bf16[8,3,32,512]{3,2,1,0:T(8,128)(2,1)}) custom-call(s32[34]{0:T(128)} %pad_add_fusion.place_ref, bf16[512,1024]{1,0:T(8,128)(2,1)} %get-tuple-element.113.refs_0_, bf16[512,1024]{1,0:T(8,128)(2,1)} %collective-permute-done.40.refs_1_, ...), custom_call_target="tpu_custom_call" | custom-call | flops 3221225472 | bytes 15000000 | tf_op jit(solution)/shard_map/qkv_grad/pallas_call | solution.py:734
  505.8 5.5 collective-permute-done.50
  517.8 12.7 %input_grad.1 = (f32[512,1024]{1,0:T(8,128)}, f32[1,1024]{1,0:T(1,128)}, f32[1,1024]{1,0:T(1,128)}) custom-call(s32[34]{0:T(128)} %pad_add_fusion.place_ref, bf16[512,1024]{1,0:T(8,128)(2,1)} %bitcast.136, f32[1,1024]{1,0:T(1,128)} %bitcast.156, f32[512,1024]{1,0:T(8,128)} %get-tuple-element.85.dmid_ref, ...), custom_call_target="tpu_custom_call" | custom-call | flops 3221225472 | bytes 20000000 | tf_op jit(solution)/shard_map/input_grad/pallas_call | solution.py:787
  531.5 4.6 collective-permute-start.48
  555.1 9.5 %collective-permute-done.45 = bf16[4,1,3,32,512]{4,2,3,1,0:T(4,128)(2,1)S(1)} collective-permute-done((bf16[4,1,3,32,512]{4,2,3,1,0:T(4,128)(2,1)S(1)}, bf16[4,1,3,32,512]{4,2,3,1,0:T(4,128)(2,1)S(1)}, u32[]{:S(2)}, u32[]{:S(2)}) %collective-permute-start.45) | collective-permute-done | bytes 393248 | tf_op jit(solution)/shard_map/ppermute | solution.py:804
  573.7 5.0 collective-permute-done.52
  578.7 12.1 %collective-permute-done.53 = bf16[2,3,32,512]{3,1,2,0:T(4,128)(2,1)S(1)} collective-permute-done((bf16[2,3,32,512]{3,1,2,0:T(4,128)(2,1)S(1)}, bf16[2,3,32,512]{3,1,2,0:T(4,128)(2,1)S(1)}, u32[]{:S(2)}, u32[]{:S(2)}) %collective-permute-start.53) | collective-permute-done | bytes 196640 | tf_op jit(solution)/shard_map/ppermute | solution.py:804
  (239 shorter events, 135.1 us)
Async XLA Ops:
  30.7 29.4 %collective-permute-start.4 = (bf16[8,3,32,512]{3,2,1,0:T(8,128)(2,1)S(1)}, bf16[8,3,32,512]{3,2,1,0:T(8,128)(2,1)S(1)}, u32[]{:S(2)}, u32[]{:S(2)}) collective-permute-start(bf16[8,3,32,512]{3,2,1,0:T(8,128)(2,1)S(1)} %constant_dynamic-update-slice_fusion.refs_0_.refs_2_), channel_id=1, source_target_pairs={{0,2},{1,3},{2,0},{3,1},{4,6},{5,7},{6,4},{7,5},{8,10},{9,11},{10,... | collective-permute-start | bytes 2359304 | tf_op jit(solution)/shard_map/ppermute | solution.py:804
  32.3 27.9 %collective-permute-start.7 = (bf16[8,3,32,512]{3,2,1,0:T(8,128)(2,1)S(1)}, bf16[8,3,32,512]{3,2,1,0:T(8,128)(2,1)S(1)}, u32[]{:S(2)}, u32[]{:S(2)}) collective-permute-start(bf16[8,3,32,512]{3,2,1,0:T(8,128)(2,1)S(1)} %constant_dynamic-update-slice_fusion.refs_0_.refs_2_), channel_id=1, source_target_pairs={{0,16},{16,0},{1,17},{17,1},{2,18},{18,2},{3,19},{19,3},{4,20},{20... | collective-permute-start | bytes 2359304 | tf_op jit(solution)/shard_map/ppermute | solution.py:804
  34.0 26.7 %collective-permute-start.6 = (bf16[8,3,32,512]{3,2,1,0:T(8,128)(2,1)S(1)}, bf16[8,3,32,512]{3,2,1,0:T(8,128)(2,1)}, u32[]{:S(2)}, u32[]{:S(2)}) collective-permute-start(bf16[8,3,32,512]{3,2,1,0:T(8,128)(2,1)S(1)} %pad_maximum_fusion.6.refs_2_.refs_4_), channel_id=1, source_target_pairs={{0,1},{1,0},{2,3},{3,2},{4,5},{5,4},{6,7},{7,6},{8,9},{9,8},{10,11... | collective-permute-start | bytes 2359304 | tf_op jit(solution)/shard_map/ppermute | solution.py:804
  34.0 19.4 %collective-permute-start.11 = (bf16[2,288,512]{2,1,0:T(8,128)(2,1)S(1)}, bf16[2,288,512]{2,1,0:T(8,128)(2,1)S(1)}, u32[]{:S(2)}, u32[]{:S(2)}) collective-permute-start(bf16[2,288,512]{2,1,0:T(8,128)(2,1)S(1)} %pad_maximum_fusion.7), channel_id=1, source_target_pairs={{0,4},{1,5},{2,6},{3,7},{4,8},{5,9},{6,10},{7,11},{8,12},{9,13},{1... | collective-permute-start | bytes 1769480 | tf_op jit(solution)/shard_map/ppermute | solution.py:818
  40.5 18.2 %collective-permute-start.14 = (bf16[2,288,512]{2,1,0:T(8,128)(2,1)S(1)}, bf16[2,288,512]{2,1,0:T(8,128)(2,1)S(1)}, u32[]{:S(2)}, u32[]{:S(2)}) collective-permute-start(bf16[2,288,512]{2,1,0:T(8,128)(2,1)S(1)} %pad_maximum_fusion.7), channel_id=1, source_target_pairs={{4,0},{5,1},{6,2},{7,3},{8,4},{9,5},{10,6},{11,7},{12,8},{13,9},{1... | collective-permute-start | bytes 1769480 | tf_op jit(solution)/shard_map/ppermute | solution.py:819
  91.2 69.2 %all-to-all-start = ((bf16[16,3,256,128]{3,2,1,0:T(8,128)(2,1)}), bf16[16,3,256,128]{3,2,1,0:T(8,128)(2,1)}, u32[]{:S(2)}, u32[]{:S(2)}) async-start(bf16[16,3,256,128]{3,2,1,0:T(8,128)(2,1)} %bitcast.127), calls=%async_computation | async-start | bytes 6291456 | tf_op jit(solution)/shard_map/all_to_all | solution.py:1002
  98.8 55.7 %collective-permute-start.18 = (bf16[4,288,512]{2,1,0:T(8,128)(2,1)S(1)}, bf16[4,288,512]{2,1,0:T(8,128)(2,1)}, u32[]{:S(2)}, u32[]{:S(2)}) collective-permute-start(bf16[4,288,512]{2,1,0:T(8,128)(2,1)S(1)} %get-tuple-element.159), channel_id=1, source_target_pairs={{0,2},{1,3},{2,0},{3,1},{4,6},{5,7},{6,4},{7,5},{8,10},{9,11},{10,... | collective-permute-start | bytes 3538952 | tf_op jit(solution)/shard_map/ppermute | solution.py:804
  100.6 56.9 %collective-permute-start.17 = (bf16[4,288,512]{2,1,0:T(8,128)(2,1)S(1)}, bf16[4,288,512]{2,1,0:T(8,128)(2,1)}, u32[]{:S(2)}, u32[]{:S(2)}) collective-permute-start(bf16[4,288,512]{2,1,0:T(8,128)(2,1)S(1)} %get-tuple-element.160), channel_id=1, source_target_pairs={{0,1},{1,0},{2,3},{3,2},{4,5},{5,4},{6,7},{7,6},{8,9},{9,8},{10,11... | collective-permute-start | bytes 3538952 | tf_op jit(solution)/shard_map/ppermute | solution.py:804
  160.4 49.0 %collective-permute-start.19 = (bf16[8,288,512]{2,1,0:T(8,128)(2,1)}, bf16[8,288,512]{2,1,0:T(8,128)(2,1)S(1)}, u32[]{:S(2)}, u32[]{:S(2)}) collective-permute-start(bf16[8,288,512]{2,1,0:T(8,128)(2,1)} %pad_maximum_fusion.1.refs_0_), channel_id=1, source_target_pairs={{0,2},{1,3},{2,0},{3,1},{4,6},{5,7},{6,4},{7,5},{8,10},{9,11},{10,... | collective-permute-start | bytes 7077896 | tf_op jit(solution)/shard_map/ppermute | solution.py:804
  160.4 64.8 %collective-permute-start.21 = (bf16[8,288,512]{2,1,0:T(8,128)(2,1)}, bf16[8,288,512]{2,1,0:T(8,128)(2,1)}, u32[]{:S(2)}, u32[]{:S(2)}) collective-permute-start(bf16[8,288,512]{2,1,0:T(8,128)(2,1)} %pad_maximum_fusion.1.refs_0_), channel_id=1, source_target_pairs={{0,16},{16,0},{1,17},{17,1},{2,18},{18,2},{3,19},{19,3},{4,20},{20... | collective-permute-start | bytes 7077896 | tf_op jit(solution)/shard_map/ppermute | solution.py:804
  160.4 54.0 %collective-permute-start.20 = (bf16[8,288,512]{2,1,0:T(8,128)(2,1)}, bf16[8,288,512]{2,1,0:T(8,128)(2,1)}, u32[]{:S(2)}, u32[]{:S(2)}) collective-permute-start(bf16[8,288,512]{2,1,0:T(8,128)(2,1)} %pad_maximum_fusion.2.refs_2_), channel_id=1, source_target_pairs={{0,1},{1,0},{2,3},{3,2},{4,5},{5,4},{6,7},{7,6},{8,9},{9,8},{10,11... | collective-permute-start | bytes 7077896 | tf_op jit(solution)/shard_map/ppermute | solution.py:804
  162.2 63.0 %collective-permute-start.23 = (bf16[8,288,512]{2,1,0:T(8,128)(2,1)}, bf16[8,288,512]{2,1,0:T(8,128)(2,1)}, u32[]{:S(2)}, u32[]{:S(2)}) collective-permute-start(bf16[8,288,512]{2,1,0:T(8,128)(2,1)} %pad_maximum_fusion.2.refs_2_), channel_id=1, source_target_pairs={{0,16},{16,0},{1,17},{17,1},{2,18},{18,2},{3,19},{19,3},{4,20},{20... | collective-permute-start | bytes 7077896 | tf_op jit(solution)/shard_map/ppermute | solution.py:804
  214.4 35.4 %collective-permute-start.22 = (bf16[8,288,512]{2,1,0:T(8,128)(2,1)S(1)}, bf16[8,288,512]{2,1,0:T(8,128)(2,1)}, u32[]{:S(2)}, u32[]{:S(2)}) collective-permute-start(bf16[8,288,512]{2,1,0:T(8,128)(2,1)S(1)} %collective-permute-done.19.refs_1_), channel_id=1, source_target_pairs={{0,16},{16,0},{1,17},{17,1},{2,18},{18,2},{3,19},{19,3},{4,20},{20... | collective-permute-start | bytes 7077896 | tf_op jit(solution)/shard_map/ppermute | solution.py:804
  214.4 35.4 %collective-permute-start.24 = (bf16[8,288,512]{2,1,0:T(8,128)(2,1)}, bf16[8,288,512]{2,1,0:T(8,128)(2,1)}, u32[]{:S(2)}, u32[]{:S(2)}) collective-permute-start(bf16[8,288,512]{2,1,0:T(8,128)(2,1)} %collective-permute-done.20.refs_3_), channel_id=1, source_target_pairs={{0,16},{16,0},{1,17},{17,1},{2,18},{18,2},{3,19},{19,3},{4,20},{20... | collective-permute-start | bytes 7077896 | tf_op jit(solution)/shard_map/ppermute | solution.py:804
  214.9 34.8 %all-to-all-start.1 = ((bf16[16,256,128]{2,1,0:T(8,128)(2,1)}), bf16[16,256,128]{2,1,0:T(8,128)(2,1)S(1)}, u32[]{:S(2)}, u32[]{:S(2)}) async-start(bf16[16,256,128]{2,1,0:T(8,128)(2,1)} %bitcast.139), calls=%async_computation.1 | async-start | bytes 2097152 | tf_op jit(solution)/shard_map/all_to_all | solution.py:1002
  291.7 37.5 %all-to-all-start.2 = ((bf16[16,256,128]{2,1,0:T(8,128)(2,1)}), bf16[16,256,128]{2,1,0:T(8,128)(2,1)S(1)}, u32[]{:S(2)}, u32[]{:S(2)}) async-start(bf16[16,256,128]{2,1,0:T(8,128)(2,1)} %bitcast.41), calls=%async_computation.2 | async-start | bytes 2097152 | tf_op jit(solution)/shard_map/all_to_all | solution.py:1002
  329.3 53.8 %collective-permute-start.31 = (bf16[8,288,512]{2,1,0:T(8,128)(2,1)}, bf16[8,288,512]{2,1,0:T(8,128)(2,1)S(1)}, u32[]{:S(2)}, u32[]{:S(2)}) collective-permute-start(bf16[8,288,512]{2,1,0:T(8,128)(2,1)} %get-tuple-element.98), channel_id=1, source_target_pairs={{0,2},{1,3},{2,0},{3,1},{4,6},{5,7},{6,4},{7,5},{8,10},{9,11},{10,... | collective-permute-start | bytes 7077896 | tf_op jit(solution)/shard_map/ppermute | solution.py:804
  331.4 53.2 %collective-permute-start.32 = (bf16[8,288,512]{2,1,0:T(8,128)(2,1)}, bf16[8,288,512]{2,1,0:T(8,128)(2,1)S(1)}, u32[]{:S(2)}, u32[]{:S(2)}) collective-permute-start(bf16[8,288,512]{2,1,0:T(8,128)(2,1)} %get-tuple-element.99), channel_id=1, source_target_pairs={{0,1},{1,0},{2,3},{3,2},{4,5},{5,4},{6,7},{7,6},{8,9},{9,8},{10,11... | collective-permute-start | bytes 7077896 | tf_op jit(solution)/shard_map/ppermute | solution.py:804
  386.0 83.0 %all-to-all-start.3 = ((bf16[16,3,256,128]{3,2,1,0:T(8,128)(2,1)}), bf16[16,3,256,128]{3,2,1,0:T(8,128)(2,1)}, u32[]{:S(2)}, u32[]{:S(2)}) async-start(bf16[16,3,256,128]{3,2,1,0:T(8,128)(2,1)} %bitcast.128), calls=%async_computation.3 | async-start | bytes 6291456 | tf_op jit(solution)/shard_map/all_to_all | solution.py:1002
  395.5 72.6 %collective-permute-start.38 = (bf16[4,1,288,512]{3,2,1,0:T(8,128)(2,1)S(1)}, bf16[4,1,288,512]{3,2,1,0:T(8,128)(2,1)S(1)}, u32[]{:S(2)}, u32[]{:S(2)}) collective-permute-start(bf16[4,1,288,512]{3,2,1,0:T(8,128)(2,1)S(1)} %slice.139), channel_id=1, source_target_pairs={{0,1},{1,0},{2,3},{3,2},{4,5},{5,4},{6,7},{7,6},{8,9},{9,8},{10,11... | collective-permute-start | bytes 3538952 | tf_op jit(solution)/shard_map/ppermute | solution.py:804
  398.3 70.1 %collective-permute-start.39 = (bf16[4,1,288,512]{3,2,1,0:T(8,128)(2,1)S(1)}, bf16[4,1,288,512]{3,2,1,0:T(8,128)(2,1)S(1)}, u32[]{:S(2)}, u32[]{:S(2)}) collective-permute-start(bf16[4,1,288,512]{3,2,1,0:T(8,128)(2,1)S(1)} %slice.141), channel_id=1, source_target_pairs={{0,2},{1,3},{2,0},{3,1},{4,6},{5,7},{6,4},{7,5},{8,10},{9,11},{10,... | collective-permute-start | bytes 3538952 | tf_op jit(solution)/shard_map/ppermute | solution.py:804
  401.3 44.6 %collective-permute-start.34 = (f32[1,8192]{1,0:T(1,128)S(1)}, f32[1,8192]{1,0:T(1,128)S(1)}, u32[]{:S(2)}, u32[]{:S(2)}) collective-permute-start(f32[1,8192]{1,0:T(1,128)S(1)} %add.165), channel_id=1, source_target_pairs={{0,1},{1,0},{2,3},{3,2},{4,5},{5,4},{6,7},{7,6},{8,9},{9,8},{10,11... | collective-permute-start | bytes 98312 | tf_op jit(solution)/shard_map/ppermute | solution.py:804
  473.3 22.5 %collective-permute-start.41 = (bf16[512,1536]{1,0:T(8,128)(2,1)}, bf16[512,1536]{1,0:T(8,128)(2,1)}, u32[]{:S(2)}, u32[]{:S(2)}) collective-permute-start(bf16[512,1536]{1,0:T(8,128)(2,1)} %get-tuple-element.112.refs_1_), channel_id=1, source_target_pairs={{0,16},{16,0},{1,17},{17,1},{2,18},{18,2},{3,19},{19,3},{4,20},{20... | collective-permute-start | bytes 4718600 | tf_op jit(solution)/shard_map/ppermute | solution.py:804
  475.5 20.3 %collective-permute-start.40 = (bf16[512,1024]{1,0:T(8,128)(2,1)}, bf16[512,1024]{1,0:T(8,128)(2,1)}, u32[]{:S(2)}, u32[]{:S(2)}) collective-permute-start(bf16[512,1024]{1,0:T(8,128)(2,1)} %get-tuple-element.113.refs_0_), channel_id=1, source_target_pairs={{0,16},{16,0},{1,17},{17,1},{2,18},{18,2},{3,19},{19,3},{4,20},{20... | collective-permute-start | bytes 3145736 | tf_op jit(solution)/shard_map/ppermute | solution.py:804
  476.1 29.7 %collective-permute-start.46 = (bf16[2,288,512]{2,1,0:T(8,128)(2,1)S(1)}, bf16[2,288,512]{2,1,0:T(8,128)(2,1)}, u32[]{:S(2)}, u32[]{:S(2)}) collective-permute-start(bf16[2,288,512]{2,1,0:T(8,128)(2,1)S(1)} %get-tuple-element.158), channel_id=1, source_target_pairs={{0,4},{1,5},{2,6},{3,7},{4,8},{5,9},{6,10},{7,11},{8,12},{9,13},{1... | collective-permute-start | bytes 1769480 | tf_op jit(solution)/shard_map/ppermute | solution.py:818
  503.5 27.7 %collective-permute-start.42 = (bf16[8,3,32,512]{3,2,1,0:T(8,128)(2,1)}, bf16[8,3,32,512]{3,2,1,0:T(8,128)(2,1)S(1)}, u32[]{:S(2)}, u32[]{:S(2)}) collective-permute-start(bf16[8,3,32,512]{3,2,1,0:T(8,128)(2,1)} %get-tuple-element.118), channel_id=1, source_target_pairs={{0,2},{1,3},{2,0},{3,1},{4,6},{5,7},{6,4},{7,5},{8,10},{9,11},{10,... | collective-permute-start | bytes 2359304 | tf_op jit(solution)/shard_map/ppermute | solution.py:804
  505.8 25.4 %collective-permute-start.43 = (bf16[8,3,32,512]{3,2,1,0:T(8,128)(2,1)}, bf16[8,3,32,512]{3,2,1,0:T(8,128)(2,1)S(1)}, u32[]{:S(2)}, u32[]{:S(2)}) collective-permute-start(bf16[8,3,32,512]{3,2,1,0:T(8,128)(2,1)} %get-tuple-element.119), channel_id=1, source_target_pairs={{0,1},{1,0},{2,3},{3,2},{4,5},{5,4},{6,7},{7,6},{8,9},{9,8},{10,11... | collective-permute-start | bytes 2359304 | tf_op jit(solution)/shard_map/ppermute | solution.py:804
  512.9 18.4 %collective-permute-start.47 = (bf16[2,288,512]{2,1,0:T(8,128)(2,1)S(1)}, bf16[2,288,512]{2,1,0:T(8,128)(2,1)S(1)}, u32[]{:S(2)}, u32[]{:S(2)}) collective-permute-start(bf16[2,288,512]{2,1,0:T(8,128)(2,1)S(1)} %get-tuple-element.156), channel_id=1, source_target_pairs={{0,4},{1,5},{2,6},{3,7},{4,8},{5,9},{6,10},{7,11},{8,12},{9,13},{1... | collective-permute-start | bytes 1769480 | tf_op jit(solution)/shard_map/ppermute | solution.py:818
  516.5 49.4 %collective-permute-start.51 = (bf16[2,288,512]{2,1,0:T(8,128)(2,1)S(1)}, bf16[2,288,512]{2,1,0:T(8,128)(2,1)S(1)}, u32[]{:S(2)}, u32[]{:S(2)}) collective-permute-start(bf16[2,288,512]{2,1,0:T(8,128)(2,1)S(1)} %get-tuple-element.155), channel_id=1, source_target_pairs={{4,0},{5,1},{6,2},{7,3},{8,4},{9,5},{10,6},{11,7},{12,8},{13,9},{1... | collective-permute-start | bytes 1769480 | tf_op jit(solution)/shard_map/ppermute | solution.py:819
  531.5 34.4 %collective-permute-start.48 = (bf16[2,288,512]{2,1,0:T(8,128)(2,1)S(1)}, bf16[2,288,512]{2,1,0:T(8,128)(2,1)S(1)}, u32[]{:S(2)}, u32[]{:S(2)}) collective-permute-start(bf16[2,288,512]{2,1,0:T(8,128)(2,1)S(1)} %fusion.4), channel_id=1, source_target_pairs={{0,4},{1,5},{2,6},{3,7},{4,8},{5,9},{6,10},{7,11},{8,12},{9,13},{1... | collective-permute-start | bytes 1769480 | tf_op jit(solution)/shard_map/ppermute | solution.py:818
  569.8 21.0 %collective-permute-start.53 = (bf16[2,3,32,512]{3,1,2,0:T(4,128)(2,1)S(1)}, bf16[2,3,32,512]{3,1,2,0:T(4,128)(2,1)S(1)}, u32[]{:S(2)}, u32[]{:S(2)}) collective-permute-start(bf16[2,3,32,512]{3,1,2,0:T(4,128)(2,1)S(1)} %get-tuple-element.169), channel_id=1, source_target_pairs={{0,8},{1,9},{2,10},{3,11},{4,12},{5,13},{6,14},{7,15},{8,0},{9,1},... | collective-permute-start | bytes 589832 | tf_op jit(solution)/shard_map/ppermute | solution.py:804
  571.2 19.5 %collective-permute-start.54 = (bf16[2,3,32,512]{3,1,2,0:T(4,128)(2,1)S(1)}, bf16[2,3,32,512]{3,1,2,0:T(4,128)(2,1)S(1)}, u32[]{:S(2)}, u32[]{:S(2)}) collective-permute-start(bf16[2,3,32,512]{3,1,2,0:T(4,128)(2,1)S(1)} %get-tuple-element.168), channel_id=1, source_target_pairs={{0,12},{1,13},{2,14},{3,15},{4,8},{5,9},{6,10},{7,11},{8,4},{9,5},... | collective-permute-start | bytes 589832 | tf_op jit(solution)/shard_map/ppermute | solution.py:804
  (63 other events, 727.5 us)

commit v3 on v2

--- a/solution.py
+++ b/solution.py
@@ -59,10 +59,14 @@
 
 
 def load_pieces(refs, wa_ref, wb_ref, sems):
-    half = wa_ref.shape[1] // 2
+    parts = len(refs) // wa_ref.shape[0]
     copies = []
+    at = 0
     for i, ref in enumerate(refs):
-        target = (wa_ref, wb_ref)[i % 4 // 2].at[i // 4, pl.ds(i % 2 * half, half)]
+        if i % (parts // 2) == 0:
+            at = 0
+        target = (wa_ref, wb_ref)[i % parts // (parts // 2)].at[i // parts, pl.ds(at, ref.shape[0])]
+        at += ref.shape[0]
         copies.append(pltpu.make_async_copy(ref, target, sems.at[i]))
     for copy in copies:
         copy.start()
@@ -79,9 +83,8 @@
     return jnp.concatenate(rows, axis=0)
 
 
-def piece_scratch(pieces, nb):
-    half = pieces[0].shape
-    full = (nb, 2 * half[0]) + half[1:]
+def piece_scratch(pieces, nb, n):
+    full = (nb, n) + pieces[0].shape[1:]
     return [pltpu.VMEM(full, BF), pltpu.VMEM(full, BF), pltpu.SemaphoreType.DMA((len(pieces),))]
 
 
@@ -102,8 +105,7 @@
             qkv_ref[m, i, 0] = y[m * local : (m + 1) * local, i * lanes : (i + 1) * lanes]
 
 
-def project(place, x, gain, shift, pieces, micros, local, lanes):
-    nb = len(pieces) // 4
+def project(place, x, gain, shift, pieces, nb, n, micros, local, lanes):
     fb = pieces[0].shape[-1]
     rows, width = x.shape
     groups = width // lanes
@@ -121,7 +123,7 @@
             jax.ShapeDtypeStruct((micros, groups, 3, local, lanes), BF),
             jax.ShapeDtypeStruct((rows, width), BF),
         ],
-        scratch_shapes=piece_scratch(pieces, nb),
+        scratch_shapes=piece_scratch(pieces, nb, n),
         compiler_params=params(),
         cost_estimate=cost(6 * rows * width * width, 14 * width * width),
         name="project",
@@ -369,6 +371,10 @@
 MIDDLE_REFS = 16
 
 
+def rest_places(n):
+    return [s % (n // 4) * 4 + s // (n // 4) for s in range(n)]
+
+
 def middle_kernel(
     place_ref,
     o_ref,
@@ -383,7 +389,7 @@
     local,
     lanes,
 ):
-    *pieces, wa_ref, wb_ref, sems = refs
+    *pieces, w_ref, sems = refs
     count = len(pieces) - MIDDLE_REFS
     pieces, others = pieces[:count], pieces[count:]
     (
@@ -406,37 +412,48 @@
     ) = others
     step = pl.program_id(0)
     micros, groups = o_ref.shape[:2]
-    nb, n, _, fb = wa_ref.shape
+    nb, n, height, fb = w_ref.shape
     width = x_ref.shape[1]
     kr = width // n
-    kh = kr // 2
-    fr = wa_ref.shape[2] - kh
+    per_b = pl.num_programs(0) // nb
+    fr = per_b * kr
     nd = fb // fr
     me_core = place_ref[2 * n]
-    per_b = pl.num_programs(0) // nb
+    at = rest_places(n)
 
     def out_block(b):
+        rows = [w_ref[b ^ me_core, at[s], 2 * fr :] for s in range(n)]
+        return jnp.concatenate(rows, axis=0)
+
+    def down_block(b):
         rows = []
-        for s in range(n):
-            rows.append(wa_ref[b ^ me_core, place_ref[s], fr : fr + kh])
-            rows.append(wb_ref[b ^ me_core, place_ref[n + s], fr : fr + kh])
-        return jnp.concatenate(rows, axis=0)
-
-    def down_block(b):
-        rows = [wa_ref[b ^ me_core, place_ref[step * nd + h], :fr] for h in range(nd)]
+        for h in range(nd):
+            s = step * nd + h
+            rows.append(w_ref[b ^ me_core, s % (n // 4) * 4 + s // (n // 4), :fr])
         return jnp.concatenate(rows, axis=0)
 
     def up_block():
         core = (step // per_b) ^ me_core
-        at = pl.ds(pl.multiple_of(step % per_b * kr, kr), kr)
-        return jnp.concatenate([wb_ref[core, place_ref[n + s], at] for s in range(n)], axis=0)
+        rows = pl.ds(pl.multiple_of(fr + step % per_b * kr, kr), kr)
+        return jnp.concatenate([w_ref[core, at[s], rows] for s in range(n)], axis=0)
+
+    def copies(part, rows):
+        found = []
+        for k, piece in enumerate(pieces):
+            copy = pltpu.make_async_copy(piece.at[:, rows], w_ref.at[k, :, rows], sems.at[part, k])
+            copy.start()
+            found.append(copy)
+        return found
 
     @pl.when(step == 0)
     def _():
-        load_pieces(pieces, wa_ref, wb_ref, sems)
+        first = copies(0, pl.ds(2 * fr, kr))
+        rest = copies(1, pl.ds(0, 2 * fr))
         for m in range(micros):
             for i in range(groups):
                 att_ref[m * local : (m + 1) * local, i * lanes : (i + 1) * lanes] = o_ref[m, i]
+        for copy in first:
+            copy.wait()
         att = att_ref[...]
         for b in range(nb):
             cols = slice(b * fb, (b + 1) * fb)
@@ -448,6 +465,8 @@
         acc_ref[...] = mid + down_bias_ref[...]
         dh_ref[...] = jnp.zeros_like(dh_ref)
         d_down_bias_ref[...] = jnp.sum(g_ref[...].astype(F32), axis=0, keepdims=True)
+        for copy in rest:
+            copy.wait()
 
     up = up_block()
     pre = nn(h_ref[...], up) + up_bias_ref[...]
@@ -494,14 +513,12 @@
                 dout_ref[m, i] = dout[m * local : (m + 1) * local, i * lanes : (i + 1) * lanes]
 
 
-def middle(place, o, x, g, pieces, out_bias, up_bias, down_bias, gain, shift):
+def middle(nb, n, place, o, x, g, pieces, out_bias, up_bias, down_bias, gain, shift):
     micros, groups, local, lanes = o.shape
     rows, width = x.shape
-    nb = len(pieces) // 4
     fb = pieces[0].shape[-1]
     hidden = up_bias.shape[1]
     steps = hidden // fb
-    n = 2 * pieces[0].shape[0]
     per_b = steps // nb
     full = lambda dtype: jax.ShapeDtypeStruct((rows, width), dtype)
     vector = jax.ShapeDtypeStruct((1, width), F32)
@@ -538,7 +555,7 @@
             whole((1, width)),
             whole((1, width)),
         ],
-    scratch_shapes=[pltpu.VMEM((rows, width), F32)] * 3 + piece_scratch(pieces, nb),
+    scratch_shapes=[pltpu.VMEM((rows, width), F32)] * 3 + [pltpu.VMEM((nb,) + pieces[0].shape, BF), pltpu.SemaphoreType.DMA((2, nb))],
         ),
         out_shape=[
             full(BF),
@@ -569,109 +586,60 @@
         target_ref[k, at, :] = value[s * kr : (s + 1) * kr]
 
 
-def ffn_grads_kernel(place_ref, *refs, nb, n):
+def ffn_grads_kernel(*refs, nb):
     groups = [refs[i * nb : (i + 1) * nb] for i in range(6)]
     act_refs, gc_refs, h_refs, gp_refs, att_refs, br_refs = groups
-    a_send_ref, a_keep_ref, b_send_ref, b_keep_ref, ht_ref, at_ref, out_ref = refs[6 * nb :]
+    out_ref, ht_ref, at_ref = refs[6 * nb :]
     step = pl.program_id(0)
-    me = place_ref[2 * n + 1]
-    first = n // 8
-    rows_a, fb = a_send_ref.shape[1:]
-    kr = ht_ref.shape[1] // n
-    kh = kr // 2
-    fr = rows_a - kh
-    per_b = fr // kr
+    count, _, height, fb = out_ref.shape
+    fr = act_refs[0].shape[1] // count
+    per_b = gp_refs[0].shape[2] // fb
+    kr = (height - fr) // (per_b + 1)
 
     @pl.when(step == 0)
     def _():
-        total = None
         for k in range(nb):
-            relative_transpose(h_refs[k], ht_ref, k, me, n)
-            relative_transpose(att_refs[k], at_ref, k, me, n)
-        for k in range(nb):
-            term = nn(at_ref[k], br_refs[k][...])
-            total = term if total is None else total + term
-        out_ref[...] = total.astype(BF).reshape(out_ref.shape)
-
-    send = step < 4
-    z = step % 4
-    down = None
+            ht_ref[k] = h_refs[k][...].T
+            at_ref[k] = att_refs[k][...].T
+
+    at = pl.ds(pl.multiple_of(step * count * kr, count * kr), count * kr)
+    down, up, out = 0.0, 0.0, 0.0
     for k in range(nb):
-        term = nn(act_refs[k][...].T, gc_refs[k][...])
-        down = term if down is None else down + term
-    down = down.astype(BF).reshape(first, fr, fb)
-    base_a = (2 * z + send.astype(jnp.int32)) * first
-
-    def put_a(ref):
-        for i in range(first):
-            place = i ^ (me % first)
-            ref[place, :fr] = down[i]
-        for i in range(first):
-            ref[i, fr:] = out_ref[base_a + i, :kh]
-
-    pl.when(send)(lambda: put_a(a_send_ref))
-    pl.when(jnp.logical_not(send))(lambda: put_a(a_keep_ref))
-
-    def put_b(ref, offset):
-        firsts = [pl.multiple_of(((2 * (step % 4 // 2) + i // first) * 2 * first + 2 * (i % first) + offset) * kr, kr) for i in range(2 * first)]
-        up = None
-        for k in range(nb):
-            rows = jnp.concatenate([ht_ref[k, pl.ds(at, kr), :] for at in firsts], axis=0)
-            term = nn(rows, gp_refs[k][0])
-            up = term if up is None else up + term
-        up = up.astype(BF).reshape(2 * first, kr, per_b * fb)
-        for i in range(2 * first):
-            for q in range(per_b):
-                ref[i, q * kr : (q + 1) * kr] = up[i, :, q * fb : (q + 1) * fb]
-            ref[i, fr:] = out_ref[firsts[i] // kr, kh:]
-
-    even = step % 2 == 0
-    pl.when(even & send)(lambda: put_b(b_send_ref, 1))
-    pl.when(even & jnp.logical_not(send))(lambda: put_b(b_keep_ref, 0))
-
-
-def ffn_grads(place, act, gc, h, gp, att, br, n):
+        down += nn(act_refs[k][...].T, gc_refs[k][...])
+        up += nn(ht_ref[k, at, :], gp_refs[k][0])
+        out += nn(at_ref[k, at, :], br_refs[k][...])
+    down, up, out = down.astype(BF), up.astype(BF), out.astype(BF)
+    for i in range(count):
+        out_ref[i, 0, :fr] = down[i * fr : (i + 1) * fr]
+        for q in range(per_b):
+            out_ref[i, 0, fr + q * kr : fr + (q + 1) * kr] = up[i * kr : (i + 1) * kr, q * fb : (q + 1) * fb]
+        out_ref[i, 0, fr + per_b * kr :] = out[i * kr : (i + 1) * kr]
+
+
+def ffn_grads(act, gc, h, gp, att, br, n):
     nb = len(act)
     rows, hidden = act[0].shape
     fb = gc[0].shape[1]
     width = h[0].shape[1]
-    first = n // 8
-    fr = hidden // n
-    kr = width // n
-    rows_a = fr + kr // 2
-    half = jax.ShapeDtypeStruct((n // 2, rows_a, fb), BF)
-    whole = lambda shape: pl.BlockSpec(shape, lambda i, place: (0,) * len(shape))
-    act_spec = pl.BlockSpec(
-        (rows, first * fr), lambda i, place: (0, (2 * (i % 4) + 1 - i // 4) ^ (place[2 * n + 1] // first))
-    )
+    fr, kr = hidden // n, width // n
+    per_b = hidden // nb // fb
+    height = fr + (per_b + 1) * kr
     return pl.pallas_call(
-        functools.partial(ffn_grads_kernel, nb=nb, n=n),
-        grid_spec=pltpu.PrefetchScalarGridSpec(
-            num_scalar_prefetch=1,
-            grid=(8,),
-            in_specs=[act_spec] * nb
-            + [whole((rows, fb))] * nb
-            + [whole((rows, width))] * nb
-            + [whole((1, rows, hidden // nb))] * nb
-            + [whole((rows, width))] * nb
-            + [whole((rows, fb))] * nb,
-            out_specs=[
-                pl.BlockSpec((first, rows_a, fb), lambda i, place: (jnp.minimum(i, 3), 0, 0)),
-                pl.BlockSpec((first, rows_a, fb), lambda i, place: (jnp.maximum(i - 4, 0), 0, 0)),
-                pl.BlockSpec((2 * first, rows_a, fb), lambda i, place: (jnp.minimum(i, 3) // 2, 0, 0)),
-                pl.BlockSpec((2 * first, rows_a, fb), lambda i, place: (jnp.maximum(i - 4, 0) // 2, 0, 0)),
-            ],
-            scratch_shapes=[
-                pltpu.VMEM((nb, width, rows), BF),
-                pltpu.VMEM((nb, width, rows), BF),
-                pltpu.VMEM((n, kr, fb), BF),
-            ],
-        ),
-        out_shape=[half] * 4,
+        functools.partial(ffn_grads_kernel, nb=nb),
+        grid=(4,),
+        in_specs=[pl.BlockSpec((rows, hidden // 4), lambda i: (0, i))] * nb
+        + [constant((rows, fb))] * nb
+        + [constant((rows, width))] * nb
+        + [constant((1, rows, hidden // nb))] * nb
+        + [constant((rows, width))] * nb
+        + [constant((rows, fb))] * nb,
+        out_specs=pl.BlockSpec((n // 4, 1, height, fb), lambda i: (0, i, 0, 0)),
+        out_shape=jax.ShapeDtypeStruct((n // 4, 4, height, fb), BF),
+        scratch_shapes=[pltpu.VMEM((nb, width, rows), BF)] * 2,
         compiler_params=params(),
         cost_estimate=cost(4 * rows * width * hidden + 2 * rows * width * width, 40e6),
         name="ffn_grads",
-    )(place, *act, *gc, *h, *gp, *att, *br)
+    )(*act, *gc, *h, *gp, *att, *br)
 
 
 def split_kernel(place_ref, grad_ref, *out_refs, n, local, lanes):
@@ -779,7 +747,7 @@
         out_ref[...] = dmid_ref[...] + rstd * inner
 
 
-def input_grad(place, grads, pieces, x, gain, dmid, earlier):
+def input_grad(place, grads, pieces, x, gain, dmid, earlier, n):
     rows, width = x.shape
     nb = len(grads)
     fb = pieces[0].shape[-1]
@@ -792,7 +760,7 @@
         + [pl.BlockSpec(memory_space=pl.ANY)] * (len(pieces) + 1),
         out_specs=[constant((rows, width)), constant((1, width)), constant((1, width))],
         out_shape=[jax.ShapeDtypeStruct((rows, width), F32), vector, vector],
-        scratch_shapes=[pltpu.VMEM((rows, width), F32)] + piece_scratch(pieces, nb),
+        scratch_shapes=[pltpu.VMEM((rows, width), F32)] + piece_scratch(pieces, nb, n),
         compiler_params=params(),
         cost_estimate=cost(6 * rows * width * width, 20e6),
         name="input_grad",
@@ -804,51 +772,36 @@
     return lax.ppermute(value, axis, [(i, i ^ k) for i in range(size)])
 
 
-def low_bits(n):
-    return [1 << i for i in range((n // 4).bit_length() - 1)]
+def powers(size):
+    return [1 << i for i in range(size.bit_length() - 1)]
 
 
 def direct(shard, n):
     return [swap_with(shard, "seq", k * n // 4) for k in range(1, 4)]
 
 
-def move(value, step, n):
+def planes(n):
     quarter = n // 4
-    if step > 0:
-        return lax.ppermute(value, "seq", [(i, i + quarter) for i in range(n - quarter)])
-    return lax.ppermute(value, "seq", [(i + quarter, i) for i in range(n - quarter)])
-
-
-def line_gather(shard, n):
-    up, down = [shard], [shard]
-    for _ in range(3):
-        up.append(move(up[-1], 1, n))
-        down.append(move(down[-1], -1, n))
-    return up[1:], down[1:]
-
-
-def line_halves(shard, up, down, position, n):
-    z = position // (n // 4)
-    by_distance = {**{-i - 1: up[i] for i in range(3)}, **{i + 1: down[i] for i in range(3)}}
-    arrived = []
-    for k in range(1, 4):
-        found = by_distance[k]
-        for at in range(1, 4):
-            found = jnp.where(z == at, by_distance[(at ^ k) - at], found)
-        arrived.append(found)
-    return halves(shard, arrived)
-
-
-def line_reduce(total, position, n):
-    z = position // (n // 4)
-    block = lambda to: lax.dynamic_index_in_dim(total, z ^ jnp.clip(to, 0, 3), 0, keepdims=False)
-    up, down = block(z + 3), block(z - 3)
-    for step in range(1, 4):
-        up, down = move(up, 1, n), move(down, -1, n)
-        if step < 3:
-            up = plus(block(z + 3 - step), up)
-            down = plus(block(z - 3 + step), down)
-    return up, down
+    return [[z * quarter + i for i in range(quarter)] for z in range(4)]
+
+
+def lines(n):
+    return [list(group) for group in zip(*planes(n))]
+
+
+def gather_line(shard, n):
+    return lax.all_gather(shard, "seq", axis_index_groups=lines(n))
+
+
+def gather_plane(line, n):
+    plane = lax.all_gather(line, "seq", axis_index_groups=planes(n))
+    return plane.reshape((n,) + line.shape[1:])
+
+
+def scatter_groups(grad, n):
+    scatter = functools.partial(lax.psum_scatter, axis_name="seq", scatter_dimension=0)
+    line = scatter(grad, axis_index_groups=planes(n))
+    return scatter(line, axis_index_groups=lines(n)).astype(F32)
 
 
 def halves(shard, arrived):
@@ -858,16 +811,6 @@
 
 def together(*values):
     return lax.optimization_barrier(values)
-
-
-def gather_rest(part, bits):
-    for bit in bits[:-1]:
-        part = jnp.concatenate([part, swap_with(part, "seq", bit)])
-    return part
-
-
-def gather_last(part, bits):
-    return [part, swap_with(part, "seq", bits[-1])]
 
 
 def gather_cores(pieces, nb):
@@ -886,7 +829,7 @@
 
 def place_table(position, core, n):
     relative = jnp.arange(n, dtype=jnp.int32) ^ position
-    bits = low_bits(n)
+    bits = powers(n // 4)
     ends = jnp.stack([core, position]).astype(jnp.int32)
     return jnp.concatenate([place_of(relative, bits, n), place_of(relative, bits[::-1], n), ends])
 
@@ -929,12 +872,9 @@
     return out[0], out[1]
 
 
-def total_over_all(value, nb, n):
-    for axis, size in (("batch", nb), ("seq", n)):
-        k = 1
-        while k < size:
-            value = value + swap_with(value, axis, k)
-            k *= 2
+def total_over(value, axis, steps):
+    for k in steps:
+        value = value + swap_with(value, axis, k)
     return value
 
 
@@ -971,24 +911,23 @@
     kh = kr // 2
     fr = hidden // n
     per_b = hidden // width
-    bits = low_bits(n)
+    bits = powers(n // 4)
     row = lambda v: v.reshape(1, -1)
     place = place_table(position, core, n)
 
     shard = query_key_value_weight.reshape(2, kh, 3, fb).transpose(0, 2, 1, 3)
+    stacked_up = up_weight.reshape(kr, per_b, fb).transpose(1, 0, 2).reshape(per_b * kr, fb)
+    rest = jnp.concatenate([down_weight, stacked_up, output_weight])
     part_a, part_b = halves(shard, direct(shard, n))
-    stacked_up = up_weight.reshape(kr, per_b, fb).transpose(1, 0, 2).reshape(per_b * kr, fb)
-    rest = jnp.stack(
-        [
-            jnp.concatenate([down_weight, output_weight[:kh]]),
-            jnp.concatenate([stacked_up, output_weight[kh:]]),
-        ]
-    )
-    part_a, rest = together(part_a, rest)
-    rest_up, rest_down = line_gather(rest, n)
-    part_a = gather_rest(part_a, bits)
-    part_b = gather_rest(part_b, bits[::-1])
-    qkv_pieces = gather_cores(gather_last(part_a, bits) + gather_last(part_b, bits[::-1]), nb)
+    rest_line = gather_line(rest, n)
+    for i, bit in enumerate(bits):
+        found_a = swap_with(part_a, "seq", bit)
+        found_b = swap_with(part_b, "seq", bits[-1 - i])
+        if i < len(bits) - 1:
+            part_a = jnp.concatenate([part_a, found_a])
+            part_b = jnp.concatenate([part_b, found_b])
+    qkv_pieces = gather_cores([part_a, found_a, part_b, found_b], nb)
+
     x = tokens.reshape(micros * local, width)
     g = cotangent.reshape(micros * local, width)
     micro = position * per // H
@@ -1008,18 +947,13 @@
         mine = lambda c: lax.dynamic_slice_in_dim(value, c * cols, cols, axis=1)
         return [mine(core)] + [swap_with(mine(core ^ k), "batch", k) for k in range(1, nb)]
 
-    qkv, h1 = project(place, x, row(gain_attn), row(shift_attn), qkv_pieces, micros, local, lanes)
-    qkv, rest_up[2], rest_down[2] = together(qkv, rest_up[2], rest_down[2])
-    rest_a, rest_b = line_halves(rest, rest_up, rest_down, position, n)
+    qkv, h1 = project(place, x, row(gain_attn), row(shift_attn), qkv_pieces, nb, n, micros, local, lanes)
+    qkv, rest_line = together(qkv, rest_line)
+    rest_plane = gather_plane(rest_line, n)
     qkv_all = swap(qkv.reshape(n, 3, local, lanes)).reshape(n, 3, bpd, BLOCK, lanes)
-    rest_a = gather_rest(rest_a, bits)
-    rest_b = gather_rest(rest_b, bits[::-1])
-    qkv_all, rest_a, rest_b = together(qkv_all, rest_a, rest_b)
-    rest_a = gather_last(rest_a, bits)
-    rest_b = gather_last(rest_b, bits[::-1])
     mixed, lse = attend(qkv_all, table, limit, per)
-    mixed, rest_a[1], rest_b[1] = together(mixed, rest_a[1], rest_b[1])
-    rest_pieces = gather_cores(rest_a + rest_b, nb)
+    mixed, rest_plane = together(mixed, rest_plane)
+    rest_pieces = gather_cores([rest_plane], nb)
     o = swap(mixed.reshape(n, local, lanes)).reshape(micros, groups, local, lanes)
     (
         result,
@@ -1036,6 +970,8 @@
         d_gain_ffn,
         d_shift_ffn,
     ) = middle(
+        nb,
+        n,
         place,
         o,
         x,
@@ -1050,8 +986,7 @@
     h1_cores = over_cores(h1)
     dout_all = swap(dout.reshape(n, local, lanes)).reshape(n, bpd, BLOCK, lanes)
 
-    parts = ffn_grads(
-        place,
+    rest_grad = ffn_grads(
         over_cores(act),
         columns_over_cores(g, fb),
         over_cores(h2),
@@ -1060,39 +995,32 @@
         columns_over_cores(branch, fb),
         n,
     )
-    dout_all, *parts = together(dout_all, *parts)
-    a_send, a_keep, b_send, b_keep = parts
-    first_a, first_b = reduce_first(a_send, b_send, n)
+    dout_all, rest_grad = together(dout_all, rest_grad)
+    grad_rest = scatter_groups(rest_grad, n)
     grads = attend_back(qkv_all, dout_all, lse, table, limit, per)
-    grads, first_a, first_b = together(grads, first_a, first_b)
     grads_back = swap(grads.reshape(n, 3, local, lanes)).reshape(micros, groups, 3, local, lanes)
-    reduced = reduce_rest(plus(a_keep, first_a), plus(b_keep, first_b), n)
-    early = [d_out_bias, d_up_bias, d_down_bias, d_gain_ffn, d_shift_ffn]
-    early_sums = total_over_all(jnp.concatenate(early, axis=1), nb, n)[0]
-    grads_back, early_sums, reduced = together(grads_back, early_sums, reduced)
-
     own_grads = split_by_core(place, grads_back, nb, n)
-    rest_arrived = line_reduce(reduced, position, n)
-
     grad_cores = [own_grads[0]] + [swap_with(own_grads[k], "batch", k) for k in range(1, nb)]
     a_send, a_keep, b_send, b_keep = qkv_grad(place, h1_cores, grad_cores, n)
     first_a, first_b = reduce_first(a_send, b_send, n)
     grad_x, d_gain_attn, d_shift_attn = input_grad(
-        place, own_grads, qkv_pieces, x, row(gain_attn), dmid, a_keep
+        place, own_grads, qkv_pieces, x, row(gain_attn), dmid, a_keep, n
     )
-    late = jnp.concatenate([d_gain_attn, d_shift_attn], axis=1)
-    late, first_a, first_b = together(late, first_a, first_b)
-    late = total_over_all(late, nb, n)[0]
+    vectors = [d_out_bias, d_up_bias, d_down_bias, d_gain_attn, d_shift_attn, d_gain_ffn, d_shift_ffn]
+    sums = jnp.concatenate(vectors, axis=1)
+    sums, first_a, first_b = together(sums, first_a, first_b)
     qkv_reduced = reduce_rest(plus(a_keep, first_a), plus(b_keep, first_b), n)
-    qkv_reduced, *rest_arrived = together(qkv_reduced, *rest_arrived)
+    sums = total_over(total_over(sums, "batch", powers(nb)), "seq", powers(n)[-2:])
+    qkv_reduced, sums = together(qkv_reduced, sums)
+    sums = total_over(sums, "seq", powers(n // 4))[0]
     grad_a, grad_b = reduce_last(qkv_reduced, reduce_direct(qkv_reduced, n))
     grad_qkv = jnp.stack([grad_a, grad_b]).transpose(0, 2, 1, 3).reshape(kr, 3 * fb)
-    grad_a, grad_b = reduce_last(reduced, rest_arrived)
-    grad_down = grad_a[:fr]
-    grad_up = grad_b[:fr].reshape(per_b, kr, fb).transpose(1, 0, 2).reshape(kr, per_b * fb)
-    grad_out = jnp.concatenate([grad_a[fr:], grad_b[fr:]])
-    ends = [width, width + hidden, 2 * width + hidden, 3 * width + hidden]
-    s_out_bias, s_up_bias, s_down_bias, s_gain_ffn, s_shift_ffn = jnp.split(early_sums, ends)
+    grad_down = grad_rest[:fr]
+    grad_up = grad_rest[fr:-kr].reshape(per_b, kr, fb).transpose(1, 0, 2).reshape(kr, per_b * fb)
+    grad_out = grad_rest[-kr:]
+    ends = []
+    for vector in vectors[:-1]:
+        ends.append((ends[-1] if ends else 0) + vector.shape[1])
     return (
         result.reshape(tokens.shape),
         grad_x.reshape(tokens.shape),
@@ -1100,13 +1028,7 @@
         grad_out,
         grad_up,
         grad_down,
-        s_out_bias,
-        s_up_bias,
-        s_down_bias,
-        late[:width],
-        late[width:],
-        s_gain_ffn,
-        s_shift_ffn,
+        *jnp.split(sums, ends),
     )
 
 

time: 601 us -> 540 us (0.90); the launches traced: 592 us -> 538 us
  blocking collectives: 0 us -> 113 us
  waiting for transfers between devices: 253 us -> 165 us
  starting transfers between devices: 120 us -> 50.1 us
  other arithmetic: 22.6 us -> 6.64 us
  between operations: 2.06 us -> 14.3 us
    all_to_all x0 -> x2, blocking collectives: none -> 113 us  [swap(): return lax.all_to_all(value, 'seq', split_axis=0, concat_axis=0, tiled=True)]
    ppermute x48 -> x32, waiting for transfers between devices: 188 us -> 84.4 us  [swap_with(): return lax.ppermute(value, axis, [(i, i ^ k) for i in range(size)])]
    ppermute x12 -> x0, waiting for transfers between devices: 40.5 us -> none  [the longest x6 20.3 us: move(): lax.ppermute(value, 'seq', [(i + quarter, i) for i in range(n - quarter)])]
    ppermute x12 -> x0, starting transfers between devices: 37.1 us -> none  [the longest x6 29.1 us: move(): lax.ppermute(value, 'seq', [(i, i + quarter) for i in range(n - quarter)])]
    all_to_all x4 -> x2, waiting for transfers between devices: 24.6 us -> 59.7 us  [swap(): return lax.all_to_all(value, 'seq', split_axis=0, concat_axis=0, tiled=True)]
    ppermute x48 -> x32, starting transfers between devices: 55.6 us -> 26.8 us  [swap_with(): return lax.ppermute(value, axis, [(i, i ^ k) for i in range(size)])]
    all_gather x0 -> x2, waiting for transfers between devices: none -> 18.2 us  [the longest x1 18.2 us: gather_plane(): plane = lax.all_gather(line, 'seq', axis_index_groups=planes(n))]
    convert_element_type x11 -> x4, other arithmetic: 9.07 us -> 1.44 us  [plus(): return (value.astype(F32) + arrived.astype(F32)).astype(BF)]
  transfers between devices with their start and end apart: 64 -> 38, of which waited for: 29 -> 21; matrix products, arithmetic and copies ran while one was open for 6% -> 3% of each run, Pallas kernels for 22% -> 25%
where the time goes in v3:
time: 540 us; the launch traced here: 538 us
  Pallas kernels  168 us (31%)
  waiting for transfers between devices  165 us (31%)
  blocking collectives  113 us (21%)
  starting transfers between devices  50.1 us (9%)
  local copies, waits for them, and re-layouts  20 us (4%)
  between operations  14.3 us (3%)
  other arithmetic  6.64 us (1%)
    all_to_all x2, blocking collectives, swap(): return lax.all_to_all(value, 'seq', split_axis=0, concat_axis=0, tiled=True)  113 us
    ppermute x32, waiting for transfers between devices, swap_with(): return lax.ppermute(value, axis, [(i, i ^ k) for i in range(size)])  84.4 us
    all_to_all x2, waiting for transfers between devices, swap(): return lax.all_to_all(value, 'seq', split_axis=0, concat_axis=0, tiled=True)  59.7 us
    pallas_call x1, Pallas kernels, attend_back(): pl.pallas_call(kernel, in_specs=[SMEM, SMEM, WHOLE, WHOLE, WHOLE], out_sp...  41.1 us
    pallas_call x1, Pallas kernels, attend(): pl.pallas_call(kernel, in_specs=[SMEM, SMEM, WHOLE], out_specs=[WHOLE, WH...  38 us
    pallas_call x1, Pallas kernels, middle(): pl.pallas_call(kernel, grid_spec=pltpu.PrefetchScalarGridSpec(num_scalar_...  36.3 us
    ppermute x32, starting transfers between devices, swap_with(): return lax.ppermute(value, axis, [(i, i ^ k) for i in range(size)])  26.8 us
    all_to_all x2, starting transfers between devices, swap(): return lax.all_to_all(value, 'seq', split_axis=0, concat_axis=0, tiled=True)  23.2 us
  transfers between devices with their start and end apart: 38, of which 21 were waited for; matrix products, arithmetic and copies ran while one was open for 3% of the time, Pallas kernels for 25%

profile of v3, /device:TPU:0, one launch (start us, length us, event | category | flops | bytes accessed | tf_op | source)
XLA Modules:
  0.0 537.7 jit_solution(1773215111068087550)
XLA Ops:
  10.4 3.1 collective-permute-start
  13.5 2.6 collective-permute-start.1
  16.1 5.7 %collective-permute-done = bf16[2,3,32,512]{3,2,1,0:T(8,128)(2,1)S(1)} collective-permute-done((bf16[2,3,32,512]{3,2,1,0:T(8,128)(2,1)S(1)}, bf16[2,3,32,512]{3,2,1,0:T(8,128)(2,1)S(1)}, u32[]{:S(2)}, u32[]{:S(2)}) %collective-permute-start) | collective-permute-done | bytes 196640 | tf_op jit(solution)/shard_map/ppermute | solution.py:772
  21.8 13.4 %collective-permute-done.1 = bf16[2,3,32,512]{3,2,1,0:T(8,128)(2,1)S(1)} collective-permute-done((bf16[2,3,32,512]{3,2,1,0:T(8,128)(2,1)S(1)}, bf16[2,3,32,512]{3,2,1,0:T(8,128)(2,1)S(1)}, u32[]{:S(2)}, u32[]{:S(2)}) %collective-permute-start.1) | collective-permute-done | bytes 196640 | tf_op jit(solution)/shard_map/ppermute | solution.py:772
  38.5 6.1 %collective-permute-done.5 = bf16[4,3,32,512]{3,2,1,0:T(8,128)(2,1)S(1)} collective-permute-done((bf16[4,3,32,512]{3,2,1,0:T(8,128)(2,1)S(1)}, bf16[4,3,32,512]{3,2,1,0:T(8,128)(2,1)S(1)}, u32[]{:S(2)}, u32[]{:S(2)}) %collective-permute-start.5) | collective-permute-done | bytes 393248 | tf_op jit(solution)/shard_map/ppermute | solution.py:772
  46.3 2.7 collective-permute-done.3
  49.7 11.8 %collective-permute-done.6.refs_3_.refs_5_ = bf16[8,3,32,512]{3,2,1,0:T(8,128)(2,1)S(1)} collective-permute-done((bf16[8,3,32,512]{3,2,1,0:T(8,128)(2,1)S(1)}, bf16[8,3,32,512]{3,2,1,0:T(8,128)(2,1)S(1)}, u32[]{:S(2)}, u32[]{:S(2)}) %collective-permute-start.6) | collective-permute-done | bytes 786464 | tf_op jit(solution)/shard_map/ppermute | solution.py:772
  65.1 10.0 %project.1 = (bf16[2,8,3,256,128]{4,3,2,1,0:T(8,128)(2,1)}, bf16[512,1024]{1,0:T(8,128)(2,1)}) custom-call(s32[34]{0:T(128)} %pad_add_fusion.place_ref, bf16[512,1024]{1,0:T(8,128)(2,1)} %bitcast.97, f32[1,1024]{1,0:T(1,128)} %bitcast.117, f32[1,1024]{1,0:T(1,128)} %bitcast.127, bf16[8,3,32,512]{3,2,1,0:T(8,128)(2,1)} %copy-done.3, ...), custom_call_target="tpu_custom_call" | custom-call | flops 3221225472 | bytes 14680064 | tf_op jit(solution)/shard_map/project/pallas_call | solution.py:113
  75.2 19.0 %all-to-all-start = ((bf16[16,3,256,128]{3,2,1,0:T(8,128)(2,1)}), bf16[16,3,256,128]{3,2,1,0:T(8,128)(2,1)S(1)}, u32[]{:S(2)}, u32[]{:S(2)}) async-start(bf16[16,3,256,128]{3,2,1,0:T(8,128)(2,1)} %bitcast.89), calls=%async_computation | async-start | bytes 6291456 | tf_op jit(solution)/shard_map/all_to_all | solution.py:941
  95.8 59.7 %all-to-all-done = bf16[16,3,256,128]{3,2,1,0:T(8,128)(2,1)S(1)} async-done(((bf16[16,3,256,128]{3,2,1,0:T(8,128)(2,1)}), bf16[16,3,256,128]{3,2,1,0:T(8,128)(2,1)S(1)}, u32[]{:S(2)}, u32[]{:S(2)}) %all-to-all-start) | async-done | bytes 3145760 | tf_op jit(solution)/shard_map/all_to_all | solution.py:941
  157.3 38.0 %attend.1 = (bf16[16,4,64,128]{3,2,1,0:T(8,128)(2,1)}, f32[64,128]{1,0:T(8,128)}) custom-call(s32[384]{0:T(512)} %reshape.131.table_ref, s32[1]{0:T(128)} %bitcast.2.limit_ref, bf16[16,3,4,64,128]{4,3,2,1,0:T(8,128)(2,1)} %bitcast.87), custom_call_target="tpu_custom_call" | custom-call | flops 40000000000 | bytes 4000000 | tf_op jit(solution)/shard_map/attend/pallas_call | solution.py:258
  195.3 18.2 %all-gather.7.cloned.1.call-done.refs_0_ = bf16[16,576,512]{2,1,0:T(8,128)(2,1)} async-done(((bf16[4,576,512]{2,1,0:T(8,128)(2,1)}), bf16[16,576,512]{2,1,0:T(8,128)(2,1)}) %all-gather.7.cloned.1.call-update) | async-done | bytes 9437200 | tf_op jit(solution)/shard_map/all_gather | solution.py:797
  213.5 34.9 %all_to_all.20 = bf16[16,256,128]{2,1,0:T(8,128)(2,1)} all-to-all(bf16[16,256,128]{2,1,0:T(8,128)(2,1)} %bitcast.102), channel_id=1, replica_groups=mesh['batch'=2,'seq'=16] {'seq'}, dimensions={0} | all-to-all | bytes 2097152 | tf_op jit(solution)/shard_map/all_to_all | solution.py:941
  248.4 36.3 %middle.1 = (bf16[512,1024]{1,0:T(8,128)(2,1)}, f32[512,1024]{1,0:T(8,128)}, bf16[512,1024]{1,0:T(8,128)(2,1)}, bf16[2,8,256,128]{3,2,1,0:T(8,128)(2,1)}, bf16[5...) custom-call(s32[34]{0:T(128)} %pad_add_fusion.place_ref, ...), custom_call_target="tpu_custom_call" | custom-call | flops 19327352832 | bytes 50000000 | tf_op jit(solution)/shard_map/middle/pallas_call | solution.py:527
  287.1 4.2 all-to-all-start.2
  291.4 2.2 constant_dynamic-slice_fusion.2
  296.6 2.9 collective-permute-done.17.refs_11_
  300.9 17.9 %ffn_grads.1 = bf16[4,4,576,512]{3,2,1,0:T(8,128)(2,1)} custom-call(bf16[512,4096]{1,0:T(8,128)(2,1)} %get-tuple-element.59.refs_0_, bf16[512,4096]{1,0:T(8,128)(2,1)} %collective-permute-done.12.refs_1_, bf16[512,512]{1,0:T(8,128)(2,1)} %get-tuple-element.132.refs_2_, bf16[512,512]{1,0:T(8,128)(2,1)} %copy-done.23, ...), custom_call_target="tpu_custom_call" | custom-call | flops 9663676416 | bytes 40000000 | tf_op jit(solution)/shard_map/ffn_grads/pallas_call | solution.py:627
  319.8 41.1 %attend_back.1 = bf16[16,3,4,64,128]{4,3,2,1,0:T(8,128)(2,1)} custom-call(s32[384]{0:T(512)} %reshape.131.table_ref, s32[1]{0:T(128)} %bitcast.2.limit_ref, bf16[16,3,4,64,128]{4,3,2,1,0:T(8,128)(2,1)} %bitcast.88, bf16[16,4,64,128]{3,2,1,0:T(8,128)(2,1)} %bitcast.100, f32[64,128]{1,0:T(8,128)} %get-tuple-element.65.lse_ref), custom_call_target="tpu_custom_call" | custom-call | flops 80000000000 | bytes 8000000 | tf_op jit(solution)/shard_map/attend_back/pallas_call | solution.py:354
  360.9 78.4 %all_to_all.21 = bf16[16,3,256,128]{3,2,1,0:T(8,128)(2,1)} all-to-all(bf16[16,3,256,128]{3,2,1,0:T(8,128)(2,1)} %bitcast.90), channel_id=1, replica_groups=mesh['batch'=2,'seq'=16] {'seq'}, dimensions={0} | all-to-all | bytes 6291456 | tf_op jit(solution)/shard_map/all_to_all | solution.py:941
  439.2 4.5 split_by_core.1
  444.3 2.6 reduce-scatter.7.cloned.1.call-done
  446.9 1.9 collective-permute-done.18.refs_1_
  450.0 7.7 %qkv_grad.1 = (bf16[8,3,32,512]{3,2,1,0:T(8,128)(2,1)}, bf16[8,3,32,512]{3,2,1,0:T(8,128)(2,1)}, bf16[8,3,32,512]{3,2,1,0:T(8,128)(2,1)}, bf16[8,3,32,512]{3,2,1,0:T(8,128)(2,1)}) custom-call(s32[34]{0:T(128)} %pad_add_fusion.place_ref, bf16[512,1024]{1,0:T(8,128)(2,1)} %get-tuple-element.68.refs_0_, bf16[512,1024]{1,0:T(8,128)(2,1)} %collective-permute-done.18.refs_1_, ...), custom_call_target="tpu_custom_call" | custom-call | flops 3221225472 | bytes 15000000 | tf_op jit(solution)/shard_map/qkv_grad/pallas_call | solution.py:702
  459.2 12.7 %input_grad.1 = (f32[512,1024]{1,0:T(8,128)}, f32[1,1024]{1,0:T(1,128)}, f32[1,1024]{1,0:T(1,128)}) custom-call(s32[34]{0:T(128)} %pad_add_fusion.place_ref, bf16[512,1024]{1,0:T(8,128)(2,1)} %bitcast.99, f32[1,1024]{1,0:T(1,128)} %bitcast.118, f32[512,1024]{1,0:T(8,128)} %get-tuple-element.57.dmid_ref, bf16[512,1536]{1,0:T(8,128)(2,1)} %get-tuple-element.66.refs_2_.refs_0_, ...), custom_call_target="tpu_custom_call" | custom-call | flops 3221225472 | bytes 20000000 | tf_op jit(solution)/shard_map/input_grad/pallas_call | solution.py:755
  473.4 4.0 collective-permute-done.20
  484.1 4.3 collective-permute-done.25
  489.8 7.9 %collective-permute-done.26 = f32[1,10240]{1,0:T(1,128)S(1)} collective-permute-done((f32[1,10240]{1,0:T(1,128)S(1)}, f32[1,10240]{1,0:T(1,128)S(1)}, u32[]{:S(2)}, u32[]{:S(2)}) %collective-permute-start.26) | collective-permute-done | bytes 40992 | tf_op jit(solution)/shard_map/ppermute | solution.py:772
  500.9 2.6 collective-permute-done.30
  506.1 3.7 collective-permute-start.29
  511.0 5.0 collective-permute-done.27
  516.0 10.3 %collective-permute-done.28 = bf16[2,3,32,512]{3,1,2,0:T(4,128)(2,1)S(1)} collective-permute-done((bf16[2,3,32,512]{3,1,2,0:T(4,128)(2,1)S(1)}, bf16[2,3,32,512]{3,1,2,0:T(4,128)(2,1)S(1)}, u32[]{:S(2)}, u32[]{:S(2)}) %collective-permute-start.28) | collective-permute-done | bytes 196640 | tf_op jit(solution)/shard_map/ppermute | solution.py:772
  (158 shorter events, 48.0 us)
Async XLA Ops:
  7.2 68.0 %all-gather.5.cloned.1.call-start = ((), (), s32[]{:S(2)}) async-start(), calls=%async_computation.7 | async-start | bytes 2949120 | tf_op jit(solution)/shard_map/all_gather | solution.py:793
  10.1 203.3 %all-gather.7.cloned.1.call-start = ((), (), s32[]{:S(2)}) async-start(), calls=%async_computation.8 | async-start | bytes 11796480 | tf_op jit(solution)/shard_map/all_gather | solution.py:797
  10.4 11.4 %collective-permute-start = (bf16[2,3,32,512]{3,2,1,0:T(8,128)(2,1)S(1)}, bf16[2,3,32,512]{3,2,1,0:T(8,128)(2,1)S(1)}, u32[]{:S(2)}, u32[]{:S(2)}) collective-permute-start(bf16[2,3,32,512]{3,2,1,0:T(8,128)(2,1)S(1)} %bitcast.106), channel_id=1, source_target_pairs={{0,4},{1,5},{2,6},{3,7},{4,0},{5,1},{6,2},{7,3},{8,12},{9,13},{10,... | collective-permute-start | bytes 589832 | tf_op jit(solution)/shard_map/ppermute | solution.py:772
  13.5 21.7 %collective-permute-start.1 = (bf16[2,3,32,512]{3,2,1,0:T(8,128)(2,1)S(1)}, bf16[2,3,32,512]{3,2,1,0:T(8,128)(2,1)S(1)}, u32[]{:S(2)}, u32[]{:S(2)}) collective-permute-start(bf16[2,3,32,512]{3,2,1,0:T(8,128)(2,1)S(1)} %bitcast.107), channel_id=1, source_target_pairs={{0,8},{1,9},{2,10},{3,11},{4,12},{5,13},{6,14},{7,15},{8,0},{9,1},... | collective-permute-start | bytes 589832 | tf_op jit(solution)/shard_map/ppermute | solution.py:772
  16.1 19.1 %collective-permute-start.2 = (bf16[2,3,32,512]{3,2,1,0:T(8,128)(2,1)S(1)}, bf16[2,3,32,512]{3,2,1,0:T(8,128)(2,1)S(1)}, u32[]{:S(2)}, u32[]{:S(2)}) collective-permute-start(bf16[2,3,32,512]{3,2,1,0:T(8,128)(2,1)S(1)} %bitcast.108), channel_id=1, source_target_pairs={{0,12},{1,13},{2,14},{3,15},{4,8},{5,9},{6,10},{7,11},{8,4},{9,5},... | collective-permute-start | bytes 589832 | tf_op jit(solution)/shard_map/ppermute | solution.py:772
  35.4 9.2 %collective-permute-start.5 = (bf16[4,3,32,512]{3,2,1,0:T(8,128)(2,1)S(1)}, bf16[4,3,32,512]{3,2,1,0:T(8,128)(2,1)S(1)}, u32[]{:S(2)}, u32[]{:S(2)}) collective-permute-start(bf16[4,3,32,512]{3,2,1,0:T(8,128)(2,1)S(1)} %get-tuple-element.137), channel_id=1, source_target_pairs={{0,2},{1,3},{2,0},{3,1},{4,6},{5,7},{6,4},{7,5},{8,10},{9,11},{10,... | collective-permute-start | bytes 1179656 | tf_op jit(solution)/shard_map/ppermute | solution.py:772
  37.0 12.0 %collective-permute-start.3 = (bf16[4,3,32,512]{3,2,1,0:T(8,128)(2,1)S(1)}, bf16[4,3,32,512]{3,2,1,0:T(8,128)(2,1)S(1)}, u32[]{:S(2)}, u32[]{:S(2)}) collective-permute-start(bf16[4,3,32,512]{3,2,1,0:T(8,128)(2,1)S(1)} %get-tuple-element.138), channel_id=1, source_target_pairs={{0,1},{1,0},{2,3},{3,2},{4,5},{5,4},{6,7},{7,6},{8,9},{9,8},{10,11... | collective-permute-start | bytes 1179656 | tf_op jit(solution)/shard_map/ppermute | solution.py:772
  44.6 16.9 %collective-permute-start.6 = (bf16[8,3,32,512]{3,2,1,0:T(8,128)(2,1)S(1)}, bf16[8,3,32,512]{3,2,1,0:T(8,128)(2,1)S(1)}, u32[]{:S(2)}, u32[]{:S(2)}) collective-permute-start(bf16[8,3,32,512]{3,2,1,0:T(8,128)(2,1)S(1)} %pad_maximum_fusion.3.refs_2_.refs_4_), channel_id=1, source_target_pairs={{0,1},{1,0},{2,3},{3,2},{4,5},{5,4},{6,7},{7,6},{8,9},{9,8},{10,11... | collective-permute-start | bytes 2359304 | tf_op jit(solution)/shard_map/ppermute | solution.py:772
  49.0 12.5 %collective-permute-start.4 = (bf16[8,3,32,512]{3,2,1,0:T(8,128)(2,1)S(1)}, bf16[8,3,32,512]{3,2,1,0:T(8,128)(2,1)S(1)}, u32[]{:S(2)}, u32[]{:S(2)}) collective-permute-start(bf16[8,3,32,512]{3,2,1,0:T(8,128)(2,1)S(1)} %pad_maximum_fusion.2.refs_0_.refs_2_), channel_id=1, source_target_pairs={{0,2},{1,3},{2,0},{3,1},{4,6},{5,7},{6,4},{7,5},{8,10},{9,11},{10,... | collective-permute-start | bytes 2359304 | tf_op jit(solution)/shard_map/ppermute | solution.py:772
  49.1 13.5 %collective-permute-start.9 = (bf16[8,3,32,512]{3,2,1,0:T(8,128)(2,1)S(1)}, bf16[8,3,32,512]{3,2,1,0:T(8,128)(2,1)}, u32[]{:S(2)}, u32[]{:S(2)}) collective-permute-start(bf16[8,3,32,512]{3,2,1,0:T(8,128)(2,1)S(1)} %pad_maximum_fusion.3.refs_2_.refs_4_), channel_id=1, source_target_pairs={{0,16},{16,0},{1,17},{17,1},{2,18},{18,2},{3,19},{19,3},{4,20},{20... | collective-permute-start | bytes 2359304 | tf_op jit(solution)/shard_map/ppermute | solution.py:772
  49.2 13.5 %collective-permute-start.7 = (bf16[8,3,32,512]{3,2,1,0:T(8,128)(2,1)S(1)}, bf16[8,3,32,512]{3,2,1,0:T(8,128)(2,1)}, u32[]{:S(2)}, u32[]{:S(2)}) collective-permute-start(bf16[8,3,32,512]{3,2,1,0:T(8,128)(2,1)S(1)} %pad_maximum_fusion.2.refs_0_.refs_2_), channel_id=1, source_target_pairs={{0,16},{16,0},{1,17},{17,1},{2,18},{18,2},{3,19},{19,3},{4,20},{20... | collective-permute-start | bytes 2359304 | tf_op jit(solution)/shard_map/ppermute | solution.py:772
  75.2 80.3 %all-to-all-start = ((bf16[16,3,256,128]{3,2,1,0:T(8,128)(2,1)}), bf16[16,3,256,128]{3,2,1,0:T(8,128)(2,1)S(1)}, u32[]{:S(2)}, u32[]{:S(2)}) async-start(bf16[16,3,256,128]{3,2,1,0:T(8,128)(2,1)} %bitcast.89), calls=%async_computation | async-start | bytes 6291456 | tf_op jit(solution)/shard_map/all_to_all | solution.py:941
  213.5 34.9 %collective-permute-start.11 = (bf16[16,576,512]{2,1,0:T(8,128)(2,1)}, bf16[16,576,512]{2,1,0:T(8,128)(2,1)}, u32[]{:S(2)}, u32[]{:S(2)}) collective-permute-start(bf16[16,576,512]{2,1,0:T(8,128)(2,1)} %all-gather.7.cloned.1.call-done.refs_0_), channel_id=1, source_target_pairs={{0,16},{16,0},{1,17},{17,1},{2,18},{18,2},{3,19},{19,3},{4,20},{20... | collective-permute-start | bytes 28311560 | tf_op jit(solution)/shard_map/ppermute | solution.py:772
  284.7 14.8 %collective-permute-start.12 = (bf16[512,4096]{1,0:T(8,128)(2,1)}, bf16[512,4096]{1,0:T(8,128)(2,1)}, u32[]{:S(2)}, u32[]{:S(2)}) collective-permute-start(bf16[512,4096]{1,0:T(8,128)(2,1)} %get-tuple-element.59.refs_0_), channel_id=1, source_target_pairs={{0,16},{16,0},{1,17},{17,1},{2,18},{18,2},{3,19},{19,3},{4,20},{20... | collective-permute-start | bytes 12582920 | tf_op jit(solution)/shard_map/ppermute | solution.py:772
  286.5 12.9 %collective-permute-start.15 = (bf16[1,512,2048]{2,1,0:T(8,128)(2,1)S(1)}, bf16[1,512,2048]{2,1,0:T(8,128)(2,1)}, u32[]{:S(2)}, u32[]{:S(2)}) collective-permute-start(bf16[1,512,2048]{2,1,0:T(8,128)(2,1)S(1)} %slice.61), channel_id=1, source_target_pairs={{0,16},{16,0},{1,17},{17,1},{2,18},{18,2},{3,19},{19,3},{4,20},{20... | collective-permute-start | bytes 6291464 | tf_op jit(solution)/shard_map/ppermute | solution.py:772
  287.1 31.7 %all-to-all-start.2 = ((bf16[16,256,128]{2,1,0:T(8,128)(2,1)}), bf16[16,256,128]{2,1,0:T(8,128)(2,1)S(1)}, u32[]{:S(2)}, u32[]{:S(2)}) async-start(bf16[16,256,128]{2,1,0:T(8,128)(2,1)} %bitcast.31), calls=%async_computation.2 | async-start | bytes 2097152 | tf_op jit(solution)/shard_map/all_to_all | solution.py:941
  291.3 155.6 %reduce-scatter.7.cloned.1.call-start = ((), (), s32[]{:S(2)}) async-start(), calls=%async_computation.9 | async-start | bytes 11796480
  293.6 5.9 %collective-permute-start.14 = (bf16[512,1024]{1,0:T(8,128)(2,1)}, bf16[512,1024]{1,0:T(8,128)(2,1)S(1)}, u32[]{:S(2)}, u32[]{:S(2)}) collective-permute-start(bf16[512,1024]{1,0:T(8,128)(2,1)} %get-tuple-element.60.refs_4_), channel_id=1, source_target_pairs={{0,16},{16,0},{1,17},{17,1},{2,18},{18,2},{3,19},{19,3},{4,20},{20... | collective-permute-start | bytes 3145736 | tf_op jit(solution)/shard_map/ppermute | solution.py:772
  294.1 5.4 collective-permute-start.16
  319.8 207.7 %reduce-scatter.5.cloned.1.call-start = ((), (), s32[]{:S(2)}) async-start(), calls=%async_computation.6 | async-start | bytes 2949120 | tf_op jit(solution)/shard_map/reduce_scatter | solution.py:804
  443.7 5.1 collective-permute-start.19
  443.8 5.0 collective-permute-start.18
  457.7 19.7 %collective-permute-start.20 = (bf16[8,3,32,512]{3,2,1,0:T(8,128)(2,1)}, bf16[8,3,32,512]{3,2,1,0:T(8,128)(2,1)S(1)}, u32[]{:S(2)}, u32[]{:S(2)}) collective-permute-start(bf16[8,3,32,512]{3,2,1,0:T(8,128)(2,1)} %get-tuple-element.78), channel_id=1, source_target_pairs={{0,2},{1,3},{2,0},{3,1},{4,6},{5,7},{6,4},{7,5},{8,10},{9,11},{10,... | collective-permute-start | bytes 2359304 | tf_op jit(solution)/shard_map/ppermute | solution.py:772
  458.7 19.5 %collective-permute-start.21 = (bf16[8,3,32,512]{3,2,1,0:T(8,128)(2,1)}, bf16[8,3,32,512]{3,2,1,0:T(8,128)(2,1)S(1)}, u32[]{:S(2)}, u32[]{:S(2)}) collective-permute-start(bf16[8,3,32,512]{3,2,1,0:T(8,128)(2,1)} %get-tuple-element.79), channel_id=1, source_target_pairs={{0,1},{1,0},{2,3},{3,2},{4,5},{5,4},{6,7},{7,6},{8,9},{9,8},{10,11... | collective-permute-start | bytes 2359304 | tf_op jit(solution)/shard_map/ppermute | solution.py:772
  478.9 18.9 %collective-permute-start.22 = (bf16[4,1,3,32,512]{4,2,3,1,0:T(4,128)(2,1)S(1)}, bf16[4,1,3,32,512]{4,2,3,1,0:T(4,128)(2,1)S(1)}, u32[]{:S(2)}, u32[]{:S(2)}) collective-permute-start(bf16[4,1,3,32,512]{4,2,3,1,0:T(4,128)(2,1)S(1)} %copy.63), channel_id=1, source_target_pairs={{0,1},{1,0},{2,3},{3,2},{4,5},{5,4},{6,7},{7,6},{8,9},{9,8},{10,11... | collective-permute-start | bytes 1179656 | tf_op jit(solution)/shard_map/ppermute | solution.py:772
  480.3 17.9 %collective-permute-start.23 = (bf16[4,1,3,32,512]{4,2,3,1,0:T(4,128)(2,1)S(1)}, bf16[4,1,3,32,512]{4,2,3,1,0:T(4,128)(2,1)S(1)}, u32[]{:S(2)}, u32[]{:S(2)}) collective-permute-start(bf16[4,1,3,32,512]{4,2,3,1,0:T(4,128)(2,1)S(1)} %copy.65), channel_id=1, source_target_pairs={{0,2},{1,3},{2,0},{3,1},{4,6},{5,7},{6,4},{7,5},{8,10},{9,11},{10,... | collective-permute-start | bytes 1179656 | tf_op jit(solution)/shard_map/ppermute | solution.py:772
  482.6 5.8 %collective-permute-start.25 = (f32[1,10240]{1,0:T(1,128)S(1)}, f32[1,10240]{1,0:T(1,128)S(1)}, u32[]{:S(2)}, u32[]{:S(2)}) collective-permute-start(f32[1,10240]{1,0:T(1,128)S(1)} %add.86), channel_id=1, source_target_pairs={{0,4},{1,5},{2,6},{3,7},{4,0},{5,1},{6,2},{7,3},{8,12},{9,13},{10,... | collective-permute-start | bytes 122888 | tf_op jit(solution)/shard_map/ppermute | solution.py:772
  488.5 9.2 %collective-permute-start.26 = (f32[1,10240]{1,0:T(1,128)S(1)}, f32[1,10240]{1,0:T(1,128)S(1)}, u32[]{:S(2)}, u32[]{:S(2)}) collective-permute-start(f32[1,10240]{1,0:T(1,128)S(1)} %add.87), channel_id=1, source_target_pairs={{0,8},{1,9},{2,10},{3,11},{4,12},{5,13},{6,14},{7,15},{8,0},{9,1},... | collective-permute-start | bytes 122888 | tf_op jit(solution)/shard_map/ppermute | solution.py:772
  503.5 6.2 %collective-permute-start.31 = (f32[1,10240]{1,0:T(1,128)S(1)}, f32[1,10240]{1,0:T(1,128)S(1)}, u32[]{:S(2)}, u32[]{:S(2)}) collective-permute-start(f32[1,10240]{1,0:T(1,128)S(1)} %add.92), channel_id=1, source_target_pairs={{0,2},{1,3},{2,0},{3,1},{4,6},{5,7},{6,4},{7,5},{8,10},{9,11},{10,... | collective-permute-start | bytes 122888 | tf_op jit(solution)/shard_map/ppermute | solution.py:772
  505.3 10.8 %collective-permute-start.27 = (bf16[2,3,32,512]{3,1,2,0:T(4,128)(2,1)S(1)}, bf16[2,3,32,512]{3,1,2,0:T(4,128)(2,1)S(1)}, u32[]{:S(2)}, u32[]{:S(2)}) collective-permute-start(bf16[2,3,32,512]{3,1,2,0:T(4,128)(2,1)S(1)} %get-tuple-element.126), channel_id=1, source_target_pairs={{0,4},{1,5},{2,6},{3,7},{4,0},{5,1},{6,2},{7,3},{8,12},{9,13},{10,... | collective-permute-start | bytes 589832 | tf_op jit(solution)/shard_map/ppermute | solution.py:772
  505.3 20.9 %collective-permute-start.28 = (bf16[2,3,32,512]{3,1,2,0:T(4,128)(2,1)S(1)}, bf16[2,3,32,512]{3,1,2,0:T(4,128)(2,1)S(1)}, u32[]{:S(2)}, u32[]{:S(2)}) collective-permute-start(bf16[2,3,32,512]{3,1,2,0:T(4,128)(2,1)S(1)} %get-tuple-element.128), channel_id=1, source_target_pairs={{0,8},{1,9},{2,10},{3,11},{4,12},{5,13},{6,14},{7,15},{8,0},{9,1},... | collective-permute-start | bytes 589832 | tf_op jit(solution)/shard_map/ppermute | solution.py:772
  506.1 20.2 %collective-permute-start.29 = (bf16[2,3,32,512]{3,1,2,0:T(4,128)(2,1)S(1)}, bf16[2,3,32,512]{3,1,2,0:T(4,128)(2,1)S(1)}, u32[]{:S(2)}, u32[]{:S(2)}) collective-permute-start(bf16[2,3,32,512]{3,1,2,0:T(4,128)(2,1)S(1)} %get-tuple-element.127), channel_id=1, source_target_pairs={{0,12},{1,13},{2,14},{3,15},{4,8},{5,9},{6,10},{7,11},{8,4},{9,5},... | collective-permute-start | bytes 589832 | tf_op jit(solution)/shard_map/ppermute | solution.py:772
  (32 other events, 261.6 us)
Sparse Core Ops, SparseCore 0:
  10.3 61.4 all-gather.4
  75.3 138.0 all-gather.6
  319.0 127.8 reduce-scatter.6
  449.0 49.9 reduce-scatter.4

commit v4 on v3

--- a/solution.py
+++ b/solution.py
@@ -161,32 +161,30 @@
 
 
 def key_lists(b, table_ref, limit, nblk, per):
+    penalty = lambda ok: jnp.where(ok, 0.0, -BIG)
     shared = [0, 1, b - 1, b, jnp.minimum(b + 1, nblk - 1)]
     lists = [[s] for s in shared]
-    biases = [
-        None,
-        None,
-        jnp.where((b - 1) * BLOCK < limit, 0.0, -BIG),
-        jnp.where(b * BLOCK < limit, 0.0, -BIG),
-        jnp.where(((b + 1) * BLOCK < limit) & (b + 1 < nblk), 0.0, -BIG),
-    ]
-    item = lane_item((1, per * HD))
+    inside = lambda block: block * BLOCK < limit
+    biases = [None, None, penalty(inside(b - 1)), penalty(inside(b)), penalty(inside(b + 1) & (b + 1 < nblk))]
+    biases = [[bias] * per for bias in biases]
     for r in range(NRAND):
         blocks = [table_ref[b * per * NRAND + i * NRAND + r] for i in range(per)]
-        bias = jnp.where(blocks[0] * BLOCK < limit, 0.0, -BIG)
-        for i in range(1, per):
-            bias = jnp.where(item == i, jnp.where(blocks[i] * BLOCK < limit, 0.0, -BIG), bias)
         lists.append(blocks)
-        biases.append(bias)
+        biases.append([penalty(inside(block)) for block in blocks])
     return lists, biases
 
 
-def masked_scores(keys, queries, biases):
-    s = nt(keys, queries)
+def add_biases(s, biases):
+    item = lane_item((1, s.shape[1]))
     parts = []
-    for i, bias in enumerate(biases):
-        part = s[i * BLOCK : (i + 1) * BLOCK]
-        parts.append(part if bias is None else part + bias)
+    for j, bias in enumerate(biases):
+        part = s[j * BLOCK : (j + 1) * BLOCK]
+        if bias[0] is not None:
+            row = bias[0]
+            for i in range(1, len(bias)):
+                row = row if bias[i] is bias[0] else jnp.where(item == i, bias[i], row)
+            part = part + row
+        parts.append(part)
     return jnp.concatenate(parts, axis=0)
 
 
@@ -195,60 +193,85 @@
     return ref[pl.ds(c * span, span), part].reshape(chunk, ref.shape[4])
 
 
+def to_row(square):
+    eye = lax.broadcasted_iota(jnp.int32, square.shape, 0) == lax.broadcasted_iota(jnp.int32, square.shape, 1)
+    return jnp.sum(jnp.where(eye, square, 0.0), axis=0, keepdims=True)
+
+
+def with_ones(values):
+    return jnp.concatenate([values, jnp.ones_like(values)], axis=1)
+
+
+def fold(value, width, combine):
+    out = value[:, :width]
+    for at in range(width, value.shape[1], width):
+        out = combine(out, value[:, at : at + width])
+    return out
+
+
 def attend_kernel(table_ref, limit_ref, qkv_ref, out_ref, lse_ref, s_ref, *, per, bpd, nblk):
     limit = limit_ref[0]
     lanes = per * HD
+    rows = per * BLOCK
     chunk = 2 * bpd * BLOCK
     chunks = nblk * BLOCK // chunk
+    tile = 2 * BLOCK
 
     def query(b):
         q = qkv_ref[b // bpd, 0, b % bpd] * jnp.asarray(SCALE, BF)
         return block_diagonal(q, per)
 
     both = jnp.concatenate([query(g) for g in range(NGLOB)], axis=0)
-    rowid = lax.broadcasted_iota(jnp.int32, (chunk, NGLOB * lanes), 0)
+    key_id = lax.broadcasted_iota(jnp.int32, (1, chunk), 1)
 
     def score(c, top):
-        s = nt(global_keys(qkv_ref, 1, c, bpd, chunk), both)
-        s = jnp.where(c * chunk + rowid < limit, s, -BIG)
-        s_ref[pl.ds(c * chunk, chunk), :] = s
-        return jnp.maximum(top, jnp.max(s, axis=0, keepdims=True))
-
-    top = lax.fori_loop(0, chunks, score, jnp.full((1, NGLOB * lanes), -BIG, F32))
-
-    def total(c, sums):
-        p = jnp.exp(s_ref[pl.ds(c * chunk, chunk), :] - top)
-        s_ref[pl.ds(c * chunk, chunk), :] = p
-        return sums + jnp.sum(p, axis=0, keepdims=True)
-
-    sums = lax.fori_loop(0, chunks, total, jnp.zeros((1, NGLOB * lanes), F32))
-    inv = 1.0 / sums
-    lse = top + jnp.log(sums)
+        s = nt(both, global_keys(qkv_ref, 1, c, bpd, chunk))
+        s = s + jnp.where(c * chunk + key_id < limit, 0.0, -BIG)
+        s_ref[c] = s
+        return jnp.maximum(top, fold(s, tile, jnp.maximum))
+
+    top = lax.fori_loop(0, chunks, score, jnp.full((NGLOB * rows, tile), -BIG, F32))
+    top = jnp.max(top, axis=1, keepdims=True)
+
+    def mix(c, acc):
+        p = jnp.exp(s_ref[c] - top)
+        return acc + nn(p.astype(BF), with_ones(global_keys(qkv_ref, 2, c, bpd, chunk)))
+
+    acc = lax.fori_loop(0, chunks, mix, jnp.zeros((NGLOB * rows, 2 * lanes), F32))
+    lse = top + jnp.log(acc[:, lanes:])
+    acc = acc[:, :lanes] * (1.0 / acc[:, lanes:])
     for g in range(NGLOB):
-        lse_ref[pl.ds(g, 1), :] = lse[:, g * lanes : (g + 1) * lanes]
-
-    def mix(c, acc):
-        w = (s_ref[pl.ds(c * chunk, chunk), :] * inv).astype(BF)
-        return acc + tn(w, global_keys(qkv_ref, 2, c, bpd, chunk))
-
-    acc = lax.fori_loop(0, chunks, mix, jnp.zeros((NGLOB * lanes, lanes), F32))
-    for g in range(NGLOB):
-        out_ref[g // bpd, g % bpd] = take_diagonal(acc[g * lanes : (g + 1) * lanes], per).astype(BF)
+        at = slice(g * rows, (g + 1) * rows)
+        lse_ref[pl.ds(g, 1), :] = to_row(lse[at])
+        out_ref[g // bpd, g % bpd] = take_diagonal(acc[at], per).astype(BF)
 
     def sparse(b, carry):
         lists, biases = key_lists(b, table_ref, limit, nblk, per)
         keys = jnp.concatenate([pick(qkv_ref, 1, blocks, bpd) for blocks in lists], axis=0)
         values = jnp.concatenate([pick(qkv_ref, 2, blocks, bpd) for blocks in lists], axis=0)
-        s = masked_scores(keys, query(b), biases)
-        top = jnp.max(s, axis=0, keepdims=True)
-        p = jnp.exp(s - top)
-        sums = jnp.sum(p, axis=0, keepdims=True)
-        w = (p * (1.0 / sums)).astype(BF)
-        lse_ref[pl.ds(b, 1), :] = top + jnp.log(sums)
-        out_ref[b // bpd, b % bpd] = take_diagonal(tn(w, values), per).astype(BF)
+        s = nt(query(b), keys)
+        which = lax.broadcasted_iota(jnp.int32, (1, tile), 1) < BLOCK
+        parts = []
+        for i in range(per):
+            for j in range(0, len(lists), 2):
+                part = s[i * BLOCK : (i + 1) * BLOCK, j * BLOCK : (j + 2) * BLOCK]
+                one, two = biases[j][i], biases[j + 1][i]
+                if one is not None or two is not None:
+                    part = part + jnp.where(which, 0.0 if one is None else one, 0.0 if two is None else two)
+                parts.append(part)
+        half = len(lists) // 2
+        s = [jnp.concatenate([parts[i * half + j] for i in range(per)], axis=0) for j in range(half)]
+        top = jnp.max(functools.reduce(jnp.maximum, s), axis=1, keepdims=True)
+        p = [jnp.exp(part - top) for part in s]
+        mixed = nn(jnp.concatenate([part.astype(BF) for part in p], axis=1), with_ones(values))
+        sums = mixed[:, lanes:]
+        lse_ref[pl.ds(b, 1), :] = to_row(top + jnp.log(sums))
+        out_ref[b // bpd, b % bpd] = take_diagonal(mixed[:, :lanes] * (1.0 / sums), per).astype(BF)
         return carry
 
-    lax.fori_loop(NGLOB, nblk, sparse, 0, unroll=2)
+    for b in range(NGLOB, 4):
+        sparse(b, 0)
+    lax.fori_loop(4, nblk, sparse, 0, unroll=4)
 
 
 def attend(qkv, table, limit, per):
@@ -263,7 +286,7 @@
             jax.ShapeDtypeStruct((n, bpd, BLOCK, lanes), BF),
             jax.ShapeDtypeStruct((nblk, lanes), F32),
         ],
-        scratch_shapes=[pltpu.VMEM((nblk * BLOCK, NGLOB * lanes), F32)],
+        scratch_shapes=[pltpu.VMEM((n // 2, NGLOB * per * BLOCK, 2 * bpd * BLOCK), F32)],
         compiler_params=params(),
         cost_estimate=cost(40e9, 4e6, 1e7),
         name="attend",
@@ -320,14 +343,19 @@
         values = jnp.concatenate([pick(qkv_ref, 2, blocks, bpd) for blocks in lists], axis=0)
         q = query(b)
         do = upstream(b)
-        s = masked_scores(keys, q, biases)
+        zero = jnp.zeros_like(q)
+        sides = jnp.concatenate(
+            [jnp.concatenate([q, zero], axis=1), jnp.concatenate([zero, do], axis=1)], axis=0
+        )
+        both_scores = nt(jnp.concatenate([keys, values], axis=1), sides)
+        s = add_biases(both_scores[:, : q.shape[0]], biases)
+        dw = both_scores[:, q.shape[0] :]
         w = jnp.exp(s - lse_ref[pl.ds(b, 1), :])
-        dw = nt(values, do)
         centre = jnp.sum(w * dw, axis=0, keepdims=True)
         ds = (w * (dw - centre)).astype(BF)
         grad_ref[b // bpd, 0, b % bpd] = (take_diagonal(tn(ds, keys), per) * SCALE).astype(BF)
-        dk = nn(ds, q)
-        dv = nn(w.astype(BF), do)
+        both_grads = nn(jnp.concatenate([ds, w.astype(BF)], axis=1), sides)
+        dk, dv = both_grads[:, :lanes], both_grads[:, lanes:]
         item = lane_item((BLOCK, lanes))
         for ref, full in ((dk_ref, dk), (dv_ref, dv)):
             for k, blocks in enumerate(lists):
@@ -337,7 +365,9 @@
                     ref[block // bpd, block % bpd] += term
         return carry
 
-    lax.fori_loop(NGLOB, nblk, sparse, 0, unroll=2)
+    for b in range(NGLOB, 4):
+        sparse(b, 0)
+    lax.fori_loop(4, nblk, sparse, 0, unroll=4)
 
     def finish(c, carry):
         grad_ref[c, 1] = dk_ref[c].astype(BF)
@@ -798,10 +828,8 @@
     return plane.reshape((n,) + line.shape[1:])
 
 
-def scatter_groups(grad, n):
-    scatter = functools.partial(lax.psum_scatter, axis_name="seq", scatter_dimension=0)
-    line = scatter(grad, axis_index_groups=planes(n))
-    return scatter(line, axis_index_groups=lines(n)).astype(F32)
+def scatter_groups(grad, groups):
+    return lax.psum_scatter(grad, "seq", scatter_dimension=0, axis_index_groups=groups)
 
 
 def halves(shard, arrived):
@@ -919,6 +947,7 @@
     stacked_up = up_weight.reshape(kr, per_b, fb).transpose(1, 0, 2).reshape(per_b * kr, fb)
     rest = jnp.concatenate([down_weight, stacked_up, output_weight])
     part_a, part_b = halves(shard, direct(shard, n))
+    part_a, part_b, rest = together(part_a, part_b, rest)
     rest_line = gather_line(rest, n)
     for i, bit in enumerate(bits):
         found_a = swap_with(part_a, "seq", bit)
@@ -952,9 +981,9 @@
     rest_plane = gather_plane(rest_line, n)
     qkv_all = swap(qkv.reshape(n, 3, local, lanes)).reshape(n, 3, bpd, BLOCK, lanes)
     mixed, lse = attend(qkv_all, table, limit, per)
-    mixed, rest_plane = together(mixed, rest_plane)
+    o = swap(mixed.reshape(n, local, lanes)).reshape(micros, groups, local, lanes)
+    o, rest_plane = together(o, rest_plane)
     rest_pieces = gather_cores([rest_plane], nb)
-    o = swap(mixed.reshape(n, local, lanes)).reshape(micros, groups, local, lanes)
     (
         result,
         dmid,
@@ -996,12 +1025,14 @@
         n,
     )
     dout_all, rest_grad = together(dout_all, rest_grad)
-    grad_rest = scatter_groups(rest_grad, n)
+    rest_line = scatter_groups(rest_grad, planes(n))
     grads = attend_back(qkv_all, dout_all, lse, table, limit, per)
     grads_back = swap(grads.reshape(n, 3, local, lanes)).reshape(micros, groups, 3, local, lanes)
     own_grads = split_by_core(place, grads_back, nb, n)
     grad_cores = [own_grads[0]] + [swap_with(own_grads[k], "batch", k) for k in range(1, nb)]
     a_send, a_keep, b_send, b_keep = qkv_grad(place, h1_cores, grad_cores, n)
+    a_keep, rest_line = together(a_keep, rest_line)
+    grad_rest = scatter_groups(rest_line, lines(n)).astype(F32)
     first_a, first_b = reduce_first(a_send, b_send, n)
     grad_x, d_gain_attn, d_shift_attn = input_grad(
         place, own_grads, qkv_pieces, x, row(gain_attn), dmid, a_keep, n

time: 540 us -> 521 us (0.965)
  Pallas kernels: 168 us -> 142 us
  waiting for transfers between devices: 165 us -> 176 us
  starting transfers between devices: 50.1 us -> 39.2 us
  blocking collectives: 113 us -> 119 us
    pallas_call x1, Pallas kernels: 38 us -> 19.2 us  [attend(): pl.pallas_call(kernel, in_specs=[SMEM, SMEM, WHOLE], out_specs=[WHOLE, WH...]
    all_gather x1, waiting for transfers between devices: 0.02 us -> 12.3 us  [gather_line(): return lax.all_gather(shard, 'seq', axis_index_groups=lines(n))]
    ppermute x32, waiting for transfers between devices: 84.4 us -> 96.5 us  [swap_with(): return lax.ppermute(value, axis, [(i, i ^ k) for i in range(size)])]
    all_gather x1, waiting for transfers between devices: 18.2 us -> 7.46 us  [gather_plane(): plane = lax.all_gather(line, 'seq', axis_index_groups=planes(n))]
    all_to_all x2, starting transfers between devices: 23.2 us -> 12.6 us  [swap(): return lax.all_to_all(value, 'seq', split_axis=0, concat_axis=0, tiled=True)]
    pallas_call x1, Pallas kernels: 41.1 us -> 33.4 us  [attend_back(): pl.pallas_call(kernel, in_specs=[SMEM, SMEM, WHOLE, WHOLE, WHOLE], out_sp...]
    all_to_all x2, blocking collectives: 113 us -> 119 us  [swap(): return lax.all_to_all(value, 'seq', split_axis=0, concat_axis=0, tiled=True)]
  transfers between devices with their start and end apart: 38 -> 38, of which waited for: 21 -> 23; matrix products, arithmetic and copies ran while one was open for 3% -> 3% of each run, Pallas kernels for 25% -> 20%
where the time goes in v4:
time: 521 us; the launch traced here: 519 us
  waiting for transfers between devices  176 us (34%)
  Pallas kernels  142 us (27%)
  blocking collectives  119 us (23%)
  starting transfers between devices  39.2 us (8%)
  local copies, waits for them, and re-layouts  22.1 us (4%)
  between operations  14.3 us (3%)
  other arithmetic  6.35 us (1%)
    all_to_all x2, blocking collectives, swap(): return lax.all_to_all(value, 'seq', split_axis=0, concat_axis=0, tiled=True)  119 us
    ppermute x32, waiting for transfers between devices, swap_with(): return lax.ppermute(value, axis, [(i, i ^ k) for i in range(size)])  96.5 us
    all_to_all x2, waiting for transfers between devices, swap(): return lax.all_to_all(value, 'seq', split_axis=0, concat_axis=0, tiled=True)  59.6 us
    pallas_call x1, Pallas kernels, middle(): pl.pallas_call(kernel, grid_spec=pltpu.PrefetchScalarGridSpec(num_scalar_...  36.4 us
    pallas_call x1, Pallas kernels, attend_back(): pl.pallas_call(kernel, in_specs=[SMEM, SMEM, WHOLE, WHOLE, WHOLE], out_sp...  33.4 us
    ppermute x32, starting transfers between devices, swap_with(): return lax.ppermute(value, axis, [(i, i ^ k) for i in range(size)])  26.5 us
    pallas_call x1, Pallas kernels, attend(): pl.pallas_call(kernel, in_specs=[SMEM, SMEM, WHOLE], out_specs=[WHOLE, WH...  19.2 us
    pallas_call x1, Pallas kernels, ffn_grads(): pl.pallas_call(functools.partial(ffn_grads_kernel, nb=nb), grid=(4,), in_...  17.9 us
  transfers between devices with their start and end apart: 38, of which 23 were waited for; matrix products, arithmetic and copies ran while one was open for 3% of the time, Pallas kernels for 20%

profile of v4, /device:TPU:0, one launch (start us, length us, event | category | flops | bytes accessed | tf_op | source)
XLA Modules:
  0.0 518.7 jit_solution(18022054759382659056)
XLA Ops:
  8.4 3.1 collective-permute-start
  11.5 2.6 collective-permute-start.1
  16.8 3.1 collective-permute-done
  19.8 8.8 %collective-permute-done.1 = bf16[2,3,32,512]{3,2,1,0:T(8,128)(2,1)S(1)} collective-permute-done((bf16[2,3,32,512]{3,2,1,0:T(8,128)(2,1)S(1)}, bf16[2,3,32,512]{3,2,1,0:T(8,128)(2,1)S(1)}, u32[]{:S(2)}, u32[]{:S(2)}) %collective-permute-start.1) | collective-permute-done | bytes 196640 | tf_op jit(solution)/shard_map/ppermute | solution.py:802
  32.0 5.3 %collective-permute-done.5 = bf16[4,3,32,512]{3,2,1,0:T(8,128)(2,1)S(1)} collective-permute-done((bf16[4,3,32,512]{3,2,1,0:T(8,128)(2,1)S(1)}, bf16[4,3,32,512]{3,2,1,0:T(8,128)(2,1)S(1)}, u32[]{:S(2)}, u32[]{:S(2)}) %collective-permute-start.5) | collective-permute-done | bytes 393248 | tf_op jit(solution)/shard_map/ppermute | solution.py:802
  41.5 13.9 %collective-permute-done.6.refs_3_.refs_5_ = bf16[8,3,32,512]{3,2,1,0:T(8,128)(2,1)S(1)} collective-permute-done((bf16[8,3,32,512]{3,2,1,0:T(8,128)(2,1)S(1)}, bf16[8,3,32,512]{3,2,1,0:T(8,128)(2,1)S(1)}, u32[]{:S(2)}, u32[]{:S(2)}) %collective-permute-start.6) | collective-permute-done | bytes 786464 | tf_op jit(solution)/shard_map/ppermute | solution.py:802
  59.2 10.0 %project.1 = (bf16[2,8,3,256,128]{4,3,2,1,0:T(8,128)(2,1)}, bf16[512,1024]{1,0:T(8,128)(2,1)}) custom-call(s32[34]{0:T(128)} %pad_add_fusion.place_ref, bf16[512,1024]{1,0:T(8,128)(2,1)} %bitcast.97, f32[1,1024]{1,0:T(1,128)} %bitcast.117, f32[1,1024]{1,0:T(1,128)} %bitcast.127, bf16[8,3,32,512]{3,2,1,0:T(8,128)(2,1)} %copy-done.5, ...), custom_call_target="tpu_custom_call" | custom-call | flops 3221225472 | bytes 14680064 | tf_op jit(solution)/shard_map/project/pallas_call | solution.py:113
  69.2 12.3 %all-gather.5.cloned.1.call-done = bf16[2304,512]{1,0:T(8,128)(2,1)} async-done(((bf16[576,512]{1,0:T(8,128)(2,1)}), bf16[2304,512]{1,0:T(8,128)(2,1)}) %all-gather.5.cloned.1.call-update) | async-done | bytes 2359312 | tf_op jit(solution)/shard_map/all_gather | solution.py:823
  81.5 4.4 all-to-all-start
  87.5 59.6 %all-to-all-done = bf16[16,3,256,128]{3,2,1,0:T(8,128)(2,1)S(1)} async-done(((bf16[16,3,256,128]{3,2,1,0:T(8,128)(2,1)}), bf16[16,3,256,128]{3,2,1,0:T(8,128)(2,1)S(1)}, u32[]{:S(2)}, u32[]{:S(2)}) %all-to-all-start) | async-done | bytes 3145760 | tf_op jit(solution)/shard_map/all_to_all | solution.py:970
  148.9 19.2 %attend.1 = (bf16[16,4,64,128]{3,2,1,0:T(8,128)(2,1)}, f32[64,128]{1,0:T(8,128)}) custom-call(s32[384]{0:T(512)} %reshape.131.table_ref, s32[1]{0:T(128)} %bitcast.2.limit_ref, bf16[16,3,4,64,128]{4,3,2,1,0:T(8,128)(2,1)} %bitcast.87), custom_call_target="tpu_custom_call" | custom-call | flops 40000000000 | bytes 4000000 | tf_op jit(solution)/shard_map/attend/pallas_call | solution.py:281
  168.1 40.7 %all_to_all.20 = bf16[16,256,128]{2,1,0:T(8,128)(2,1)} all-to-all(bf16[16,256,128]{2,1,0:T(8,128)(2,1)} %bitcast.102), channel_id=1, replica_groups=mesh['batch'=2,'seq'=16] {'seq'}, dimensions={0} | all-to-all | bytes 2097152 | tf_op jit(solution)/shard_map/all_to_all | solution.py:970
  208.8 7.5 %all-gather.7.cloned.1.call-done.refs_0_ = bf16[16,576,512]{2,1,0:T(8,128)(2,1)} async-done(((bf16[4,576,512]{2,1,0:T(8,128)(2,1)}), bf16[16,576,512]{2,1,0:T(8,128)(2,1)}) %all-gather.7.cloned.1.call-update) | async-done | bytes 9437200 | tf_op jit(solution)/shard_map/all_gather | solution.py:827
  216.2 15.0 %collective-permute-done.11.refs_1_ = bf16[16,576,512]{2,1,0:T(8,128)(2,1)} collective-permute-done((bf16[16,576,512]{2,1,0:T(8,128)(2,1)}, bf16[16,576,512]{2,1,0:T(8,128)(2,1)}, u32[]{:S(2)}, u32[]{:S(2)}) %collective-permute-start.11) | collective-permute-done | bytes 9437216 | tf_op jit(solution)/shard_map/ppermute | solution.py:802
  231.2 36.4 %middle.1 = (bf16[512,1024]{1,0:T(8,128)(2,1)}, f32[512,1024]{1,0:T(8,128)}, bf16[512,1024]{1,0:T(8,128)(2,1)}, bf16[2,8,256,128]{3,2,1,0:T(8,128)(2,1)}, bf16[5...) custom-call(s32[34]{0:T(128)} %pad_add_fusion.place_ref, ...), custom_call_target="tpu_custom_call" | custom-call | flops 19327352832 | bytes 50000000 | tf_op jit(solution)/shard_map/middle/pallas_call | solution.py:557
  270.0 8.1 %all-to-all-start.2 = ((bf16[16,256,128]{2,1,0:T(8,128)(2,1)}), bf16[16,256,128]{2,1,0:T(8,128)(2,1)S(1)}, u32[]{:S(2)}, u32[]{:S(2)}) async-start(bf16[16,256,128]{2,1,0:T(8,128)(2,1)} %bitcast.31), calls=%async_computation.2 | async-start | bytes 2097152 | tf_op jit(solution)/shard_map/all_to_all | solution.py:970
  278.2 2.2 constant_dynamic-slice_fusion.2
  283.2 2.9 collective-permute-done.17.refs_11_
  287.6 17.9 %ffn_grads.1 = bf16[4,4,576,512]{3,2,1,0:T(8,128)(2,1)} custom-call(bf16[512,4096]{1,0:T(8,128)(2,1)} %get-tuple-element.67.refs_0_, bf16[512,4096]{1,0:T(8,128)(2,1)} %collective-permute-done.12.refs_1_, bf16[512,512]{1,0:T(8,128)(2,1)} %get-tuple-element.142.refs_2_, bf16[512,512]{1,0:T(8,128)(2,1)} %copy-done.25, ...), custom_call_target="tpu_custom_call" | custom-call | flops 9663676416 | bytes 40000000 | tf_op jit(solution)/shard_map/ffn_grads/pallas_call | solution.py:657
  306.4 33.4 %attend_back.1 = bf16[16,3,4,64,128]{4,3,2,1,0:T(8,128)(2,1)} custom-call(s32[384]{0:T(512)} %reshape.131.table_ref, s32[1]{0:T(128)} %bitcast.2.limit_ref, bf16[16,3,4,64,128]{4,3,2,1,0:T(8,128)(2,1)} %bitcast.88, bf16[16,4,64,128]{3,2,1,0:T(8,128)(2,1)} %bitcast.100, f32[64,128]{1,0:T(8,128)} %get-tuple-element.73.lse_ref), custom_call_target="tpu_custom_call" | custom-call | flops 80000000000 | bytes 8000000 | tf_op jit(solution)/shard_map/attend_back/pallas_call | solution.py:384
  339.8 78.6 %all_to_all.21 = bf16[16,3,256,128]{3,2,1,0:T(8,128)(2,1)} all-to-all(bf16[16,3,256,128]{3,2,1,0:T(8,128)(2,1)} %bitcast.90), channel_id=1, replica_groups=mesh['batch'=2,'seq'=16] {'seq'}, dimensions={0} | all-to-all | bytes 6291456 | tf_op jit(solution)/shard_map/all_to_all | solution.py:970
  418.3 4.4 split_by_core.1
  423.3 4.0 collective-permute-done.18.refs_1_
  429.0 7.7 %qkv_grad.1 = (bf16[8,3,32,512]{3,2,1,0:T(8,128)(2,1)}, bf16[8,3,32,512]{3,2,1,0:T(8,128)(2,1)}, bf16[8,3,32,512]{3,2,1,0:T(8,128)(2,1)}, bf16[8,3,32,512]{3,2,1,0:T(8,128)(2,1)}) custom-call(s32[34]{0:T(128)} %pad_add_fusion.place_ref, bf16[512,1024]{1,0:T(8,128)(2,1)} %get-tuple-element.76.refs_0_, bf16[512,1024]{1,0:T(8,128)(2,1)} %copy-done.22, ...), custom_call_target="tpu_custom_call" | custom-call | flops 3221225472 | bytes 15000000 | tf_op jit(solution)/shard_map/qkv_grad/pallas_call | solution.py:732
  439.5 12.8 %input_grad.1 = (f32[512,1024]{1,0:T(8,128)}, f32[1,1024]{1,0:T(1,128)}, f32[1,1024]{1,0:T(1,128)}) custom-call(s32[34]{0:T(128)} %pad_add_fusion.place_ref, bf16[512,1024]{1,0:T(8,128)(2,1)} %bitcast.99, f32[1,1024]{1,0:T(1,128)} %bitcast.118, f32[512,1024]{1,0:T(8,128)} %get-tuple-element.65.dmid_ref, bf16[512,1536]{1,0:T(8,128)(2,1)} %get-tuple-element.74.refs_2_.refs_0_, ...), custom_call_target="tpu_custom_call" | custom-call | flops 3221225472 | bytes 20000000 | tf_op jit(solution)/shard_map/input_grad/pallas_call | solution.py:785
  453.7 3.8 collective-permute-done.20
  464.2 4.5 collective-permute-done.25
  469.6 8.6 %collective-permute-done.26 = f32[1,10240]{1,0:T(1,128)S(1)} collective-permute-done((f32[1,10240]{1,0:T(1,128)S(1)}, f32[1,10240]{1,0:T(1,128)S(1)}, u32[]{:S(2)}, u32[]{:S(2)}) %collective-permute-start.26) | collective-permute-done | bytes 40992 | tf_op jit(solution)/shard_map/ppermute | solution.py:802
  481.4 2.6 collective-permute-done.30
  485.9 2.5 collective-permute-start.28
  491.5 6.6 %collective-permute-done.27 = bf16[2,3,32,512]{3,1,2,0:T(4,128)(2,1)S(1)} collective-permute-done((bf16[2,3,32,512]{3,1,2,0:T(4,128)(2,1)S(1)}, bf16[2,3,32,512]{3,1,2,0:T(4,128)(2,1)S(1)}, u32[]{:S(2)}, u32[]{:S(2)}) %collective-permute-start.27) | collective-permute-done | bytes 196640 | tf_op jit(solution)/shard_map/ppermute | solution.py:802
  498.1 9.2 %collective-permute-done.28 = bf16[2,3,32,512]{3,1,2,0:T(4,128)(2,1)S(1)} collective-permute-done((bf16[2,3,32,512]{3,1,2,0:T(4,128)(2,1)S(1)}, bf16[2,3,32,512]{3,1,2,0:T(4,128)(2,1)S(1)}, u32[]{:S(2)}, u32[]{:S(2)}) %collective-permute-start.28) | collective-permute-done | bytes 196640 | tf_op jit(solution)/shard_map/ppermute | solution.py:802
  (164 shorter events, 52.9 us)
Async XLA Ops:
  7.2 74.3 %all-gather.5.cloned.1.call-start = ((), (), s32[]{:S(2)}) async-start(), calls=%async_computation.7 | async-start | bytes 2949120 | tf_op jit(solution)/shard_map/all_gather | solution.py:823
  8.4 11.4 %collective-permute-start = (bf16[2,3,32,512]{3,2,1,0:T(8,128)(2,1)S(1)}, bf16[2,3,32,512]{3,2,1,0:T(8,128)(2,1)S(1)}, u32[]{:S(2)}, u32[]{:S(2)}) collective-permute-start(bf16[2,3,32,512]{3,2,1,0:T(8,128)(2,1)S(1)} %bitcast.106), channel_id=1, source_target_pairs={{0,4},{1,5},{2,6},{3,7},{4,0},{5,1},{6,2},{7,3},{8,12},{9,13},{10,... | collective-permute-start | bytes 589832 | tf_op jit(solution)/shard_map/ppermute | solution.py:802
  11.5 17.2 %collective-permute-start.1 = (bf16[2,3,32,512]{3,2,1,0:T(8,128)(2,1)S(1)}, bf16[2,3,32,512]{3,2,1,0:T(8,128)(2,1)S(1)}, u32[]{:S(2)}, u32[]{:S(2)}) collective-permute-start(bf16[2,3,32,512]{3,2,1,0:T(8,128)(2,1)S(1)} %bitcast.107), channel_id=1, source_target_pairs={{0,8},{1,9},{2,10},{3,11},{4,12},{5,13},{6,14},{7,15},{8,0},{9,1},... | collective-permute-start | bytes 589832 | tf_op jit(solution)/shard_map/ppermute | solution.py:802
  14.1 14.6 %collective-permute-start.2 = (bf16[2,3,32,512]{3,2,1,0:T(8,128)(2,1)S(1)}, bf16[2,3,32,512]{3,2,1,0:T(8,128)(2,1)S(1)}, u32[]{:S(2)}, u32[]{:S(2)}) collective-permute-start(bf16[2,3,32,512]{3,2,1,0:T(8,128)(2,1)S(1)} %bitcast.108), channel_id=1, source_target_pairs={{0,12},{1,13},{2,14},{3,15},{4,8},{5,9},{6,10},{7,11},{8,4},{9,5},... | collective-permute-start | bytes 589832 | tf_op jit(solution)/shard_map/ppermute | solution.py:802
  28.8 187.4 %all-gather.7.cloned.1.call-start = ((), (), s32[]{:S(2)}) async-start(), calls=%async_computation.8 | async-start | bytes 11796480 | tf_op jit(solution)/shard_map/all_gather | solution.py:827
  28.9 8.5 %collective-permute-start.5 = (bf16[4,3,32,512]{3,2,1,0:T(8,128)(2,1)S(1)}, bf16[4,3,32,512]{3,2,1,0:T(8,128)(2,1)S(1)}, u32[]{:S(2)}, u32[]{:S(2)}) collective-permute-start(bf16[4,3,32,512]{3,2,1,0:T(8,128)(2,1)S(1)} %get-tuple-element.56), channel_id=1, source_target_pairs={{0,2},{1,3},{2,0},{3,1},{4,6},{5,7},{6,4},{7,5},{8,10},{9,11},{10,... | collective-permute-start | bytes 1179656 | tf_op jit(solution)/shard_map/ppermute | solution.py:802
  30.5 10.1 %collective-permute-start.3 = (bf16[4,3,32,512]{3,2,1,0:T(8,128)(2,1)S(1)}, bf16[4,3,32,512]{3,2,1,0:T(8,128)(2,1)S(1)}, u32[]{:S(2)}, u32[]{:S(2)}) collective-permute-start(bf16[4,3,32,512]{3,2,1,0:T(8,128)(2,1)S(1)} %get-tuple-element.55), channel_id=1, source_target_pairs={{0,1},{1,0},{2,3},{3,2},{4,5},{5,4},{6,7},{7,6},{8,9},{9,8},{10,11... | collective-permute-start | bytes 1179656 | tf_op jit(solution)/shard_map/ppermute | solution.py:802
  37.4 18.1 %collective-permute-start.6 = (bf16[8,3,32,512]{3,2,1,0:T(8,128)(2,1)S(1)}, bf16[8,3,32,512]{3,2,1,0:T(8,128)(2,1)S(1)}, u32[]{:S(2)}, u32[]{:S(2)}) collective-permute-start(bf16[8,3,32,512]{3,2,1,0:T(8,128)(2,1)S(1)} %constant_dynamic-update-slice_fusion.2.refs_2_.refs_4_), channel_id=1, source_target_pairs={{0,1},{1,0},{2,3},{3,2},{4,5},{5,4},{6,7},{7,6},{8,9},{9,8},{10,11... | collective-permute-start | bytes 2359304 | tf_op jit(solution)/shard_map/ppermute | solution.py:802
  40.7 14.8 %collective-permute-start.4 = (bf16[8,3,32,512]{3,2,1,0:T(8,128)(2,1)S(1)}, bf16[8,3,32,512]{3,2,1,0:T(8,128)(2,1)}, u32[]{:S(2)}, u32[]{:S(2)}) collective-permute-start(bf16[8,3,32,512]{3,2,1,0:T(8,128)(2,1)S(1)} %constant_dynamic-update-slice_fusion.refs_0_.refs_2_), channel_id=1, source_target_pairs={{0,2},{1,3},{2,0},{3,1},{4,6},{5,7},{6,4},{7,5},{8,10},{9,11},{10,... | collective-permute-start | bytes 2359304 | tf_op jit(solution)/shard_map/ppermute | solution.py:802
  41.0 15.6 %collective-permute-start.9 = (bf16[8,3,32,512]{3,2,1,0:T(8,128)(2,1)S(1)}, bf16[8,3,32,512]{3,2,1,0:T(8,128)(2,1)}, u32[]{:S(2)}, u32[]{:S(2)}) collective-permute-start(bf16[8,3,32,512]{3,2,1,0:T(8,128)(2,1)S(1)} %constant_dynamic-update-slice_fusion.2.refs_2_.refs_4_), channel_id=1, source_target_pairs={{0,16},{16,0},{1,17},{17,1},{2,18},{18,2},{3,19},{19,3},{4,20},{20... | collective-permute-start | bytes 2359304 | tf_op jit(solution)/shard_map/ppermute | solution.py:802
  41.0 15.6 %collective-permute-start.7 = (bf16[8,3,32,512]{3,2,1,0:T(8,128)(2,1)S(1)}, bf16[8,3,32,512]{3,2,1,0:T(8,128)(2,1)}, u32[]{:S(2)}, u32[]{:S(2)}) collective-permute-start(bf16[8,3,32,512]{3,2,1,0:T(8,128)(2,1)S(1)} %constant_dynamic-update-slice_fusion.refs_0_.refs_2_), channel_id=1, source_target_pairs={{0,16},{16,0},{1,17},{17,1},{2,18},{18,2},{3,19},{19,3},{4,20},{20... | collective-permute-start | bytes 2359304 | tf_op jit(solution)/shard_map/ppermute | solution.py:802
  81.5 65.6 %all-to-all-start = ((bf16[16,3,256,128]{3,2,1,0:T(8,128)(2,1)}), bf16[16,3,256,128]{3,2,1,0:T(8,128)(2,1)S(1)}, u32[]{:S(2)}, u32[]{:S(2)}) async-start(bf16[16,3,256,128]{3,2,1,0:T(8,128)(2,1)} %bitcast.89), calls=%async_computation | async-start | bytes 6291456 | tf_op jit(solution)/shard_map/all_to_all | solution.py:970
  216.2 15.0 %collective-permute-start.11 = (bf16[16,576,512]{2,1,0:T(8,128)(2,1)}, bf16[16,576,512]{2,1,0:T(8,128)(2,1)}, u32[]{:S(2)}, u32[]{:S(2)}) collective-permute-start(bf16[16,576,512]{2,1,0:T(8,128)(2,1)} %all-gather.7.cloned.1.call-done.refs_0_), channel_id=1, source_target_pairs={{0,16},{16,0},{1,17},{17,1},{2,18},{18,2},{3,19},{19,3},{4,20},{20... | collective-permute-start | bytes 28311560 | tf_op jit(solution)/shard_map/ppermute | solution.py:802
  267.6 18.5 %collective-permute-start.12 = (bf16[512,4096]{1,0:T(8,128)(2,1)}, bf16[512,4096]{1,0:T(8,128)(2,1)}, u32[]{:S(2)}, u32[]{:S(2)}) collective-permute-start(bf16[512,4096]{1,0:T(8,128)(2,1)} %get-tuple-element.67.refs_0_), channel_id=1, source_target_pairs={{0,16},{16,0},{1,17},{17,1},{2,18},{18,2},{3,19},{19,3},{4,20},{20... | collective-permute-start | bytes 12582920 | tf_op jit(solution)/shard_map/ppermute | solution.py:802
  269.5 16.5 %collective-permute-start.15 = (bf16[1,512,2048]{2,1,0:T(8,128)(2,1)S(1)}, bf16[1,512,2048]{2,1,0:T(8,128)(2,1)}, u32[]{:S(2)}, u32[]{:S(2)}) collective-permute-start(bf16[1,512,2048]{2,1,0:T(8,128)(2,1)S(1)} %slice.61), channel_id=1, source_target_pairs={{0,16},{16,0},{1,17},{17,1},{2,18},{18,2},{3,19},{19,3},{4,20},{20... | collective-permute-start | bytes 6291464 | tf_op jit(solution)/shard_map/ppermute | solution.py:802
  270.0 35.5 %all-to-all-start.2 = ((bf16[16,256,128]{2,1,0:T(8,128)(2,1)}), bf16[16,256,128]{2,1,0:T(8,128)(2,1)S(1)}, u32[]{:S(2)}, u32[]{:S(2)}) async-start(bf16[16,256,128]{2,1,0:T(8,128)(2,1)} %bitcast.31), calls=%async_computation.2 | async-start | bytes 2097152 | tf_op jit(solution)/shard_map/all_to_all | solution.py:970
  278.1 158.6 %reduce-scatter.7.cloned.1.call-start = ((), (), s32[]{:S(2)}) async-start(), calls=%async_computation.9 | async-start | bytes 11796480
  280.4 5.7 %collective-permute-start.14 = (bf16[512,1024]{1,0:T(8,128)(2,1)}, bf16[512,1024]{1,0:T(8,128)(2,1)S(1)}, u32[]{:S(2)}, u32[]{:S(2)}) collective-permute-start(bf16[512,1024]{1,0:T(8,128)(2,1)} %get-tuple-element.68.refs_4_), channel_id=1, source_target_pairs={{0,16},{16,0},{1,17},{17,1},{2,18},{18,2},{3,19},{19,3},{4,20},{20... | collective-permute-start | bytes 3145736 | tf_op jit(solution)/shard_map/ppermute | solution.py:802
  280.9 5.2 collective-permute-start.16
  306.4 202.1 %reduce-scatter.5.cloned.1.call-start = ((), (), s32[]{:S(2)}) async-start(), calls=%async_computation.6 | async-start | bytes 2949120 | tf_op jit(solution)/shard_map/reduce_scatter | solution.py:832
  422.7 5.1 collective-permute-start.19
  422.7 4.5 collective-permute-start.18
  437.8 19.6 %collective-permute-start.20 = (bf16[8,3,32,512]{3,2,1,0:T(8,128)(2,1)S(1)}, bf16[8,3,32,512]{3,2,1,0:T(8,128)(2,1)S(1)}, u32[]{:S(2)}, u32[]{:S(2)}) collective-permute-start(bf16[8,3,32,512]{3,2,1,0:T(8,128)(2,1)S(1)} %copy-done.24), channel_id=1, source_target_pairs={{0,2},{1,3},{2,0},{3,1},{4,6},{5,7},{6,4},{7,5},{8,10},{9,11},{10,... | collective-permute-start | bytes 2359304 | tf_op jit(solution)/shard_map/ppermute | solution.py:802
  438.9 19.3 %collective-permute-start.21 = (bf16[8,3,32,512]{3,2,1,0:T(8,128)(2,1)S(1)}, bf16[8,3,32,512]{3,2,1,0:T(8,128)(2,1)S(1)}, u32[]{:S(2)}, u32[]{:S(2)}) collective-permute-start(bf16[8,3,32,512]{3,2,1,0:T(8,128)(2,1)S(1)} %copy-done.23), channel_id=1, source_target_pairs={{0,1},{1,0},{2,3},{3,2},{4,5},{5,4},{6,7},{7,6},{8,9},{9,8},{10,11... | collective-permute-start | bytes 2359304 | tf_op jit(solution)/shard_map/ppermute | solution.py:802
  458.9 19.3 %collective-permute-start.22 = (bf16[4,1,3,32,512]{4,2,3,1,0:T(4,128)(2,1)S(1)}, bf16[4,1,3,32,512]{4,2,3,1,0:T(4,128)(2,1)S(1)}, u32[]{:S(2)}, u32[]{:S(2)}) collective-permute-start(bf16[4,1,3,32,512]{4,2,3,1,0:T(4,128)(2,1)S(1)} %copy.63), channel_id=1, source_target_pairs={{0,1},{1,0},{2,3},{3,2},{4,5},{5,4},{6,7},{7,6},{8,9},{9,8},{10,11... | collective-permute-start | bytes 1179656 | tf_op jit(solution)/shard_map/ppermute | solution.py:802
  460.4 18.4 %collective-permute-start.23 = (bf16[4,1,3,32,512]{4,2,3,1,0:T(4,128)(2,1)S(1)}, bf16[4,1,3,32,512]{4,2,3,1,0:T(4,128)(2,1)S(1)}, u32[]{:S(2)}, u32[]{:S(2)}) collective-permute-start(bf16[4,1,3,32,512]{4,2,3,1,0:T(4,128)(2,1)S(1)} %copy.65), channel_id=1, source_target_pairs={{0,2},{1,3},{2,0},{3,1},{4,6},{5,7},{6,4},{7,5},{8,10},{9,11},{10,... | collective-permute-start | bytes 1179656 | tf_op jit(solution)/shard_map/ppermute | solution.py:802
  462.7 6.1 %collective-permute-start.25 = (f32[1,10240]{1,0:T(1,128)S(1)}, f32[1,10240]{1,0:T(1,128)S(1)}, u32[]{:S(2)}, u32[]{:S(2)}) collective-permute-start(f32[1,10240]{1,0:T(1,128)S(1)} %add.86), channel_id=1, source_target_pairs={{0,4},{1,5},{2,6},{3,7},{4,0},{5,1},{6,2},{7,3},{8,12},{9,13},{10,... | collective-permute-start | bytes 122888 | tf_op jit(solution)/shard_map/ppermute | solution.py:802
  468.8 9.5 %collective-permute-start.26 = (f32[1,10240]{1,0:T(1,128)S(1)}, f32[1,10240]{1,0:T(1,128)S(1)}, u32[]{:S(2)}, u32[]{:S(2)}) collective-permute-start(f32[1,10240]{1,0:T(1,128)S(1)} %add.87), channel_id=1, source_target_pairs={{0,8},{1,9},{2,10},{3,11},{4,12},{5,13},{6,14},{7,15},{8,0},{9,1},... | collective-permute-start | bytes 122888 | tf_op jit(solution)/shard_map/ppermute | solution.py:802
  484.1 6.2 %collective-permute-start.31 = (f32[1,10240]{1,0:T(1,128)S(1)}, f32[1,10240]{1,0:T(1,128)S(1)}, u32[]{:S(2)}, u32[]{:S(2)}) collective-permute-start(f32[1,10240]{1,0:T(1,128)S(1)} %add.92), channel_id=1, source_target_pairs={{0,2},{1,3},{2,0},{3,1},{4,6},{5,7},{6,4},{7,5},{8,10},{9,11},{10,... | collective-permute-start | bytes 122888 | tf_op jit(solution)/shard_map/ppermute | solution.py:802
  485.8 12.3 %collective-permute-start.27 = (bf16[2,3,32,512]{3,1,2,0:T(4,128)(2,1)S(1)}, bf16[2,3,32,512]{3,1,2,0:T(4,128)(2,1)S(1)}, u32[]{:S(2)}, u32[]{:S(2)}) collective-permute-start(bf16[2,3,32,512]{3,1,2,0:T(4,128)(2,1)S(1)} %get-tuple-element.136), channel_id=1, source_target_pairs={{0,4},{1,5},{2,6},{3,7},{4,0},{5,1},{6,2},{7,3},{8,12},{9,13},{10,... | collective-permute-start | bytes 589832 | tf_op jit(solution)/shard_map/ppermute | solution.py:802
  485.9 21.4 %collective-permute-start.28 = (bf16[2,3,32,512]{3,1,2,0:T(4,128)(2,1)S(1)}, bf16[2,3,32,512]{3,1,2,0:T(4,128)(2,1)S(1)}, u32[]{:S(2)}, u32[]{:S(2)}) collective-permute-start(bf16[2,3,32,512]{3,1,2,0:T(4,128)(2,1)S(1)} %get-tuple-element.138), channel_id=1, source_target_pairs={{0,8},{1,9},{2,10},{3,11},{4,12},{5,13},{6,14},{7,15},{8,0},{9,1},... | collective-permute-start | bytes 589832 | tf_op jit(solution)/shard_map/ppermute | solution.py:802
  488.4 18.9 %collective-permute-start.29 = (bf16[2,3,32,512]{3,1,2,0:T(4,128)(2,1)S(1)}, bf16[2,3,32,512]{3,1,2,0:T(4,128)(2,1)S(1)}, u32[]{:S(2)}, u32[]{:S(2)}) collective-permute-start(bf16[2,3,32,512]{3,1,2,0:T(4,128)(2,1)S(1)} %get-tuple-element.137), channel_id=1, source_target_pairs={{0,12},{1,13},{2,14},{3,15},{4,8},{5,9},{6,10},{7,11},{8,4},{9,5},... | collective-permute-start | bytes 589832 | tf_op jit(solution)/shard_map/ppermute | solution.py:802
  (34 other events, 237.4 us)
Sparse Core Ops, SparseCore 0:
  29.0 52.4 all-gather.4
  83.3 132.8 all-gather.6
  305.6 128.3 reduce-scatter.6
  436.9 48.8 reduce-scatter.4

commit v5 on v4

--- a/solution.py
+++ b/solution.py
@@ -70,6 +70,10 @@
         copies.append(pltpu.make_async_copy(ref, target, sems.at[i]))
     for copy in copies:
         copy.start()
+    return copies
+
+
+def finish(copies):
     for copy in copies:
         copy.wait()
 
@@ -94,9 +98,10 @@
 
     @pl.when(pl.program_id(0) == 0)
     def _():
+        copies = load_pieces(pieces, wa_ref, wb_ref, sems)
         xhat, _ = norm_stats(x_ref[...].astype(F32))
         h_ref[...] = (xhat * gain_ref[...] + shift_ref[...]).astype(BF)
-        load_pieces(pieces, wa_ref, wb_ref, sems)
+        finish(copies)
 
     core = (pl.program_id(0) // 3) ^ place_ref[2 * wa_ref.shape[1]]
     y = nn(h_ref[...], qkv_block(core, pl.program_id(0) % 3, place_ref, wa_ref, wb_ref)).astype(BF)
@@ -672,26 +677,25 @@
     )(*act, *gc, *h, *gp, *att, *br)
 
 
-def split_kernel(place_ref, grad_ref, *out_refs, n, local, lanes):
-    micros, groups = grad_ref.shape[:2]
+def split_kernel(place_ref, grad_ref, *out_refs, n, lanes):
+    groups = grad_ref.shape[1]
     core = place_ref[2 * n]
     count = out_refs[0].shape[1] // lanes
     for k, out_ref in enumerate(out_refs):
-        for m in range(micros):
-            for i in range(count):
-                at = (core ^ k) * count + i
-                block = grad_ref[m, at % groups, at // groups]
-                out_ref[m * local : (m + 1) * local, i * lanes : (i + 1) * lanes] = block
+        for i in range(count):
+            at = (core ^ k) * count + i
+            out_ref[:, i * lanes : (i + 1) * lanes] = grad_ref[0, at % groups, at // groups]
 
 
 def split_by_core(place, grad, nb, n):
     micros, groups, _, local, lanes = grad.shape
-    shape = jax.ShapeDtypeStruct((micros * local, 3 * groups * lanes // nb), BF)
+    cols = 3 * groups * lanes // nb
     return pl.pallas_call(
-        functools.partial(split_kernel, n=n, local=local, lanes=lanes),
-        in_specs=[SMEM, WHOLE],
-        out_specs=[WHOLE] * nb,
-        out_shape=[shape] * nb,
+        functools.partial(split_kernel, n=n, lanes=lanes),
+        grid=(micros,),
+        in_specs=[SMEM, pl.BlockSpec((1, groups, 3, local, lanes), lambda m: (m, 0, 0, 0, 0))],
+        out_specs=[pl.BlockSpec((local, cols), lambda m: (m, 0))] * nb,
+        out_shape=[jax.ShapeDtypeStruct((micros * local, cols), BF)] * nb,
         compiler_params=params(),
         cost_estimate=cost(1e6, 6e6),
         name="split_by_core",
@@ -751,7 +755,7 @@
 
     @pl.when(step == 0)
     def _():
-        load_pieces(pieces, wa_ref, wb_ref, sems)
+        finish(load_pieces(pieces, wa_ref, wb_ref, sems))
 
     total = None
     for k in range(nb):
@@ -980,6 +984,8 @@
     qkv, rest_line = together(qkv, rest_line)
     rest_plane = gather_plane(rest_line, n)
     qkv_all = swap(qkv.reshape(n, 3, local, lanes)).reshape(n, 3, bpd, BLOCK, lanes)
+    g_cores, h1_cores = columns_over_cores(g, fb), over_cores(h1)
+    qkv_all, g_cores, h1_cores = together(qkv_all, g_cores, h1_cores)
     mixed, lse = attend(qkv_all, table, limit, per)
     o = swap(mixed.reshape(n, local, lanes)).reshape(micros, groups, local, lanes)
     o, rest_plane = together(o, rest_plane)
@@ -1012,12 +1018,11 @@
         row(gain_ffn),
         row(shift_ffn),
     )
-    h1_cores = over_cores(h1)
     dout_all = swap(dout.reshape(n, local, lanes)).reshape(n, bpd, BLOCK, lanes)
 
     rest_grad = ffn_grads(
         over_cores(act),
-        columns_over_cores(g, fb),
+        g_cores,
         over_cores(h2),
         [pre_grad] + [swap_with(pre_grad[k : k + 1], "batch", k) for k in range(1, nb)],
         over_cores(att),
@@ -1041,14 +1046,17 @@
     sums = jnp.concatenate(vectors, axis=1)
     sums, first_a, first_b = together(sums, first_a, first_b)
     qkv_reduced = reduce_rest(plus(a_keep, first_a), plus(b_keep, first_b), n)
-    sums = total_over(total_over(sums, "batch", powers(nb)), "seq", powers(n)[-2:])
+    sums = total_over(total_over(sums, "batch", powers(nb)), "seq", powers(n // 4))
     qkv_reduced, sums = together(qkv_reduced, sums)
-    sums = total_over(sums, "seq", powers(n // 4))[0]
-    grad_a, grad_b = reduce_last(qkv_reduced, reduce_direct(qkv_reduced, n))
-    grad_qkv = jnp.stack([grad_a, grad_b]).transpose(0, 2, 1, 3).reshape(kr, 3 * fb)
     grad_down = grad_rest[:fr]
     grad_up = grad_rest[fr:-kr].reshape(per_b, kr, fb).transpose(1, 0, 2).reshape(kr, per_b * fb)
     grad_out = grad_rest[-kr:]
+    arrived = reduce_direct(qkv_reduced, n)
+    near, far, diagonal = direct(sums, n)
+    *arrived, grad_down, grad_up, grad_out = together(*arrived, grad_down, grad_up, grad_out)
+    grad_a, grad_b = reduce_last(qkv_reduced, arrived)
+    grad_qkv = jnp.stack([grad_a, grad_b]).transpose(0, 2, 1, 3).reshape(kr, 3 * fb)
+    sums = ((sums + near) + (far + diagonal))[0]
     ends = []
     for vector in vectors[:-1]:
         ends.append((ends[-1] if ends else 0) + vector.shape[1])

time: 521 us -> 515 us (0.988)
  waiting for transfers between devices: 176 us -> 170 us
    ppermute x32 -> x33, starting transfers between devices: 26.5 us -> 29.9 us  [swap_with(): return lax.ppermute(value, axis, [(i, i ^ k) for i in range(size)])]
    ppermute x32 -> x33, waiting for transfers between devices: 96.5 us -> 96.4 us  [swap_with(): return lax.ppermute(value, axis, [(i, i ^ k) for i in range(size)])]
  transfers between devices with their start and end apart: 38 -> 39, of which waited for: 23 -> 25; matrix products, arithmetic and copies ran while one was open for 3% -> 4% of each run, Pallas kernels for 20% -> 20%
where the time goes in v5:
time: 515 us; the launch traced here: 514 us
  waiting for transfers between devices  170 us (33%)
  Pallas kernels  141 us (27%)
  blocking collectives  119 us (23%)
  starting transfers between devices  42.6 us (8%)
  local copies, waits for them, and re-layouts  23.2 us (5%)
  between operations  14.2 us (3%)
  other arithmetic  5.15 us (1%)
    all_to_all x2, blocking collectives, swap(): return lax.all_to_all(value, 'seq', split_axis=0, concat_axis=0, tiled=True)  119 us
    ppermute x33, waiting for transfers between devices, swap_with(): return lax.ppermute(value, axis, [(i, i ^ k) for i in range(size)])  96.4 us
    all_to_all x2, waiting for transfers between devices, swap(): return lax.all_to_all(value, 'seq', split_axis=0, concat_axis=0, tiled=True)  56.7 us
    pallas_call x1, Pallas kernels, middle(): pl.pallas_call(kernel, grid_spec=pltpu.PrefetchScalarGridSpec(num_scalar_...  36.3 us
    pallas_call x1, Pallas kernels, attend_back(): pl.pallas_call(kernel, in_specs=[SMEM, SMEM, WHOLE, WHOLE, WHOLE], out_sp...  33.3 us
    ppermute x33, starting transfers between devices, swap_with(): return lax.ppermute(value, axis, [(i, i ^ k) for i in range(size)])  29.9 us
    pallas_call x1, Pallas kernels, attend(): pl.pallas_call(kernel, in_specs=[SMEM, SMEM, WHOLE], out_specs=[WHOLE, WH...  19.3 us
    pallas_call x1, Pallas kernels, ffn_grads(): pl.pallas_call(functools.partial(ffn_grads_kernel, nb=nb), grid=(4,), in_...  17.8 us
  transfers between devices with their start and end apart: 39, of which 25 were waited for; matrix products, arithmetic and copies ran while one was open for 4% of the time, Pallas kernels for 20%

profile of v5, /device:TPU:0, one launch (start us, length us, event | category | flops | bytes accessed | tf_op | source)
XLA Modules:
  0.0 514.5 jit_solution(6231909204577602846)
XLA Ops:
  8.4 3.1 collective-permute-start
  11.5 2.5 collective-permute-start.2
  16.8 7.2 %collective-permute-done.2 = bf16[2,3,32,512]{3,2,1,0:T(8,128)(2,1)S(1)} collective-permute-done((bf16[2,3,32,512]{3,2,1,0:T(8,128)(2,1)S(1)}, bf16[2,3,32,512]{3,2,1,0:T(8,128)(2,1)S(1)}, u32[]{:S(2)}, u32[]{:S(2)}) %collective-permute-start.2) | collective-permute-done | bytes 196640 | tf_op jit(solution)/shard_map/ppermute | solution.py:806
  24.0 7.3 %collective-permute-done.1 = bf16[2,3,32,512]{3,2,1,0:T(8,128)(2,1)S(1)} collective-permute-done((bf16[2,3,32,512]{3,2,1,0:T(8,128)(2,1)S(1)}, bf16[2,3,32,512]{3,2,1,0:T(8,128)(2,1)S(1)}, u32[]{:S(2)}, u32[]{:S(2)}) %collective-permute-start.1) | collective-permute-done | bytes 196640 | tf_op jit(solution)/shard_map/ppermute | solution.py:806
  34.7 6.9 %collective-permute-done.5 = bf16[4,3,32,512]{3,2,1,0:T(8,128)(2,1)S(1)} collective-permute-done((bf16[4,3,32,512]{3,2,1,0:T(8,128)(2,1)S(1)}, bf16[4,3,32,512]{3,2,1,0:T(8,128)(2,1)S(1)}, u32[]{:S(2)}, u32[]{:S(2)}) %collective-permute-start.5) | collective-permute-done | bytes 393248 | tf_op jit(solution)/shard_map/ppermute | solution.py:806
  45.4 14.4 %collective-permute-done.6.refs_3_.refs_5_ = bf16[8,3,32,512]{3,2,1,0:T(8,128)(2,1)S(1)} collective-permute-done((bf16[8,3,32,512]{3,2,1,0:T(8,128)(2,1)S(1)}, bf16[8,3,32,512]{3,2,1,0:T(8,128)(2,1)S(1)}, u32[]{:S(2)}, u32[]{:S(2)}) %collective-permute-start.6) | collective-permute-done | bytes 786464 | tf_op jit(solution)/shard_map/ppermute | solution.py:806
  63.5 10.0 %project.1 = (bf16[2,8,3,256,128]{4,3,2,1,0:T(8,128)(2,1)}, bf16[512,1024]{1,0:T(8,128)(2,1)}) custom-call(s32[34]{0:T(128)} %pad_add_fusion.place_ref, bf16[512,1024]{1,0:T(8,128)(2,1)} %bitcast.97, f32[1,1024]{1,0:T(1,128)} %bitcast.117, f32[1,1024]{1,0:T(1,128)} %bitcast.127, bf16[8,3,32,512]{3,2,1,0:T(8,128)(2,1)} %copy-done.5, ...), custom_call_target="tpu_custom_call" | custom-call | flops 3221225472 | bytes 14680064 | tf_op jit(solution)/shard_map/project/pallas_call | solution.py:118
  73.5 8.9 %all-gather.5.cloned.1.call-done = bf16[2304,512]{1,0:T(8,128)(2,1)} async-done(((bf16[576,512]{1,0:T(8,128)(2,1)}), bf16[2304,512]{1,0:T(8,128)(2,1)}) %all-gather.5.cloned.1.call-update) | async-done | bytes 2359312 | tf_op jit(solution)/shard_map/all_gather | solution.py:827
  82.5 4.4 all-to-all-start
  87.0 2.2 constant_dynamic-slice_fusion.2
  91.6 56.4 %all-to-all-done = bf16[16,3,256,128]{3,2,1,0:T(8,128)(2,1)S(1)} async-done(((bf16[16,3,256,128]{3,2,1,0:T(8,128)(2,1)}), bf16[16,3,256,128]{3,2,1,0:T(8,128)(2,1)S(1)}, u32[]{:S(2)}, u32[]{:S(2)}) %all-to-all-start) | async-done | bytes 3145760 | tf_op jit(solution)/shard_map/all_to_all | solution.py:974
  149.8 19.3 %attend.1 = (bf16[16,4,64,128]{3,2,1,0:T(8,128)(2,1)}, f32[64,128]{1,0:T(8,128)}) custom-call(s32[384]{0:T(512)} %reshape.131.table_ref, s32[1]{0:T(128)} %bitcast.2.limit_ref, bf16[16,3,4,64,128]{4,3,2,1,0:T(8,128)(2,1)} %bitcast.87), custom_call_target="tpu_custom_call" | custom-call | flops 40000000000 | bytes 4000000 | tf_op jit(solution)/shard_map/attend/pallas_call | solution.py:286
  169.1 40.7 %all_to_all.20 = bf16[16,256,128]{2,1,0:T(8,128)(2,1)} all-to-all(bf16[16,256,128]{2,1,0:T(8,128)(2,1)} %bitcast.102), channel_id=1, replica_groups=mesh['batch'=2,'seq'=16] {'seq'}, dimensions={0} | all-to-all | bytes 2097152 | tf_op jit(solution)/shard_map/all_to_all | solution.py:974
  209.8 7.4 %all-gather.7.cloned.1.call-done.refs_0_ = bf16[16,576,512]{2,1,0:T(8,128)(2,1)} async-done(((bf16[4,576,512]{2,1,0:T(8,128)(2,1)}), bf16[16,576,512]{2,1,0:T(8,128)(2,1)}) %all-gather.7.cloned.1.call-update) | async-done | bytes 9437200 | tf_op jit(solution)/shard_map/all_gather | solution.py:831
  217.2 15.0 %collective-permute-done.13.refs_1_ = bf16[16,576,512]{2,1,0:T(8,128)(2,1)} collective-permute-done((bf16[16,576,512]{2,1,0:T(8,128)(2,1)}, bf16[16,576,512]{2,1,0:T(8,128)(2,1)}, u32[]{:S(2)}, u32[]{:S(2)}) %collective-permute-start.13) | collective-permute-done | bytes 9437216 | tf_op jit(solution)/shard_map/ppermute | solution.py:806
  232.2 36.3 %middle.1 = (bf16[512,1024]{1,0:T(8,128)(2,1)}, f32[512,1024]{1,0:T(8,128)}, bf16[512,1024]{1,0:T(8,128)(2,1)}, bf16[2,8,256,128]{3,2,1,0:T(8,128)(2,1)}, bf16[5...) custom-call(s32[34]{0:T(128)} %pad_add_fusion.place_ref, ...), custom_call_target="tpu_custom_call" | custom-call | flops 19327352832 | bytes 50000000 | tf_op jit(solution)/shard_map/middle/pallas_call | solution.py:562
  270.9 8.1 %all-to-all-start.2 = ((bf16[16,256,128]{2,1,0:T(8,128)(2,1)}), bf16[16,256,128]{2,1,0:T(8,128)(2,1)S(1)}, u32[]{:S(2)}, u32[]{:S(2)}) async-start(bf16[16,256,128]{2,1,0:T(8,128)(2,1)} %bitcast.31), calls=%async_computation.2 | async-start | bytes 2097152 | tf_op jit(solution)/shard_map/all_to_all | solution.py:974
  281.8 2.3 collective-permute-done.18.refs_11_
  285.6 17.8 %ffn_grads.1 = bf16[4,4,576,512]{3,2,1,0:T(8,128)(2,1)} custom-call(bf16[512,4096]{1,0:T(8,128)(2,1)} %get-tuple-element.80.refs_0_, bf16[512,4096]{1,0:T(8,128)(2,1)} %collective-permute-done.14.refs_1_, bf16[512,512]{1,0:T(8,128)(2,1)} %get-tuple-element.81.refs_2_, bf16[512,512]{1,0:T(8,128)(2,1)} %collective-permute-done.11.refs_3_, ...), custom_call_target="tpu_custom_call" | custom-call | flops 9663676416 | bytes 40000000 | tf_op jit(solution)/shard_map/ffn_grads/pallas_call | solution.py:662
  304.6 33.3 %attend_back.1 = bf16[16,3,4,64,128]{4,3,2,1,0:T(8,128)(2,1)} custom-call(s32[384]{0:T(512)} %reshape.131.table_ref, s32[1]{0:T(128)} %bitcast.2.limit_ref, bf16[16,3,4,64,128]{4,3,2,1,0:T(8,128)(2,1)} %bitcast.88, bf16[16,4,64,128]{3,2,1,0:T(8,128)(2,1)} %bitcast.100, f32[64,128]{1,0:T(8,128)} %get-tuple-element.88.lse_ref), custom_call_target="tpu_custom_call" | custom-call | flops 80000000000 | bytes 8000000 | tf_op jit(solution)/shard_map/attend_back/pallas_call | solution.py:389
  337.9 78.3 %all_to_all.21 = bf16[16,3,256,128]{3,2,1,0:T(8,128)(2,1)} all-to-all(bf16[16,3,256,128]{3,2,1,0:T(8,128)(2,1)} %bitcast.90), channel_id=1, replica_groups=mesh['batch'=2,'seq'=16] {'seq'}, dimensions={0} | all-to-all | bytes 6291456 | tf_op jit(solution)/shard_map/all_to_all | solution.py:974
  416.2 3.5 split_by_core.1
  419.8 3.6 collective-permute-done.19.refs_3_
  424.5 7.8 %qkv_grad.1 = (bf16[8,3,32,512]{3,2,1,0:T(8,128)(2,1)}, bf16[8,3,32,512]{3,2,1,0:T(8,128)(2,1)}, bf16[8,3,32,512]{3,2,1,0:T(8,128)(2,1)}, bf16[8,3,32,512]{3,2,1,0:T(8,128)(2,1)}) custom-call(s32[34]{0:T(128)} %pad_add_fusion.place_ref, bf16[512,1024]{1,0:T(8,128)(2,1)} %get-tuple-element.91.refs_0_, bf16[512,1024]{1,0:T(8,128)(2,1)} %collective-permute-done.12.refs_1_, ...), custom_call_target="tpu_custom_call" | custom-call | flops 3221225472 | bytes 15000000 | tf_op jit(solution)/shard_map/qkv_grad/pallas_call | solution.py:736
  434.1 12.7 %input_grad.1 = (f32[512,1024]{1,0:T(8,128)}, f32[1,1024]{1,0:T(1,128)}, f32[1,1024]{1,0:T(1,128)}) custom-call(s32[34]{0:T(128)} %pad_add_fusion.place_ref, bf16[512,1024]{1,0:T(8,128)(2,1)} %bitcast.99, f32[1,1024]{1,0:T(1,128)} %bitcast.118, f32[512,1024]{1,0:T(8,128)} %get-tuple-element.78.dmid_ref, bf16[512,1536]{1,0:T(8,128)(2,1)} %get-tuple-element.89.refs_2_.refs_0_, ...), custom_call_target="tpu_custom_call" | custom-call | flops 3221225472 | bytes 20000000 | tf_op jit(solution)/shard_map/input_grad/pallas_call | solution.py:789
  448.1 4.0 collective-permute-done.20
  458.8 10.2 %collective-permute-done.25 = f32[1,10240]{1,0:T(1,128)S(1)} collective-permute-done((f32[1,10240]{1,0:T(1,128)S(1)}, f32[1,10240]{1,0:T(1,128)S(1)}, u32[]{:S(2)}, u32[]{:S(2)}) %collective-permute-start.25) | collective-permute-done | bytes 40992 | tf_op jit(solution)/shard_map/ppermute | solution.py:806
  470.2 2.9 collective-permute-done.26
  474.8 2.4 collective-permute-start.32
  479.5 2.4 collective-permute-start.29
  482.3 2.9 collective-permute-start.27
  491.7 15.1 %collective-permute-done.28 = bf16[2,3,32,512]{3,1,2,0:T(4,128)(2,1)S(1)} collective-permute-done((bf16[2,3,32,512]{3,1,2,0:T(4,128)(2,1)S(1)}, bf16[2,3,32,512]{3,1,2,0:T(4,128)(2,1)S(1)}, u32[]{:S(2)}, u32[]{:S(2)}) %collective-permute-start.28) | collective-permute-done | bytes 196640 | tf_op jit(solution)/shard_map/ppermute | solution.py:806
  (151 shorter events, 50.7 us)
Async XLA Ops:
  7.2 75.3 %all-gather.5.cloned.1.call-start = ((), (), s32[]{:S(2)}) async-start(), calls=%async_computation.7 | async-start | bytes 2949120 | tf_op jit(solution)/shard_map/all_gather | solution.py:827
  8.4 8.4 %collective-permute-start = (bf16[2,3,32,512]{3,2,1,0:T(8,128)(2,1)S(1)}, bf16[2,3,32,512]{3,2,1,0:T(8,128)(2,1)S(1)}, u32[]{:S(2)}, u32[]{:S(2)}) collective-permute-start(bf16[2,3,32,512]{3,2,1,0:T(8,128)(2,1)S(1)} %bitcast.106), channel_id=1, source_target_pairs={{0,4},{1,5},{2,6},{3,7},{4,0},{5,1},{6,2},{7,3},{8,12},{9,13},{10,... | collective-permute-start | bytes 589832 | tf_op jit(solution)/shard_map/ppermute | solution.py:806
  11.5 12.6 %collective-permute-start.2 = (bf16[2,3,32,512]{3,2,1,0:T(8,128)(2,1)S(1)}, bf16[2,3,32,512]{3,2,1,0:T(8,128)(2,1)S(1)}, u32[]{:S(2)}, u32[]{:S(2)}) collective-permute-start(bf16[2,3,32,512]{3,2,1,0:T(8,128)(2,1)S(1)} %bitcast.107), channel_id=1, source_target_pairs={{0,12},{1,13},{2,14},{3,15},{4,8},{5,9},{6,10},{7,11},{8,4},{9,5},... | collective-permute-start | bytes 589832 | tf_op jit(solution)/shard_map/ppermute | solution.py:806
  14.0 17.4 %collective-permute-start.1 = (bf16[2,3,32,512]{3,2,1,0:T(8,128)(2,1)S(1)}, bf16[2,3,32,512]{3,2,1,0:T(8,128)(2,1)S(1)}, u32[]{:S(2)}, u32[]{:S(2)}) collective-permute-start(bf16[2,3,32,512]{3,2,1,0:T(8,128)(2,1)S(1)} %bitcast.108), channel_id=1, source_target_pairs={{0,8},{1,9},{2,10},{3,11},{4,12},{5,13},{6,14},{7,15},{8,0},{9,1},... | collective-permute-start | bytes 589832 | tf_op jit(solution)/shard_map/ppermute | solution.py:806
  31.5 185.7 %all-gather.7.cloned.1.call-start = ((), (), s32[]{:S(2)}) async-start(), calls=%async_computation.8 | async-start | bytes 11796480 | tf_op jit(solution)/shard_map/all_gather | solution.py:831
  31.6 10.0 %collective-permute-start.5 = (bf16[4,3,32,512]{3,2,1,0:T(8,128)(2,1)S(1)}, bf16[4,3,32,512]{3,2,1,0:T(8,128)(2,1)S(1)}, u32[]{:S(2)}, u32[]{:S(2)}) collective-permute-start(bf16[4,3,32,512]{3,2,1,0:T(8,128)(2,1)S(1)} %get-tuple-element.67), channel_id=1, source_target_pairs={{0,2},{1,3},{2,0},{3,1},{4,6},{5,7},{6,4},{7,5},{8,10},{9,11},{10,... | collective-permute-start | bytes 1179656 | tf_op jit(solution)/shard_map/ppermute | solution.py:806
  33.2 10.1 %collective-permute-start.3 = (bf16[4,3,32,512]{3,2,1,0:T(8,128)(2,1)S(1)}, bf16[4,3,32,512]{3,2,1,0:T(8,128)(2,1)S(1)}, u32[]{:S(2)}, u32[]{:S(2)}) collective-permute-start(bf16[4,3,32,512]{3,2,1,0:T(8,128)(2,1)S(1)} %get-tuple-element.66), channel_id=1, source_target_pairs={{0,1},{1,0},{2,3},{3,2},{4,5},{5,4},{6,7},{7,6},{8,9},{9,8},{10,11... | collective-permute-start | bytes 1179656 | tf_op jit(solution)/shard_map/ppermute | solution.py:806
  41.7 18.1 %collective-permute-start.6 = (bf16[8,3,32,512]{3,2,1,0:T(8,128)(2,1)S(1)}, bf16[8,3,32,512]{3,2,1,0:T(8,128)(2,1)S(1)}, u32[]{:S(2)}, u32[]{:S(2)}) collective-permute-start(bf16[8,3,32,512]{3,2,1,0:T(8,128)(2,1)S(1)} %constant_dynamic-update-slice_fusion.2.refs_2_.refs_4_), channel_id=1, source_target_pairs={{0,1},{1,0},{2,3},{3,2},{4,5},{5,4},{6,7},{7,6},{8,9},{9,8},{10,11... | collective-permute-start | bytes 2359304 | tf_op jit(solution)/shard_map/ppermute | solution.py:806
  43.3 17.3 %collective-permute-start.4 = (bf16[8,3,32,512]{3,2,1,0:T(8,128)(2,1)S(1)}, bf16[8,3,32,512]{3,2,1,0:T(8,128)(2,1)}, u32[]{:S(2)}, u32[]{:S(2)}) collective-permute-start(bf16[8,3,32,512]{3,2,1,0:T(8,128)(2,1)S(1)} %constant_dynamic-update-slice_fusion.refs_0_.refs_2_), channel_id=1, source_target_pairs={{0,2},{1,3},{2,0},{3,1},{4,6},{5,7},{6,4},{7,5},{8,10},{9,11},{10,... | collective-permute-start | bytes 2359304 | tf_op jit(solution)/shard_map/ppermute | solution.py:806
  44.9 16.4 %collective-permute-start.9 = (bf16[8,3,32,512]{3,2,1,0:T(8,128)(2,1)S(1)}, bf16[8,3,32,512]{3,2,1,0:T(8,128)(2,1)}, u32[]{:S(2)}, u32[]{:S(2)}) collective-permute-start(bf16[8,3,32,512]{3,2,1,0:T(8,128)(2,1)S(1)} %constant_dynamic-update-slice_fusion.2.refs_2_.refs_4_), channel_id=1, source_target_pairs={{0,16},{16,0},{1,17},{17,1},{2,18},{18,2},{3,19},{19,3},{4,20},{20... | collective-permute-start | bytes 2359304 | tf_op jit(solution)/shard_map/ppermute | solution.py:806
  44.9 16.4 %collective-permute-start.7 = (bf16[8,3,32,512]{3,2,1,0:T(8,128)(2,1)S(1)}, bf16[8,3,32,512]{3,2,1,0:T(8,128)(2,1)}, u32[]{:S(2)}, u32[]{:S(2)}) collective-permute-start(bf16[8,3,32,512]{3,2,1,0:T(8,128)(2,1)S(1)} %constant_dynamic-update-slice_fusion.refs_0_.refs_2_), channel_id=1, source_target_pairs={{0,16},{16,0},{1,17},{17,1},{2,18},{18,2},{3,19},{19,3},{4,20},{20... | collective-permute-start | bytes 2359304 | tf_op jit(solution)/shard_map/ppermute | solution.py:806
  82.5 65.6 %all-to-all-start = ((bf16[16,3,256,128]{3,2,1,0:T(8,128)(2,1)}), bf16[16,3,256,128]{3,2,1,0:T(8,128)(2,1)S(1)}, u32[]{:S(2)}, u32[]{:S(2)}) async-start(bf16[16,3,256,128]{3,2,1,0:T(8,128)(2,1)} %bitcast.89), calls=%async_computation | async-start | bytes 6291456 | tf_op jit(solution)/shard_map/all_to_all | solution.py:974
  86.9 4.7 collective-permute-start.12
  217.2 15.0 %collective-permute-start.13 = (bf16[16,576,512]{2,1,0:T(8,128)(2,1)}, bf16[16,576,512]{2,1,0:T(8,128)(2,1)}, u32[]{:S(2)}, u32[]{:S(2)}) collective-permute-start(bf16[16,576,512]{2,1,0:T(8,128)(2,1)} %all-gather.7.cloned.1.call-done.refs_0_), channel_id=1, source_target_pairs={{0,16},{16,0},{1,17},{17,1},{2,18},{18,2},{3,19},{19,3},{4,20},{20... | collective-permute-start | bytes 28311560 | tf_op jit(solution)/shard_map/ppermute | solution.py:806
  268.5 15.6 %collective-permute-start.14 = (bf16[512,4096]{1,0:T(8,128)(2,1)}, bf16[512,4096]{1,0:T(8,128)(2,1)}, u32[]{:S(2)}, u32[]{:S(2)}) collective-permute-start(bf16[512,4096]{1,0:T(8,128)(2,1)} %get-tuple-element.80.refs_0_), channel_id=1, source_target_pairs={{0,16},{16,0},{1,17},{17,1},{2,18},{18,2},{3,19},{19,3},{4,20},{20... | collective-permute-start | bytes 12582920 | tf_op jit(solution)/shard_map/ppermute | solution.py:806
  270.5 13.6 %collective-permute-start.16 = (bf16[1,512,2048]{2,1,0:T(8,128)(2,1)S(1)}, bf16[1,512,2048]{2,1,0:T(8,128)(2,1)}, u32[]{:S(2)}, u32[]{:S(2)}) collective-permute-start(bf16[1,512,2048]{2,1,0:T(8,128)(2,1)S(1)} %slice.61), channel_id=1, source_target_pairs={{0,16},{16,0},{1,17},{17,1},{2,18},{18,2},{3,19},{19,3},{4,20},{20... | collective-permute-start | bytes 6291464 | tf_op jit(solution)/shard_map/ppermute | solution.py:806
  270.9 32.7 %all-to-all-start.2 = ((bf16[16,256,128]{2,1,0:T(8,128)(2,1)}), bf16[16,256,128]{2,1,0:T(8,128)(2,1)S(1)}, u32[]{:S(2)}, u32[]{:S(2)}) async-start(bf16[16,256,128]{2,1,0:T(8,128)(2,1)} %bitcast.31), calls=%async_computation.2 | async-start | bytes 2097152 | tf_op jit(solution)/shard_map/all_to_all | solution.py:974
  279.0 155.0 %reduce-scatter.7.cloned.1.call-start = ((), (), s32[]{:S(2)}) async-start(), calls=%async_computation.9 | async-start | bytes 11796480
  279.1 5.0 collective-permute-start.15
  279.2 4.9 collective-permute-start.17
  304.6 183.2 %reduce-scatter.5.cloned.1.call-start = ((), (), s32[]{:S(2)}) async-start(), calls=%async_computation.6 | async-start | bytes 2949120 | tf_op jit(solution)/shard_map/reduce_scatter | solution.py:836
  432.4 19.8 %collective-permute-start.20 = (bf16[8,3,32,512]{3,2,1,0:T(8,128)(2,1)}, bf16[8,3,32,512]{3,2,1,0:T(8,128)(2,1)S(1)}, u32[]{:S(2)}, u32[]{:S(2)}) collective-permute-start(bf16[8,3,32,512]{3,2,1,0:T(8,128)(2,1)} %get-tuple-element.104), channel_id=1, source_target_pairs={{0,2},{1,3},{2,0},{3,1},{4,6},{5,7},{6,4},{7,5},{8,10},{9,11},{10,... | collective-permute-start | bytes 2359304 | tf_op jit(solution)/shard_map/ppermute | solution.py:806
  433.4 19.6 %collective-permute-start.21 = (bf16[8,3,32,512]{3,2,1,0:T(8,128)(2,1)}, bf16[8,3,32,512]{3,2,1,0:T(8,128)(2,1)S(1)}, u32[]{:S(2)}, u32[]{:S(2)}) collective-permute-start(bf16[8,3,32,512]{3,2,1,0:T(8,128)(2,1)} %get-tuple-element.105), channel_id=1, source_target_pairs={{0,1},{1,0},{2,3},{3,2},{4,5},{5,4},{6,7},{7,6},{8,9},{9,8},{10,11... | collective-permute-start | bytes 2359304 | tf_op jit(solution)/shard_map/ppermute | solution.py:806
  453.6 19.5 %collective-permute-start.23 = (bf16[4,1,3,32,512]{4,2,3,1,0:T(4,128)(2,1)S(1)}, bf16[4,1,3,32,512]{4,2,3,1,0:T(4,128)(2,1)S(1)}, u32[]{:S(2)}, u32[]{:S(2)}) collective-permute-start(bf16[4,1,3,32,512]{4,2,3,1,0:T(4,128)(2,1)S(1)} %copy.65), channel_id=1, source_target_pairs={{0,2},{1,3},{2,0},{3,1},{4,6},{5,7},{6,4},{7,5},{8,10},{9,11},{10,... | collective-permute-start | bytes 1179656 | tf_op jit(solution)/shard_map/ppermute | solution.py:806
  455.3 18.3 %collective-permute-start.22 = (bf16[4,1,3,32,512]{4,2,3,1,0:T(4,128)(2,1)S(1)}, bf16[4,1,3,32,512]{4,2,3,1,0:T(4,128)(2,1)S(1)}, u32[]{:S(2)}, u32[]{:S(2)}) collective-permute-start(bf16[4,1,3,32,512]{4,2,3,1,0:T(4,128)(2,1)S(1)} %copy.63), channel_id=1, source_target_pairs={{0,1},{1,0},{2,3},{3,2},{4,5},{5,4},{6,7},{7,6},{8,9},{9,8},{10,11... | collective-permute-start | bytes 1179656 | tf_op jit(solution)/shard_map/ppermute | solution.py:806
  457.3 11.7 %collective-permute-start.25 = (f32[1,10240]{1,0:T(1,128)S(1)}, f32[1,10240]{1,0:T(1,128)S(1)}, u32[]{:S(2)}, u32[]{:S(2)}) collective-permute-start(f32[1,10240]{1,0:T(1,128)S(1)} %add.89), channel_id=1, source_target_pairs={{0,1},{1,0},{2,3},{3,2},{4,5},{5,4},{6,7},{7,6},{8,9},{9,8},{10,11... | collective-permute-start | bytes 122888 | tf_op jit(solution)/shard_map/ppermute | solution.py:806
  474.8 7.5 %collective-permute-start.32 = (f32[1,10240]{1,0:T(1,128)S(1)}, f32[1,10240]{1,0:T(1,128)S(1)}, u32[]{:S(2)}, u32[]{:S(2)}) collective-permute-start(f32[1,10240]{1,0:T(1,128)S(1)} %add.91), channel_id=1, source_target_pairs={{0,12},{1,13},{2,14},{3,15},{4,8},{5,9},{6,10},{7,11},{8,4},{9,5},... | collective-permute-start | bytes 122888 | tf_op jit(solution)/shard_map/ppermute | solution.py:806
  477.3 9.2 %collective-permute-start.31 = (f32[1,10240]{1,0:T(1,128)S(1)}, f32[1,10240]{1,0:T(1,128)S(1)}, u32[]{:S(2)}, u32[]{:S(2)}) collective-permute-start(f32[1,10240]{1,0:T(1,128)S(1)} %add.91), channel_id=1, source_target_pairs={{0,8},{1,9},{2,10},{3,11},{4,12},{5,13},{6,14},{7,15},{8,0},{9,1},... | collective-permute-start | bytes 122888 | tf_op jit(solution)/shard_map/ppermute | solution.py:806
  477.7 8.8 %collective-permute-start.30 = (f32[1,10240]{1,0:T(1,128)S(1)}, f32[1,10240]{1,0:T(1,128)S(1)}, u32[]{:S(2)}, u32[]{:S(2)}) collective-permute-start(f32[1,10240]{1,0:T(1,128)S(1)} %add.91), channel_id=1, source_target_pairs={{0,4},{1,5},{2,6},{3,7},{4,0},{5,1},{6,2},{7,3},{8,12},{9,13},{10,... | collective-permute-start | bytes 122888 | tf_op jit(solution)/shard_map/ppermute | solution.py:806
  479.5 12.2 %collective-permute-start.29 = (bf16[2,3,32,512]{3,1,2,0:T(4,128)(2,1)S(1)}, bf16[2,3,32,512]{3,1,2,0:T(4,128)(2,1)S(1)}, u32[]{:S(2)}, u32[]{:S(2)}) collective-permute-start(bf16[2,3,32,512]{3,1,2,0:T(4,128)(2,1)S(1)} %get-tuple-element.158), channel_id=1, source_target_pairs={{0,12},{1,13},{2,14},{3,15},{4,8},{5,9},{6,10},{7,11},{8,4},{9,5},... | collective-permute-start | bytes 589832 | tf_op jit(solution)/shard_map/ppermute | solution.py:806
  482.0 24.8 %collective-permute-start.28 = (bf16[2,3,32,512]{3,1,2,0:T(4,128)(2,1)S(1)}, bf16[2,3,32,512]{3,1,2,0:T(4,128)(2,1)S(1)}, u32[]{:S(2)}, u32[]{:S(2)}) collective-permute-start(bf16[2,3,32,512]{3,1,2,0:T(4,128)(2,1)S(1)} %get-tuple-element.159), channel_id=1, source_target_pairs={{0,8},{1,9},{2,10},{3,11},{4,12},{5,13},{6,14},{7,15},{8,0},{9,1},... | collective-permute-start | bytes 589832 | tf_op jit(solution)/shard_map/ppermute | solution.py:806
  482.3 24.5 %collective-permute-start.27 = (bf16[2,3,32,512]{3,1,2,0:T(4,128)(2,1)S(1)}, bf16[2,3,32,512]{3,1,2,0:T(4,128)(2,1)S(1)}, u32[]{:S(2)}, u32[]{:S(2)}) collective-permute-start(bf16[2,3,32,512]{3,1,2,0:T(4,128)(2,1)S(1)} %get-tuple-element.160), channel_id=1, source_target_pairs={{0,4},{1,5},{2,6},{3,7},{4,0},{5,1},{6,2},{7,3},{8,12},{9,13},{10,... | collective-permute-start | bytes 589832 | tf_op jit(solution)/shard_map/ppermute | solution.py:806
  (28 other events, 250.7 us)
Sparse Core Ops, SparseCore 0:
  31.7 50.7 all-gather.4
  84.3 132.8 all-gather.6
  303.8 128.1 reduce-scatter.6
  434.1 50.6 reduce-scatter.4

commit v6 on v5

--- a/solution.py
+++ b/solution.py
@@ -702,16 +702,30 @@
     )(place, grad)
 
 
-def qkv_grad_kernel(place_ref, *refs, nb, n):
-    h_refs, ga_refs = refs[:nb], refs[nb : 2 * nb]
-    a_send_ref, a_keep_ref, b_send_ref, b_keep_ref, ht_ref = refs[2 * nb :]
+def turn_kernel(place_ref, *refs, nb, n):
+    for k in range(nb):
+        relative_transpose(refs[k], refs[nb], k, place_ref[2 * n + 1], n)
+
+
+def turn(place, h, n):
+    nb = len(h)
+    rows, width = h[0].shape
+    return pl.pallas_call(
+        functools.partial(turn_kernel, nb=nb, n=n),
+        in_specs=[SMEM] + [WHOLE] * nb,
+        out_specs=WHOLE,
+        out_shape=jax.ShapeDtypeStruct((nb, width, rows), BF),
+        compiler_params=params(),
+        cost_estimate=cost(1e6, 4e6),
+        name="turn",
+    )(place, *h)
+
+
+def qkv_grad_kernel(ht_ref, *refs, nb, n):
+    ga_refs = refs[:nb]
+    a_send_ref, a_keep_ref, b_send_ref, b_keep_ref = refs[nb:]
     first = n // 8
     _, _, kh, fb = a_send_ref.shape
-
-    @pl.when(pl.program_id(0) == 0)
-    def _():
-        for k in range(nb):
-            relative_transpose(h_refs[k], ht_ref, k, place_ref[2 * n + 1], n)
 
     y = None
     for k in range(nb):
@@ -727,25 +741,22 @@
             b_keep_ref[at, 0] = y[z, 2 * i, 1]
 
 
-def qkv_grad(place, h, ga, n):
-    nb = len(h)
-    rows, width = h[0].shape
+def qkv_grad(turned, ga, n):
+    nb, width, rows = turned.shape
     fb = ga[0].shape[1] // 3
     kh = width // n // 2
     half = jax.ShapeDtypeStruct((n // 2, 3, kh, fb), BF)
     return pl.pallas_call(
         functools.partial(qkv_grad_kernel, nb=nb, n=n),
         grid=(3,),
-        in_specs=[SMEM]
-        + [constant((rows, width))] * nb
+        in_specs=[constant((nb, width, rows))]
         + [pl.BlockSpec((rows, fb), lambda t: (0, t))] * nb,
         out_specs=[pl.BlockSpec((n // 2, 1, kh, fb), lambda t: (0, t, 0, 0))] * 4,
         out_shape=[half] * 4,
-        scratch_shapes=[pltpu.VMEM((nb, width, rows), BF)],
         compiler_params=params(),
         cost_estimate=cost(6 * rows * width * width, 15e6),
         name="qkv_grad",
-    )(place, *h, *ga)
+    )(turned, *ga)
 
 
 def input_grad_kernel(place_ref, x_ref, gain_ref, dmid_ref, *refs, nb):
@@ -985,7 +996,8 @@
     rest_plane = gather_plane(rest_line, n)
     qkv_all = swap(qkv.reshape(n, 3, local, lanes)).reshape(n, 3, bpd, BLOCK, lanes)
     g_cores, h1_cores = columns_over_cores(g, fb), over_cores(h1)
-    qkv_all, g_cores, h1_cores = together(qkv_all, g_cores, h1_cores)
+    turned = turn(place, h1_cores, n)
+    qkv_all, g_cores, turned = together(qkv_all, g_cores, turned)
     mixed, lse = attend(qkv_all, table, limit, per)
     o = swap(mixed.reshape(n, local, lanes)).reshape(micros, groups, local, lanes)
     o, rest_plane = together(o, rest_plane)
@@ -1035,7 +1047,7 @@
     grads_back = swap(grads.reshape(n, 3, local, lanes)).reshape(micros, groups, 3, local, lanes)
     own_grads = split_by_core(place, grads_back, nb, n)
     grad_cores = [own_grads[0]] + [swap_with(own_grads[k], "batch", k) for k in range(1, nb)]
-    a_send, a_keep, b_send, b_keep = qkv_grad(place, h1_cores, grad_cores, n)
+    a_send, a_keep, b_send, b_keep = qkv_grad(turned, grad_cores, n)
     a_keep, rest_line = together(a_keep, rest_line)
     grad_rest = scatter_groups(rest_line, lines(n)).astype(F32)
     first_a, first_b = reduce_first(a_send, b_send, n)

time: 515 us -> 515 us (level)
  transfers between devices with their start and end apart: 39 -> 39, of which waited for: 25 -> 23; matrix products, arithmetic and copies ran while one was open for 4% -> 4% of each run, Pallas kernels for 20% -> 21%
where the time goes in v6:
time: 515 us; the launch traced here: 514 us
  waiting for transfers between devices  166 us (32%)
  Pallas kernels  144 us (28%)
  blocking collectives  119 us (23%)
  starting transfers between devices  42.7 us (8%)
  local copies, waits for them, and re-layouts  23.1 us (4%)
  between operations  14.2 us (3%)
  other arithmetic  5.3 us (1%)
    all_to_all x2, blocking collectives, swap(): return lax.all_to_all(value, 'seq', split_axis=0, concat_axis=0, tiled=True)  119 us
    ppermute x33, waiting for transfers between devices, swap_with(): return lax.ppermute(value, axis, [(i, i ^ k) for i in range(size)])  96.4 us
    all_to_all x2, waiting for transfers between devices, swap(): return lax.all_to_all(value, 'seq', split_axis=0, concat_axis=0, tiled=True)  53.2 us
    pallas_call x1, Pallas kernels, middle(): pl.pallas_call(kernel, grid_spec=pltpu.PrefetchScalarGridSpec(num_scalar_...  36.3 us
    pallas_call x1, Pallas kernels, attend_back(): pl.pallas_call(kernel, in_specs=[SMEM, SMEM, WHOLE, WHOLE, WHOLE], out_sp...  33.5 us
    ppermute x33, starting transfers between devices, swap_with(): return lax.ppermute(value, axis, [(i, i ^ k) for i in range(size)])  30 us
    pallas_call x1, Pallas kernels, attend(): pl.pallas_call(kernel, in_specs=[SMEM, SMEM, WHOLE], out_specs=[WHOLE, WH...  19.3 us
    pallas_call x1, Pallas kernels, ffn_grads(): pl.pallas_call(functools.partial(ffn_grads_kernel, nb=nb), grid=(4,), in_...  17.8 us
  transfers between devices with their start and end apart: 39, of which 23 were waited for; matrix products, arithmetic and copies ran while one was open for 4% of the time, Pallas kernels for 21%

profile of v6, /device:TPU:0, one launch (start us, length us, event | category | flops | bytes accessed | tf_op | source)
XLA Modules:
  0.0 514.5 jit_solution(14398511723560036506)
XLA Ops:
  8.4 3.1 collective-permute-start
  11.4 2.5 collective-permute-start.2
  16.9 7.1 %collective-permute-done.2 = bf16[2,3,32,512]{3,2,1,0:T(8,128)(2,1)S(1)} collective-permute-done((bf16[2,3,32,512]{3,2,1,0:T(8,128)(2,1)S(1)}, bf16[2,3,32,512]{3,2,1,0:T(8,128)(2,1)S(1)}, u32[]{:S(2)}, u32[]{:S(2)}) %collective-permute-start.2) | collective-permute-done | bytes 196640 | tf_op jit(solution)/shard_map/ppermute | solution.py:817
  24.0 7.3 %collective-permute-done.1 = bf16[2,3,32,512]{3,2,1,0:T(8,128)(2,1)S(1)} collective-permute-done((bf16[2,3,32,512]{3,2,1,0:T(8,128)(2,1)S(1)}, bf16[2,3,32,512]{3,2,1,0:T(8,128)(2,1)S(1)}, u32[]{:S(2)}, u32[]{:S(2)}) %collective-permute-start.1) | collective-permute-done | bytes 196640 | tf_op jit(solution)/shard_map/ppermute | solution.py:817
  34.7 6.9 %collective-permute-done.5 = bf16[4,3,32,512]{3,2,1,0:T(8,128)(2,1)S(1)} collective-permute-done((bf16[4,3,32,512]{3,2,1,0:T(8,128)(2,1)S(1)}, bf16[4,3,32,512]{3,2,1,0:T(8,128)(2,1)S(1)}, u32[]{:S(2)}, u32[]{:S(2)}) %collective-permute-start.5) | collective-permute-done | bytes 393248 | tf_op jit(solution)/shard_map/ppermute | solution.py:817
  45.3 14.4 %collective-permute-done.6.refs_3_.refs_5_ = bf16[8,3,32,512]{3,2,1,0:T(8,128)(2,1)S(1)} collective-permute-done((bf16[8,3,32,512]{3,2,1,0:T(8,128)(2,1)S(1)}, bf16[8,3,32,512]{3,2,1,0:T(8,128)(2,1)S(1)}, u32[]{:S(2)}, u32[]{:S(2)}) %collective-permute-start.6) | collective-permute-done | bytes 786464 | tf_op jit(solution)/shard_map/ppermute | solution.py:817
  63.4 10.0 %project.1 = (bf16[2,8,3,256,128]{4,3,2,1,0:T(8,128)(2,1)}, bf16[512,1024]{1,0:T(8,128)(2,1)}) custom-call(s32[34]{0:T(128)} %pad_add_fusion.place_ref, bf16[512,1024]{1,0:T(8,128)(2,1)} %bitcast.97, f32[1,1024]{1,0:T(1,128)} %bitcast.117, f32[1,1024]{1,0:T(1,128)} %bitcast.127, bf16[8,3,32,512]{3,2,1,0:T(8,128)(2,1)} %copy-done.5, ...), custom_call_target="tpu_custom_call" | custom-call | flops 3221225472 | bytes 14680064 | tf_op jit(solution)/shard_map/project/pallas_call | solution.py:118
  73.4 9.0 %all-gather.5.cloned.1.call-done = bf16[2304,512]{1,0:T(8,128)(2,1)} async-done(((bf16[576,512]{1,0:T(8,128)(2,1)}), bf16[2304,512]{1,0:T(8,128)(2,1)}) %all-gather.5.cloned.1.call-update) | async-done | bytes 2359312 | tf_op jit(solution)/shard_map/all_gather | solution.py:838
  82.4 4.4 all-to-all-start
  91.2 3.8 turn.1.ht_ref
  95.0 53.0 %all-to-all-done = bf16[16,3,256,128]{3,2,1,0:T(8,128)(2,1)S(1)} async-done(((bf16[16,3,256,128]{3,2,1,0:T(8,128)(2,1)}), bf16[16,3,256,128]{3,2,1,0:T(8,128)(2,1)S(1)}, u32[]{:S(2)}, u32[]{:S(2)}) %all-to-all-start) | async-done | bytes 3145760 | tf_op jit(solution)/shard_map/all_to_all | solution.py:985
  149.7 19.3 %attend.1 = (bf16[16,4,64,128]{3,2,1,0:T(8,128)(2,1)}, f32[64,128]{1,0:T(8,128)}) custom-call(s32[384]{0:T(512)} %reshape.131.table_ref, s32[1]{0:T(128)} %bitcast.2.limit_ref, bf16[16,3,4,64,128]{4,3,2,1,0:T(8,128)(2,1)} %bitcast.87), custom_call_target="tpu_custom_call" | custom-call | flops 40000000000 | bytes 4000000 | tf_op jit(solution)/shard_map/attend/pallas_call | solution.py:286
  169.0 40.7 %all_to_all.20 = bf16[16,256,128]{2,1,0:T(8,128)(2,1)} all-to-all(bf16[16,256,128]{2,1,0:T(8,128)(2,1)} %bitcast.102), channel_id=1, replica_groups=mesh['batch'=2,'seq'=16] {'seq'}, dimensions={0} | all-to-all | bytes 2097152 | tf_op jit(solution)/shard_map/all_to_all | solution.py:985
  209.7 7.4 %all-gather.7.cloned.1.call-done.refs_0_ = bf16[16,576,512]{2,1,0:T(8,128)(2,1)} async-done(((bf16[4,576,512]{2,1,0:T(8,128)(2,1)}), bf16[16,576,512]{2,1,0:T(8,128)(2,1)}) %all-gather.7.cloned.1.call-update) | async-done | bytes 9437200 | tf_op jit(solution)/shard_map/all_gather | solution.py:842
  217.1 15.0 %collective-permute-done.13.refs_1_ = bf16[16,576,512]{2,1,0:T(8,128)(2,1)} collective-permute-done((bf16[16,576,512]{2,1,0:T(8,128)(2,1)}, bf16[16,576,512]{2,1,0:T(8,128)(2,1)}, u32[]{:S(2)}, u32[]{:S(2)}) %collective-permute-start.13) | collective-permute-done | bytes 9437216 | tf_op jit(solution)/shard_map/ppermute | solution.py:817
  232.1 36.3 %middle.1 = (bf16[512,1024]{1,0:T(8,128)(2,1)}, f32[512,1024]{1,0:T(8,128)}, bf16[512,1024]{1,0:T(8,128)(2,1)}, bf16[2,8,256,128]{3,2,1,0:T(8,128)(2,1)}, bf16[5...) custom-call(s32[34]{0:T(128)} %pad_add_fusion.place_ref, ...), custom_call_target="tpu_custom_call" | custom-call | flops 19327352832 | bytes 50000000 | tf_op jit(solution)/shard_map/middle/pallas_call | solution.py:562
  270.9 8.1 %all-to-all-start.2 = ((bf16[16,256,128]{2,1,0:T(8,128)(2,1)}), bf16[16,256,128]{2,1,0:T(8,128)(2,1)S(1)}, u32[]{:S(2)}, u32[]{:S(2)}) async-start(bf16[16,256,128]{2,1,0:T(8,128)(2,1)} %bitcast.31), calls=%async_computation.2 | async-start | bytes 2097152 | tf_op jit(solution)/shard_map/all_to_all | solution.py:985
  285.5 17.8 %ffn_grads.1 = bf16[4,4,576,512]{3,2,1,0:T(8,128)(2,1)} custom-call(bf16[512,4096]{1,0:T(8,128)(2,1)} %get-tuple-element.79.refs_0_, bf16[512,4096]{1,0:T(8,128)(2,1)} %collective-permute-done.14.refs_1_, bf16[512,512]{1,0:T(8,128)(2,1)} %get-tuple-element.80.refs_2_, bf16[512,512]{1,0:T(8,128)(2,1)} %collective-permute-done.11.refs_3_, ...), custom_call_target="tpu_custom_call" | custom-call | flops 9663676416 | bytes 40000000 | tf_op jit(solution)/shard_map/ffn_grads/pallas_call | solution.py:662
  304.6 33.5 %attend_back.1 = bf16[16,3,4,64,128]{4,3,2,1,0:T(8,128)(2,1)} custom-call(s32[384]{0:T(512)} %reshape.131.table_ref, s32[1]{0:T(128)} %bitcast.2.limit_ref, bf16[16,3,4,64,128]{4,3,2,1,0:T(8,128)(2,1)} %bitcast.88, bf16[16,4,64,128]{3,2,1,0:T(8,128)(2,1)} %bitcast.100, f32[64,128]{1,0:T(8,128)} %get-tuple-element.87.lse_ref), custom_call_target="tpu_custom_call" | custom-call | flops 80000000000 | bytes 8000000 | tf_op jit(solution)/shard_map/attend_back/pallas_call | solution.py:389
  338.0 78.3 %all_to_all.21 = bf16[16,3,256,128]{3,2,1,0:T(8,128)(2,1)} all-to-all(bf16[16,3,256,128]{3,2,1,0:T(8,128)(2,1)} %bitcast.90), channel_id=1, replica_groups=mesh['batch'=2,'seq'=16] {'seq'}, dimensions={0} | all-to-all | bytes 6291456 | tf_op jit(solution)/shard_map/all_to_all | solution.py:985
  416.3 3.6 split_by_core.1
  420.0 3.6 collective-permute-done.19.refs_1_
  424.7 7.2 %qkv_grad.1 = (bf16[8,3,32,512]{3,2,1,0:T(8,128)(2,1)}, bf16[8,3,32,512]{3,2,1,0:T(8,128)(2,1)}, bf16[8,3,32,512]{3,2,1,0:T(8,128)(2,1)}, bf16[8,3,32,512]{3,2,1,0:T(8,128)(2,1)}) custom-call(bf16[2,1024,512]{2,1,0:T(8,128)(2,1)} %turn.1.ht_ref, bf16[512,1536]{1,0:T(8,128)(2,1)} %get-tuple-element.88.refs_0_, bf16[512,1536]{1,0:T(8,128)(2,1)} %copy-done.15), custom_call_target="tpu_custom_call" | custom-call | flops 3221225472 | bytes 15000000 | tf_op jit(solution)/shard_map/qkv_grad/pallas_call | solution.py:749
  433.6 12.7 %input_grad.1 = (f32[512,1024]{1,0:T(8,128)}, f32[1,1024]{1,0:T(1,128)}, f32[1,1024]{1,0:T(1,128)}) custom-call(s32[34]{0:T(128)} %pad_add_fusion.place_ref, bf16[512,1024]{1,0:T(8,128)(2,1)} %bitcast.99, f32[1,1024]{1,0:T(1,128)} %bitcast.118, f32[512,1024]{1,0:T(8,128)} %get-tuple-element.77.dmid_ref, bf16[512,1536]{1,0:T(8,128)(2,1)} %get-tuple-element.88.refs_0_, ...), custom_call_target="tpu_custom_call" | custom-call | flops 3221225472 | bytes 20000000 | tf_op jit(solution)/shard_map/input_grad/pallas_call | solution.py:800
  447.7 3.9 collective-permute-done.20
  458.3 10.1 %collective-permute-done.25 = f32[1,10240]{1,0:T(1,128)S(1)} collective-permute-done((f32[1,10240]{1,0:T(1,128)S(1)}, f32[1,10240]{1,0:T(1,128)S(1)}, u32[]{:S(2)}, u32[]{:S(2)}) %collective-permute-start.25) | collective-permute-done | bytes 40992 | tf_op jit(solution)/shard_map/ppermute | solution.py:817
  469.7 2.7 collective-permute-done.26
  474.1 2.4 collective-permute-start.32
  478.9 2.4 collective-permute-start.29
  481.5 2.9 collective-permute-start.27
  484.5 2.6 collective-permute-done.31
  491.9 14.9 %collective-permute-done.28 = bf16[2,3,32,512]{3,1,2,0:T(4,128)(2,1)S(1)} collective-permute-done((bf16[2,3,32,512]{3,1,2,0:T(4,128)(2,1)S(1)}, bf16[2,3,32,512]{3,1,2,0:T(4,128)(2,1)S(1)}, u32[]{:S(2)}, u32[]{:S(2)}) %collective-permute-start.28) | collective-permute-done | bytes 196640 | tf_op jit(solution)/shard_map/ppermute | solution.py:817
  (150 shorter events, 53.5 us)
Async XLA Ops:
  7.2 75.2 %all-gather.5.cloned.1.call-start = ((), (), s32[]{:S(2)}) async-start(), calls=%async_computation.7 | async-start | bytes 2949120 | tf_op jit(solution)/shard_map/all_gather | solution.py:838
  8.4 8.5 %collective-permute-start = (bf16[2,3,32,512]{3,2,1,0:T(8,128)(2,1)S(1)}, bf16[2,3,32,512]{3,2,1,0:T(8,128)(2,1)S(1)}, u32[]{:S(2)}, u32[]{:S(2)}) collective-permute-start(bf16[2,3,32,512]{3,2,1,0:T(8,128)(2,1)S(1)} %bitcast.106), channel_id=1, source_target_pairs={{0,4},{1,5},{2,6},{3,7},{4,0},{5,1},{6,2},{7,3},{8,12},{9,13},{10,... | collective-permute-start | bytes 589832 | tf_op jit(solution)/shard_map/ppermute | solution.py:817
  11.4 12.6 %collective-permute-start.2 = (bf16[2,3,32,512]{3,2,1,0:T(8,128)(2,1)S(1)}, bf16[2,3,32,512]{3,2,1,0:T(8,128)(2,1)S(1)}, u32[]{:S(2)}, u32[]{:S(2)}) collective-permute-start(bf16[2,3,32,512]{3,2,1,0:T(8,128)(2,1)S(1)} %bitcast.107), channel_id=1, source_target_pairs={{0,12},{1,13},{2,14},{3,15},{4,8},{5,9},{6,10},{7,11},{8,4},{9,5},... | collective-permute-start | bytes 589832 | tf_op jit(solution)/shard_map/ppermute | solution.py:817
  13.9 17.4 %collective-permute-start.1 = (bf16[2,3,32,512]{3,2,1,0:T(8,128)(2,1)S(1)}, bf16[2,3,32,512]{3,2,1,0:T(8,128)(2,1)S(1)}, u32[]{:S(2)}, u32[]{:S(2)}) collective-permute-start(bf16[2,3,32,512]{3,2,1,0:T(8,128)(2,1)S(1)} %bitcast.108), channel_id=1, source_target_pairs={{0,8},{1,9},{2,10},{3,11},{4,12},{5,13},{6,14},{7,15},{8,0},{9,1},... | collective-permute-start | bytes 589832 | tf_op jit(solution)/shard_map/ppermute | solution.py:817
  31.5 185.7 %all-gather.7.cloned.1.call-start = ((), (), s32[]{:S(2)}) async-start(), calls=%async_computation.8 | async-start | bytes 11796480 | tf_op jit(solution)/shard_map/all_gather | solution.py:842
  31.5 10.0 %collective-permute-start.5 = (bf16[4,3,32,512]{3,2,1,0:T(8,128)(2,1)S(1)}, bf16[4,3,32,512]{3,2,1,0:T(8,128)(2,1)S(1)}, u32[]{:S(2)}, u32[]{:S(2)}) collective-permute-start(bf16[4,3,32,512]{3,2,1,0:T(8,128)(2,1)S(1)} %get-tuple-element.66), channel_id=1, source_target_pairs={{0,2},{1,3},{2,0},{3,1},{4,6},{5,7},{6,4},{7,5},{8,10},{9,11},{10,... | collective-permute-start | bytes 1179656 | tf_op jit(solution)/shard_map/ppermute | solution.py:817
  33.1 10.1 %collective-permute-start.3 = (bf16[4,3,32,512]{3,2,1,0:T(8,128)(2,1)S(1)}, bf16[4,3,32,512]{3,2,1,0:T(8,128)(2,1)S(1)}, u32[]{:S(2)}, u32[]{:S(2)}) collective-permute-start(bf16[4,3,32,512]{3,2,1,0:T(8,128)(2,1)S(1)} %get-tuple-element.65), channel_id=1, source_target_pairs={{0,1},{1,0},{2,3},{3,2},{4,5},{5,4},{6,7},{7,6},{8,9},{9,8},{10,11... | collective-permute-start | bytes 1179656 | tf_op jit(solution)/shard_map/ppermute | solution.py:817
  41.6 18.1 %collective-permute-start.6 = (bf16[8,3,32,512]{3,2,1,0:T(8,128)(2,1)S(1)}, bf16[8,3,32,512]{3,2,1,0:T(8,128)(2,1)S(1)}, u32[]{:S(2)}, u32[]{:S(2)}) collective-permute-start(bf16[8,3,32,512]{3,2,1,0:T(8,128)(2,1)S(1)} %constant_dynamic-update-slice_fusion.2.refs_2_.refs_4_), channel_id=1, source_target_pairs={{0,1},{1,0},{2,3},{3,2},{4,5},{5,4},{6,7},{7,6},{8,9},{9,8},{10,11... | collective-permute-start | bytes 2359304 | tf_op jit(solution)/shard_map/ppermute | solution.py:817
  43.3 17.3 %collective-permute-start.4 = (bf16[8,3,32,512]{3,2,1,0:T(8,128)(2,1)S(1)}, bf16[8,3,32,512]{3,2,1,0:T(8,128)(2,1)}, u32[]{:S(2)}, u32[]{:S(2)}) collective-permute-start(bf16[8,3,32,512]{3,2,1,0:T(8,128)(2,1)S(1)} %constant_dynamic-update-slice_fusion.refs_0_.refs_2_), channel_id=1, source_target_pairs={{0,2},{1,3},{2,0},{3,1},{4,6},{5,7},{6,4},{7,5},{8,10},{9,11},{10,... | collective-permute-start | bytes 2359304 | tf_op jit(solution)/shard_map/ppermute | solution.py:817
  44.8 16.4 %collective-permute-start.9 = (bf16[8,3,32,512]{3,2,1,0:T(8,128)(2,1)S(1)}, bf16[8,3,32,512]{3,2,1,0:T(8,128)(2,1)}, u32[]{:S(2)}, u32[]{:S(2)}) collective-permute-start(bf16[8,3,32,512]{3,2,1,0:T(8,128)(2,1)S(1)} %constant_dynamic-update-slice_fusion.2.refs_2_.refs_4_), channel_id=1, source_target_pairs={{0,16},{16,0},{1,17},{17,1},{2,18},{18,2},{3,19},{19,3},{4,20},{20... | collective-permute-start | bytes 2359304 | tf_op jit(solution)/shard_map/ppermute | solution.py:817
  44.8 16.4 %collective-permute-start.7 = (bf16[8,3,32,512]{3,2,1,0:T(8,128)(2,1)S(1)}, bf16[8,3,32,512]{3,2,1,0:T(8,128)(2,1)}, u32[]{:S(2)}, u32[]{:S(2)}) collective-permute-start(bf16[8,3,32,512]{3,2,1,0:T(8,128)(2,1)S(1)} %constant_dynamic-update-slice_fusion.refs_0_.refs_2_), channel_id=1, source_target_pairs={{0,16},{16,0},{1,17},{17,1},{2,18},{18,2},{3,19},{19,3},{4,20},{20... | collective-permute-start | bytes 2359304 | tf_op jit(solution)/shard_map/ppermute | solution.py:817
  82.4 65.6 %all-to-all-start = ((bf16[16,3,256,128]{3,2,1,0:T(8,128)(2,1)}), bf16[16,3,256,128]{3,2,1,0:T(8,128)(2,1)S(1)}, u32[]{:S(2)}, u32[]{:S(2)}) async-start(bf16[16,3,256,128]{3,2,1,0:T(8,128)(2,1)} %bitcast.89), calls=%async_computation | async-start | bytes 6291456 | tf_op jit(solution)/shard_map/all_to_all | solution.py:985
  89.2 5.8 %collective-permute-start.11 = (bf16[512,512]{1,0:T(8,128)(2,1)}, bf16[512,512]{1,0:T(8,128)(2,1)}, u32[]{:S(2)}, u32[]{:S(2)}) collective-permute-start(bf16[512,512]{1,0:T(8,128)(2,1)} %get-tuple-element.161), channel_id=1, source_target_pairs={{0,16},{16,0},{1,17},{17,1},{2,18},{18,2},{3,19},{19,3},{4,20},{20... | collective-permute-start | bytes 1572872 | tf_op jit(solution)/shard_map/ppermute | solution.py:817
  217.1 15.0 %collective-permute-start.13 = (bf16[16,576,512]{2,1,0:T(8,128)(2,1)}, bf16[16,576,512]{2,1,0:T(8,128)(2,1)}, u32[]{:S(2)}, u32[]{:S(2)}) collective-permute-start(bf16[16,576,512]{2,1,0:T(8,128)(2,1)} %all-gather.7.cloned.1.call-done.refs_0_), channel_id=1, source_target_pairs={{0,16},{16,0},{1,17},{17,1},{2,18},{18,2},{3,19},{19,3},{4,20},{20... | collective-permute-start | bytes 28311560 | tf_op jit(solution)/shard_map/ppermute | solution.py:817
  268.5 15.6 %collective-permute-start.14 = (bf16[512,4096]{1,0:T(8,128)(2,1)}, bf16[512,4096]{1,0:T(8,128)(2,1)}, u32[]{:S(2)}, u32[]{:S(2)}) collective-permute-start(bf16[512,4096]{1,0:T(8,128)(2,1)} %get-tuple-element.79.refs_0_), channel_id=1, source_target_pairs={{0,16},{16,0},{1,17},{17,1},{2,18},{18,2},{3,19},{19,3},{4,20},{20... | collective-permute-start | bytes 12582920 | tf_op jit(solution)/shard_map/ppermute | solution.py:817
  270.4 13.6 %collective-permute-start.16 = (bf16[1,512,2048]{2,1,0:T(8,128)(2,1)S(1)}, bf16[1,512,2048]{2,1,0:T(8,128)(2,1)}, u32[]{:S(2)}, u32[]{:S(2)}) collective-permute-start(bf16[1,512,2048]{2,1,0:T(8,128)(2,1)S(1)} %slice.61), channel_id=1, source_target_pairs={{0,16},{16,0},{1,17},{17,1},{2,18},{18,2},{3,19},{19,3},{4,20},{20... | collective-permute-start | bytes 6291464 | tf_op jit(solution)/shard_map/ppermute | solution.py:817
  270.9 32.7 %all-to-all-start.2 = ((bf16[16,256,128]{2,1,0:T(8,128)(2,1)}), bf16[16,256,128]{2,1,0:T(8,128)(2,1)S(1)}, u32[]{:S(2)}, u32[]{:S(2)}) async-start(bf16[16,256,128]{2,1,0:T(8,128)(2,1)} %bitcast.31), calls=%async_computation.2 | async-start | bytes 2097152 | tf_op jit(solution)/shard_map/all_to_all | solution.py:985
  279.0 154.6 %reduce-scatter.7.cloned.1.call-start = ((), (), s32[]{:S(2)}) async-start(), calls=%async_computation.9 | async-start | bytes 11796480
  279.0 5.0 collective-permute-start.15
  279.1 4.9 collective-permute-start.17
  304.6 183.8 %reduce-scatter.5.cloned.1.call-start = ((), (), s32[]{:S(2)}) async-start(), calls=%async_computation.6 | async-start | bytes 2949120 | tf_op jit(solution)/shard_map/reduce_scatter | solution.py:847
  431.9 19.7 %collective-permute-start.20 = (bf16[8,3,32,512]{3,2,1,0:T(8,128)(2,1)}, bf16[8,3,32,512]{3,2,1,0:T(8,128)(2,1)S(1)}, u32[]{:S(2)}, u32[]{:S(2)}) collective-permute-start(bf16[8,3,32,512]{3,2,1,0:T(8,128)(2,1)} %get-tuple-element.102), channel_id=1, source_target_pairs={{0,2},{1,3},{2,0},{3,1},{4,6},{5,7},{6,4},{7,5},{8,10},{9,11},{10,... | collective-permute-start | bytes 2359304 | tf_op jit(solution)/shard_map/ppermute | solution.py:817
  433.0 19.5 %collective-permute-start.21 = (bf16[8,3,32,512]{3,2,1,0:T(8,128)(2,1)}, bf16[8,3,32,512]{3,2,1,0:T(8,128)(2,1)S(1)}, u32[]{:S(2)}, u32[]{:S(2)}) collective-permute-start(bf16[8,3,32,512]{3,2,1,0:T(8,128)(2,1)} %get-tuple-element.103), channel_id=1, source_target_pairs={{0,1},{1,0},{2,3},{3,2},{4,5},{5,4},{6,7},{7,6},{8,9},{9,8},{10,11... | collective-permute-start | bytes 2359304 | tf_op jit(solution)/shard_map/ppermute | solution.py:817
  453.2 19.3 %collective-permute-start.23 = (bf16[4,1,3,32,512]{4,2,3,1,0:T(4,128)(2,1)S(1)}, bf16[4,1,3,32,512]{4,2,3,1,0:T(4,128)(2,1)S(1)}, u32[]{:S(2)}, u32[]{:S(2)}) collective-permute-start(bf16[4,1,3,32,512]{4,2,3,1,0:T(4,128)(2,1)S(1)} %copy.65), channel_id=1, source_target_pairs={{0,2},{1,3},{2,0},{3,1},{4,6},{5,7},{6,4},{7,5},{8,10},{9,11},{10,... | collective-permute-start | bytes 1179656 | tf_op jit(solution)/shard_map/ppermute | solution.py:817
  454.8 18.1 %collective-permute-start.22 = (bf16[4,1,3,32,512]{4,2,3,1,0:T(4,128)(2,1)S(1)}, bf16[4,1,3,32,512]{4,2,3,1,0:T(4,128)(2,1)S(1)}, u32[]{:S(2)}, u32[]{:S(2)}) collective-permute-start(bf16[4,1,3,32,512]{4,2,3,1,0:T(4,128)(2,1)S(1)} %copy.63), channel_id=1, source_target_pairs={{0,1},{1,0},{2,3},{3,2},{4,5},{5,4},{6,7},{7,6},{8,9},{9,8},{10,11... | collective-permute-start | bytes 1179656 | tf_op jit(solution)/shard_map/ppermute | solution.py:817
  456.8 11.5 %collective-permute-start.25 = (f32[1,10240]{1,0:T(1,128)S(1)}, f32[1,10240]{1,0:T(1,128)S(1)}, u32[]{:S(2)}, u32[]{:S(2)}) collective-permute-start(f32[1,10240]{1,0:T(1,128)S(1)} %add.89), channel_id=1, source_target_pairs={{0,1},{1,0},{2,3},{3,2},{4,5},{5,4},{6,7},{7,6},{8,9},{9,8},{10,11... | collective-permute-start | bytes 122888 | tf_op jit(solution)/shard_map/ppermute | solution.py:817
  474.1 7.4 %collective-permute-start.32 = (f32[1,10240]{1,0:T(1,128)S(1)}, f32[1,10240]{1,0:T(1,128)S(1)}, u32[]{:S(2)}, u32[]{:S(2)}) collective-permute-start(f32[1,10240]{1,0:T(1,128)S(1)} %add.91), channel_id=1, source_target_pairs={{0,12},{1,13},{2,14},{3,15},{4,8},{5,9},{6,10},{7,11},{8,4},{9,5},... | collective-permute-start | bytes 122888 | tf_op jit(solution)/shard_map/ppermute | solution.py:817
  476.5 10.5 %collective-permute-start.31 = (f32[1,10240]{1,0:T(1,128)S(1)}, f32[1,10240]{1,0:T(1,128)S(1)}, u32[]{:S(2)}, u32[]{:S(2)}) collective-permute-start(f32[1,10240]{1,0:T(1,128)S(1)} %add.91), channel_id=1, source_target_pairs={{0,8},{1,9},{2,10},{3,11},{4,12},{5,13},{6,14},{7,15},{8,0},{9,1},... | collective-permute-start | bytes 122888 | tf_op jit(solution)/shard_map/ppermute | solution.py:817
  477.1 9.9 %collective-permute-start.30 = (f32[1,10240]{1,0:T(1,128)S(1)}, f32[1,10240]{1,0:T(1,128)S(1)}, u32[]{:S(2)}, u32[]{:S(2)}) collective-permute-start(f32[1,10240]{1,0:T(1,128)S(1)} %add.91), channel_id=1, source_target_pairs={{0,4},{1,5},{2,6},{3,7},{4,0},{5,1},{6,2},{7,3},{8,12},{9,13},{10,... | collective-permute-start | bytes 122888 | tf_op jit(solution)/shard_map/ppermute | solution.py:817
  478.9 13.0 %collective-permute-start.29 = (bf16[2,3,32,512]{3,1,2,0:T(4,128)(2,1)S(1)}, bf16[2,3,32,512]{3,1,2,0:T(4,128)(2,1)S(1)}, u32[]{:S(2)}, u32[]{:S(2)}) collective-permute-start(bf16[2,3,32,512]{3,1,2,0:T(4,128)(2,1)S(1)} %get-tuple-element.156), channel_id=1, source_target_pairs={{0,12},{1,13},{2,14},{3,15},{4,8},{5,9},{6,10},{7,11},{8,4},{9,5},... | collective-permute-start | bytes 589832 | tf_op jit(solution)/shard_map/ppermute | solution.py:817
  481.2 25.6 %collective-permute-start.28 = (bf16[2,3,32,512]{3,1,2,0:T(4,128)(2,1)S(1)}, bf16[2,3,32,512]{3,1,2,0:T(4,128)(2,1)S(1)}, u32[]{:S(2)}, u32[]{:S(2)}) collective-permute-start(bf16[2,3,32,512]{3,1,2,0:T(4,128)(2,1)S(1)} %get-tuple-element.157), channel_id=1, source_target_pairs={{0,8},{1,9},{2,10},{3,11},{4,12},{5,13},{6,14},{7,15},{8,0},{9,1},... | collective-permute-start | bytes 589832 | tf_op jit(solution)/shard_map/ppermute | solution.py:817
  481.5 25.3 %collective-permute-start.27 = (bf16[2,3,32,512]{3,1,2,0:T(4,128)(2,1)S(1)}, bf16[2,3,32,512]{3,1,2,0:T(4,128)(2,1)S(1)}, u32[]{:S(2)}, u32[]{:S(2)}) collective-permute-start(bf16[2,3,32,512]{3,1,2,0:T(4,128)(2,1)S(1)} %get-tuple-element.158), channel_id=1, source_target_pairs={{0,4},{1,5},{2,6},{3,7},{4,0},{5,1},{6,2},{7,3},{8,12},{9,13},{10,... | collective-permute-start | bytes 589832 | tf_op jit(solution)/shard_map/ppermute | solution.py:817
  (27 other events, 244.2 us)
Sparse Core Ops, SparseCore 0:
  31.6 50.7 all-gather.4
  84.3 132.8 all-gather.6
  303.7 128.0 reduce-scatter.6
  434.0 51.5 reduce-scatter.4
